TPU v7x, 32 devices: a whole 2x2x4 slice. The times are simulated.
32 devices in a mesh: replay: 4 (over y, core), mp: 8 (over z, x).
Axes of the slice: x: 2, y: 2, z: 4, core: 2. Of those that a mesh axis runs over, the one named last changes fastest.
Arguments:
- features: bfloat16 [1024, 32, 2048], P(('replay', 'mp')), may hold values from -40 to 40
- rewards: bfloat16 [1024, 32], P(('replay', 'mp')), may hold values from -32 to 32
- tail_value: bfloat16 [1024], P(('replay', 'mp')), may hold values from -12 to 12
- actions: int32 [1024, 32], P(('replay', 'mp')), may hold values from 0 to 1023
- episode_ends: int32 [1024, 32], P(('replay', 'mp')), may hold values 0 or 1
- sample_owner: int32 [1024, 1], P(('replay', 'mp')), may hold values from 0 to 3; in each aligned block of 32 rows (0 to 31, 32 to 63, ...) at most 8 rows name the same one
- sample_row: int32 [1024], P(('replay', 'mp')), may hold values from 0 to 31
- norm_gain: float32 [2048], replicated, may hold values from 0.1 to 1.9
- value_weight: bfloat16 [2048], replicated, may hold values from -0.125 to 0.125
- policy_weight: float32 [2048, 1024], P('mp'), may hold values from -1 to 1
- first_moment: float32 [2048, 1024], P('mp'), may hold values from -0.00048828125 to 0.00048828125
- second_moment: float32 [2048, 1024], P('mp'), may hold values from 2.9802323e-09 to 2.9802322e-08
Outputs:
- normalized_advantage: float32 [32768], P(('replay', 'mp'))
- update_direction: float32 [2048, 1024], P('mp')
- actor_policy: bfloat16 [2048, 1024], replicated
Inputs may be any that keep to these rules, and one draw needn't show every extreme that they name: `sample_owner`: at most 8 of the 32 samples of one device name the same owner; exactly 8 do so on some devices.
All inputs are finite; a program needn't handle non-finite values. No bound on the sum of `episode_ends` on one device may be relied on, other than what follows from the above.
Results may differ from a plain program's by a relative error of at most 0.003.
Values may be sent and summed in bfloat16 or wider, within the bound.
No kernel may reach another device: no remote copies, remote signals or barrier semaphores. Data moves between devices by JAX's collectives and lax.ppermute only.
A program may use at most 128 MiB of HBM per device.

v0:
```python
import jax
import jax.numpy as jnp
from jax import lax
from jax.sharding import PartitionSpec as P

DISCOUNT = 0.97
STEP_RATE = 0.002


def normalize(rows, norm_gain):
    widened = rows.astype(jnp.float32)
    mean_square = jnp.mean(widened * widened, axis=-1, keepdims=True)
    return (widened * lax.rsqrt(mean_square + 1e-05) * norm_gain).astype(jnp.bfloat16)


def discount(step_rewards, step_ends, tail_values):

    def backward(carried, inputs):
        reward_now, end_now = inputs
        carried = reward_now + DISCOUNT * (1.0 - end_now.astype(jnp.float32)) * carried
        return (carried, carried)

    _, stacked = lax.scan(backward, tail_values, (step_rewards.T, step_ends.T), reverse=True)
    return stacked.T


def body(
    features,
    rewards,
    tail_value,
    actions,
    episode_ends,
    sample_owner,
    sample_row,
    norm_gain,
    value_weight,
    policy_weight,
    first_moment,
    second_moment,
):
    groups_count = lax.axis_size("replay")
    devices_all = groups_count * lax.axis_size("mp")
    sample_count = sample_owner.shape[0]
    slot_count = sample_count // 4
    seg_len = features.shape[1]
    model_width = features.shape[2]
    flat_slots = groups_count * slot_count
    owners = sample_owner[:, 0]
    owner_marks = (owners[:, None] == jnp.arange(groups_count, dtype=jnp.int32)[None, :]).astype(
        jnp.int32
    )
    earlier = jnp.cumsum(owner_marks, axis=0) - owner_marks
    position = owners * slot_count + jnp.sum(earlier * owner_marks, axis=1)
    wanted = jnp.full((flat_slots,), -1, jnp.int32).at[position].set(sample_row)
    asked_rows = lax.all_to_all(
        wanted.reshape(groups_count, slot_count), "replay", split_axis=0, concat_axis=0, tiled=True
    )
    asked_safe = jnp.maximum(asked_rows, 0)
    rows_back = (
        lax.all_to_all(features[asked_safe], "replay", split_axis=0, concat_axis=0, tiled=True),
        lax.all_to_all(rewards[asked_safe], "replay", split_axis=0, concat_axis=0, tiled=True),
        lax.all_to_all(tail_value[asked_safe], "replay", split_axis=0, concat_axis=0, tiled=True),
    )
    labels_back = (
        lax.all_to_all(actions[asked_safe], "replay", split_axis=0, concat_axis=0, tiled=True),
        lax.all_to_all(episode_ends[asked_safe], "replay", split_axis=0, concat_axis=0, tiled=True),
    )
    fetched = rows_back[0].reshape(flat_slots, seg_len, model_width)[position]
    step_rewards = rows_back[1].reshape(flat_slots, seg_len)[position].astype(jnp.float32)
    tail_values = rows_back[2].reshape(flat_slots)[position].astype(jnp.float32)
    step_actions = labels_back[0].reshape(flat_slots, seg_len)[position].reshape(-1)
    step_ends = labels_back[1].reshape(flat_slots, seg_len)[position]
    normed = normalize(fetched, norm_gain).reshape(sample_count * seg_len, model_width)
    multiplicity = jnp.ones((sample_count * seg_len,), jnp.float32)
    values = jnp.dot(normed, value_weight, preferred_element_type=jnp.float32)
    returns = discount(step_rewards, step_ends, tail_values).reshape(-1)
    advantage = returns - values
    token_total = devices_all * sample_count * seg_len
    mean_adv = lax.psum(jnp.sum(multiplicity * advantage), ("replay", "mp")) / token_total
    centered = advantage - mean_adv
    spread = lax.psum(jnp.sum(multiplicity * centered * centered), ("replay", "mp")) / token_total
    local_norm = centered * lax.rsqrt(spread + 1e-05)
    weights = jnp.exp(jnp.minimum(local_norm, 3.0))
    total_weight = lax.psum(jnp.sum(multiplicity * weights), ("replay", "mp"))
    policy_low = policy_weight.astype(jnp.bfloat16)
    action_count = policy_weight.shape[1]
    logits = jnp.dot(
        normed,
        lax.all_gather(policy_low, "mp", axis=0, tiled=True),
        preferred_element_type=jnp.float32,
    )
    row_top = jnp.max(logits, axis=1, keepdims=True)
    shifted = logits - row_top
    chances = jnp.exp(shifted - jnp.log(jnp.sum(jnp.exp(shifted), axis=1, keepdims=True)))
    chosen = (step_actions[:, None] == jnp.arange(action_count, dtype=jnp.int32)[None, :]).astype(
        jnp.float32
    )
    signal = (weights[:, None] * (chances - chosen)).astype(jnp.bfloat16)
    signal_parts = (signal,)
    contract = (((0,), (0,)), ((), ()))
    shard_rows = policy_weight.shape[0]
    full_grad = lax.dot_general(
        normed, signal_parts[0], contract, preferred_element_type=jnp.float32
    )
    summed = lax.psum(full_grad, ("replay", "mp"))
    gradient_sum = lax.dynamic_slice_in_dim(
        summed, lax.axis_index("mp") * shard_rows, shard_rows, 0
    )
    gradient = gradient_sum / total_weight
    first_new = 0.9 * first_moment + 0.1 * gradient
    second_new = 0.95 * second_moment + 0.05 * gradient * gradient
    update = first_new / (jnp.sqrt(second_new) + 1e-08)
    actor_low = (policy_weight - STEP_RATE * update).astype(jnp.bfloat16)
    actor_policy = lax.all_gather(actor_low, "mp", axis=0, tiled=True)
    return (local_norm, update, actor_policy)


def solution(mesh):
    return jax.shard_map(
        body,
        mesh=mesh,
        in_specs=(
            P(("replay", "mp"), None, None),
            P(("replay", "mp"), None),
            P(("replay", "mp")),
            P(("replay", "mp"), None),
            P(("replay", "mp"), None),
            P(("replay", "mp"), None),
            P(("replay", "mp")),
            P(),
            P(),
            P("mp", None),
            P("mp", None),
            P("mp", None),
        ),
        out_specs=(P(("replay", "mp")), P("mp", None), P()),
        check_vma=False,
    )
```

profile of v0, /device:TPU:0, one launch (start us, length us, event | category | flops | bytes accessed | tf_op | source)
XLA Modules:
  0.0 490.4 jit_solution(4506939995330862545)
XLA Ops:
  7.2 0.7 fusion.12
  8.0 0.8 select_reduce_fusion
  8.8 0.7 fusion.13
  9.5 0.8 scatter_custom_fusion
  10.4 7.8 %all_to_all.39 = s32[4,1,8]{2,1,0:T(1,128)S(1)} all-to-all(s32[4,1,8]{2,1,0:T(1,128)S(1)} %bitcast.56), channel_id=1, replica_groups=mesh['replay'=4,'mp'=8] {'replay'}, dimensions={0} | all-to-all | bytes 256 | tf_op jit(solution)/shard_map/all_to_all | solution.py:55
  18.3 1.4 gather_fusion
  19.6 0.7 all_to_all.32
  20.3 3.2 all-to-all-start.1
  23.5 1.3 gather_fusion.2
  24.8 0.7 reshape.195
  25.5 1.7 all-to-all-done.1
  27.2 3.2 all-to-all-start.2
  30.4 2.1 convert_element_type.56
  32.6 0.6 gather_fusion.4
  33.1 0.7 reshape.197
  34.0 3.2 all-to-all-start.3
  37.3 0.7 reshape.183
  38.0 5.0 %gather_fusion.6 = bf16[32,32,2048]{2,1,0:T(8,128)(2,1)} fusion(bf16[32,32,2048]{2,1,0:T(8,128)(2,1)} %param.14, s32[1024]{0:T(1024)S(1)} %pad_clamp_fusion.1), kind=kCustom, calls=%fused_computation.6 | custom fusion | bytes 8388736 | tf_op jit(solution)/shard_map/gather | solution.py:60
  43.6 0.7 reshape.199
  44.4 0.7 gather_fusion.1
  45.2 0.6 gather_fusion.3
  45.8 3.3 all-to-all-start.5
  49.6 0.7 reduce.5
  50.4 0.6 gather_fusion.5
  51.0 1.8 all-to-all-done.5
  52.8 4.8 all-to-all-start.4
  57.7 2.4 while.16
  60.3 0.7 reduce.6
  61.6 44.3 %all-to-all-done.4 = bf16[4,8,32,2048]{3,2,1,0:T(8,128)(2,1)} async-done(((bf16[4,8,32,2048]{3,2,1,0:T(8,128)(2,1)}), bf16[4,8,32,2048]{3,2,1,0:T(8,128)(2,1)}, u32[]{:S(2)}, u32[]{:S(2)}) %all-to-all-start.4) | async-done | bytes 4194336 | tf_op jit(solution)/shard_map/all_to_all | solution.py:60
  105.9 5.0 %gather_fusion.7 = bf16[32,32,2048]{2,1,0:T(8,128)(2,1)} fusion(bf16[32,32,2048]{2,1,0:T(8,128)(2,1)} %bitcast.15, s32[1024]{0:T(1024)S(1)} %pad_clamp_fusion), kind=kCustom, calls=%fused_computation.7 | custom fusion | bytes 8388736 | tf_op jit(solution)/shard_map/gather | solution.py:68
  110.9 3.1 multiply_reduce_fusion
  114.1 3.2 fusion.2
  117.3 2.0 copy-done.1
  119.3 1.2 fusion.20
  120.5 0.6 fusion.18
  121.1 39.7 %psum.28 = f32[]{:T(128)} all-reduce(f32[]{:T(128)} %get-tuple-element.141), channel_id=1, replica_groups=mesh['replay'=4,'mp'=8] {'replay','mp'}, use_global_device_ids=true, to_apply=%region_7.8 | all-reduce | flops 1 | bytes 8 | tf_op jit(solution)/shard_map/psum | solution.py:79
  161.5 0.6 multiply_reduce_fusion.1
  162.1 41.6 %psum.29 = f32[]{:T(128)} all-reduce(f32[]{:T(128)} %multiply_reduce_fusion.1), channel_id=1, replica_groups=mesh['replay'=4,'mp'=8] {'replay','mp'}, use_global_device_ids=true, to_apply=%region_9.10 | all-reduce | flops 1 | bytes 8 | tf_op jit(solution)/shard_map/psum | solution.py:81
  204.5 0.6 fusion.16
  205.1 7.6 %fusion.19 = (f32[1024]{0:T(1024)S(1)}, f32[1024,1024]{0,1:T(8,128)S(1)}) fusion(bf16[1024,2048]{1,0:T(8,128)(2,1)} %copy-done.1, bf16[2048,1024]{1,0:T(8,128)(2,1)} %all-gather.3.cloned.1.call-done), kind=kOutput, calls=%fused_computation.49 | convolution fusion | flops 4296014848 | bytes 12587008 | tf_op jit(solution)/shard_map/dot_general | solution.py:87
  212.7 0.6 exponential_reduce_fusion
  213.4 1.5 copy-done.2
  214.9 7.1 %fusion.3 = f32[2048,1024]{1,0:T(8,128)} fusion(bf16[1024,2048]{1,0:T(8,128)(2,1)S(1)} %copy-done.2, f32[1024,1024]{0,1:T(8,128)S(1)} %get-tuple-element.144, s32[1024]{0:T(1024)S(1)} %eq.34, f32[1024]{0:T(1024)S(1)} %log.8, f32[1024]{0:T(1024)S(1)} %get-tuple-element.143, f32[1024]{0:T(1024)S(1)} %minimum_exponential_fusion), kind=kOutput, calls=%fused_computation.20 | convolution fusion | flops 4302307328 | bytes 16793600 | tf_op jit(solution)/shard_map/dot_general | solution.py:102
  222.2 41.2 %psum.31 = f32[]{:T(128)} all-reduce(f32[]{:T(128)} %get-tuple-element.139), channel_id=1, replica_groups=mesh['replay'=4,'mp'=8] {'replay','mp'}, use_global_device_ids=true, to_apply=%region_14.15 | all-reduce | flops 1 | bytes 8 | tf_op jit(solution)/shard_map/psum | solution.py:84
  263.4 138.5 %all-reduce.2.cloned.1.call-done = f32[2048,1024]{1,0:T(8,128)} async-done(((f32[2048,1024]{1,0:T(8,128)}), f32[2048,1024]{1,0:T(8,128)}) %all-reduce.2.cloned.1.call-update) | async-done | bytes 8388624 | tf_op jit(solution)/shard_map/psum | solution.py:105
  401.9 3.8 subtract_convert_fusion
  405.6 73.6 %all-gather.5.cloned.1.call-done = bf16[2048,1024]{1,0:T(8,128)(2,1)} async-done(((bf16[256,1024]{1,0:T(8,128)(2,1)}), bf16[2048,1024]{1,0:T(8,128)(2,1)}) %all-gather.5.cloned.1.call-update) | async-done | bytes 4194320 | tf_op jit(solution)/shard_map/all_gather | solution.py:114
  479.2 4.6 copy.42
  (115 shorter events, 5.1 us)
Async XLA Ops:
  7.2 25.4 %copy-start = (s32[32,32]{1,0:T(8,128)S(1)}, s32[32,32]{1,0:T(8,128)}, u32[]{:S(2)}) copy-start(s32[32,32]{1,0:T(8,128)} %param.18) | copy-start | bytes 12292
  20.3 6.9 %all-to-all-start.1 = ((bf16[4,1,8]{2,1,0:T(2,128)(2,1)}), bf16[4,1,8]{2,1,0:T(2,128)(2,1)S(1)}, u32[]{:S(2)}, u32[]{:S(2)}) async-start(bf16[4,1,8]{2,1,0:T(2,128)(2,1)} %all_to_all.32), calls=%async_computation.1 | async-start | bytes 4096 | tf_op jit(solution)/shard_map/all_to_all | solution.py:62
  27.2 6.9 %all-to-all-start.2 = ((bf16[4,2,128]{2,1,0:T(2,128)(2,1)}), bf16[4,2,128]{2,1,0:T(2,128)(2,1)S(1)}, u32[]{:S(2)}, u32[]{:S(2)}) async-start(bf16[4,2,128]{2,1,0:T(2,128)(2,1)} %reshape.195), calls=%async_computation.2 | async-start | bytes 4096 | tf_op jit(solution)/shard_map/all_to_all | solution.py:61
  30.4 174.7 %all-gather.3.cloned.1.call-start = ((), (), s32[]{:S(2)}) async-start(), calls=%async_computation.6 | async-start | bytes 4718592 | tf_op jit(solution)/shard_map/all_gather | solution.py:89
  34.0 11.8 %all-to-all-start.3 = ((s32[4,1,256]{2,1,0:T(1,128)}), s32[4,1,256]{2,1,0:T(1,128)S(1)}, u32[]{:S(2)}, u32[]{:S(2)}) async-start(s32[4,1,256]{2,1,0:T(1,128)} %reshape.197), calls=%async_computation.3 | async-start | bytes 8192 | tf_op jit(solution)/shard_map/all_to_all | solution.py:66
  38.0 5.0 %copy-start.4 = (s32[32,32]{1,0:T(8,128)S(1)}, s32[32,32]{1,0:T(8,128)}, u32[]{:S(2)}) copy-start(s32[32,32]{1,0:T(8,128)} %param.17) | copy-start | bytes 12292
  45.8 7.0 %all-to-all-start.5 = ((s32[4,1,256]{2,1,0:T(1,128)}), s32[4,1,256]{2,1,0:T(1,128)S(1)}, u32[]{:S(2)}, u32[]{:S(2)}) async-start(s32[4,1,256]{2,1,0:T(1,128)} %reshape.199), calls=%async_computation.5 | async-start | bytes 8192 | tf_op jit(solution)/shard_map/all_to_all | solution.py:65
  52.8 53.1 %all-to-all-start.4 = ((bf16[4,8,32,2048]{3,2,1,0:T(8,128)(2,1)}), bf16[4,8,32,2048]{3,2,1,0:T(8,128)(2,1)}, u32[]{:S(2)}, u32[]{:S(2)}) async-start(bf16[4,8,32,2048]{3,2,1,0:T(8,128)(2,1)} %bitcast.45), calls=%async_computation.4 | async-start | bytes 8388608 | tf_op jit(solution)/shard_map/all_to_all | solution.py:60
  57.7 344.2 %all-reduce.2.cloned.1.call-start = ((), (), s32[]{:S(2)}) async-start(), calls=%async_computation.7 | async-start | bytes 16777216 | tf_op jit(solution)/shard_map/psum | solution.py:105
  110.9 3.2 copy-start.8
  117.3 2.0 copy-start.1
  205.1 7.7 %copy-start.7 = (f32[1024]{0:T(1024)}, f32[1024]{0:T(1024)S(1)}, u32[]{:S(2)}) copy-start(f32[1024]{0:T(1024)S(1)} %get-tuple-element.203) | copy-start | bytes 12292
  212.7 2.2 copy-start.2
  222.1 179.8 %copy-start.3 = (f32[256,1024]{1,0:T(8,128)S(1)}, f32[256,1024]{1,0:T(8,128)}, u32[]{:S(2)}) copy-start(f32[256,1024]{1,0:T(8,128)} %param.23) | copy-start | bytes 3145732
  222.1 179.8 %copy-start.5 = (f32[256,1024]{1,0:T(8,128)S(1)}, f32[256,1024]{1,0:T(8,128)}, u32[]{:S(2)}) copy-start(f32[256,1024]{1,0:T(8,128)} %param.25) | copy-start | bytes 3145732
  222.1 179.8 %copy-start.6 = (f32[256,1024]{1,0:T(8,128)S(1)}, f32[256,1024]{1,0:T(8,128)}, u32[]{:S(2)}) copy-start(f32[256,1024]{1,0:T(8,128)} %param.24) | copy-start | bytes 3145732
  222.1 257.1 %all-gather.5.cloned.1.call-start = ((), (), s32[]{:S(2)}) async-start(), calls=%async_computation.8 | async-start | bytes 4718592 | tf_op jit(solution)/shard_map/all_gather | solution.py:114
Sparse Core Ops, SparseCore 0:
  33.9 75.0 all-gather.2
  222.2 179.5 all-reduce.1
  405.8 73.4 all-gather.4
where the time goes:
time: 492 us; the launch traced here: 490 us
  waiting for transfers between devices  260 us (53%)
  blocking collectives  130 us (26%)
  local copies, waits for them, and re-layouts  31.4 us (6%)
  other arithmetic  19 us (4%)
  starting transfers between devices  17.9 us (4%)
  matrix products  16 us (3%)
  between operations  15.3 us (3%)
    psum x1, waiting for transfers between devices, body(): summed = lax.psum(full_grad, ('replay', 'mp'))  138 us
    all_gather x1, waiting for transfers between devices, body(): actor_policy = lax.all_gather(actor_low, 'mp', axis=0, tiled=True)  73.6 us
    all_to_all x1, waiting for transfers between devices, body(): lax.all_to_all(features[asked_safe], 'replay', split_axis=0, concat_axis=...  44.3 us
    psum x1, blocking collectives, body(): lax.psum(jnp.sum(multiplicity * centered * centered), ('replay', 'mp'))  41.6 us
    psum x1, blocking collectives, body(): total_weight = lax.psum(jnp.sum(multiplicity * weights), ('replay', 'mp'))  41.2 us
    psum x1, blocking collectives, body(): lax.psum(jnp.sum(multiplicity * advantage), ('replay', 'mp')) / token_total  39.7 us
    unnamed x26, local copies, waits for them, and re-layouts  11.2 us
  transfers between devices with their start and end apart: 8, of which 6 were waited for; matrix products, arithmetic and copies ran while one was open for 7% of the time, Pallas kernels for 0%

commit v1 on v0

v1 whole, which is shorter than its diff:
```python
import functools

import jax
import jax.numpy as jnp
from jax import lax
from jax.experimental import pallas as pl
from jax.experimental.pallas import tpu as pltpu
from jax.sharding import PartitionSpec as P

DISCOUNT = 0.97
STEP_RATE = 0.002
ALL = ("replay", "mp")
LANES = 128
BF16 = jnp.bfloat16
F32 = jnp.float32
VMEM = pl.BlockSpec(memory_space=pltpu.VMEM)
SMEM = pl.BlockSpec(memory_space=pltpu.SMEM)
ANY = pl.BlockSpec(memory_space=pl.ANY)


class Plan:
    def __init__(self, replay, mp, actions):
        self.C = 2
        self.Y = replay // self.C
        self.Z = 4
        self.X = mp // self.Z
        self.mp = mp
        self.swap = self.X == self.Y
        self.block = LANES
        self.J = max(1, actions // (self.C * self.Y * self.block))

    def permute(self, value, axis, k):
        pairs = []
        for y in range(self.Y):
            for c in range(self.C):
                for z in range(self.Z):
                    for x in range(self.X):
                        along = axis
                        if axis in ("p", "q"):
                            along = "y" if (axis == "p") == (c == 0 or not self.swap) else "x"
                        to = dict(y=y, c=c, z=z, x=x)
                        to[along] ^= k
                        pairs.append((self.index(y, c, z, x), self.index(**to)))
        return lax.ppermute(value, ALL, pairs)

    def index(self, y, c, z, x):
        return (y * self.C + c) * self.mp + z * self.X + x

    def here(self):
        replay, mp = lax.axis_index("replay"), lax.axis_index("mp")
        return jnp.stack([replay // self.C, replay % self.C, mp // self.X, mp % self.X]).astype(jnp.int32)

    def relative(self, core, dy, dx):
        if not self.swap:
            return dy, dx
        return jnp.where(core == 0, dy, dx), jnp.where(core == 0, dx, dy)

    def gather_column(self, block):
        return jnp.stack([block] + [self.permute(block, "z", k) for k in range(1, self.Z)])

    def gather_rest(self, column):
        plane = jnp.stack([column] + [self.permute(column, "q", k) for k in range(1, self.X)])
        mine = [plane] + [self.permute(plane, "p", k) for k in range(1, self.Y)]
        return mine + [self.permute(piece, "c", 1) for piece in mine]

    def reduce(self, keep, send):
        total = keep + self.permute(send, "c", 1).astype(F32)
        for axis in ("p", "q", "z"):
            low = total[1:].astype(BF16)
            total = total[0]
            terms = [self.permute(low[k - 1], axis, k) for k in range(1, low.shape[0] + 1)]
            if axis == "z":
                return total, terms
            for term in terms:
                total = total + term.astype(F32)


def shard_kernel(place_ref, w_ref, out_ref):
    out_ref[0] = w_ref[...].T.astype(BF16)


def own_shard(plan, place, policy_weight):
    depth = policy_weight.shape[0]
    block = plan.block
    return pl.pallas_call(
        shard_kernel,
        grid_spec=pltpu.PrefetchScalarGridSpec(
            num_scalar_prefetch=1,
            grid=(plan.J,),
            in_specs=[pl.BlockSpec((depth, block), lambda j, place: (0, j * 2 * plan.Y + place[0]))],
            out_specs=pl.BlockSpec((1, block, depth), lambda j, place: (j, 0, 0)),
        ),
        out_shape=jax.ShapeDtypeStruct((plan.J, block, depth), BF16),
        name="shard",
    )(place, policy_weight)


def update_kernel(count, place_ref, mass_ref, base_ref, *refs):
    terms, (w_ref, m_ref, v_ref, update_ref, low_ref) = refs[:count], refs[count:]
    total = base_ref[...]
    for term in terms:
        total = total + term[...].astype(F32)
    gradient = total.T / mass_ref[0, 0]
    first_new = 0.9 * m_ref[...] + 0.1 * gradient
    second_new = 0.95 * v_ref[...] + 0.05 * gradient * gradient
    update = first_new / (jnp.sqrt(second_new) + 1e-08)
    update_ref[...] = update
    low_ref[...] = (w_ref[...] - STEP_RATE * update).astype(BF16)


def own_update(plan, j, place, mass, base, terms, policy_weight, first_moment, second_moment):
    depth = policy_weight.shape[0]
    block = plan.block
    whole = pl.BlockSpec((block, depth), lambda i, place: (0, 0))
    own = pl.BlockSpec((depth, block), lambda i, place: (0, j * 2 * plan.Y + place[0]))
    out = pl.BlockSpec((depth, block), lambda i, place: (0, 0))
    return pl.pallas_call(
        functools.partial(update_kernel, len(terms)),
        grid_spec=pltpu.PrefetchScalarGridSpec(
            num_scalar_prefetch=1,
            grid=(1,),
            in_specs=[SMEM, whole] + [whole] * len(terms) + [own] * 3,
            out_specs=[out, out],
        ),
        out_shape=[
            jax.ShapeDtypeStruct((depth, block), F32),
            jax.ShapeDtypeStruct((depth, block), BF16),
        ],
        name="update",
    )(place, mass, base, *terms, policy_weight, first_moment, second_moment)


def norm_kernel(x_ref, gain_ref, value_ref, out_ref, val_ref):
    wide = x_ref[...].astype(F32)
    mean_square = jnp.mean(wide * wide, axis=-1, keepdims=True)
    normed = (wide * lax.rsqrt(mean_square + 1e-05) * gain_ref[...]).astype(BF16)
    out_ref[...] = normed
    val_ref[...] = lax.dot_general(
        value_ref[...], normed, (((1,), (1,)), ((), ())), preferred_element_type=F32
    )


def normalize(rows, norm_gain, value_weight):
    tokens, width = rows.shape
    tile = 256
    normed, values = pl.pallas_call(
        norm_kernel,
        grid=(tokens // tile,),
        in_specs=[
            pl.BlockSpec((tile, width), lambda i: (i, 0)),
            pl.BlockSpec((1, width), lambda i: (0, 0)),
            pl.BlockSpec((16, width), lambda i: (0, 0)),
        ],
        out_specs=[
            pl.BlockSpec((tile, width), lambda i: (i, 0)),
            pl.BlockSpec((16, tile), lambda i: (0, i)),
        ],
        out_shape=[
            jax.ShapeDtypeStruct((tokens, width), BF16),
            jax.ShapeDtypeStruct((16, tokens), F32),
        ],
        compiler_params=pltpu.CompilerParams(vmem_limit_bytes=32 * 2**20),
        cost_estimate=pl.CostEstimate(
            flops=10 * tokens * width, bytes_accessed=4 * tokens * width, transcendentals=0
        ),
        name="normalize",
    )(rows, norm_gain.reshape(1, width), jnp.broadcast_to(value_weight[None, :], (16, width)))
    return normed, values[0]


def advantage_kernel(seg_len, r_ref, e_ref, tail_ref, v_ref, out_ref):
    lane = lax.broadcasted_iota(jnp.int32, r_ref.shape, 1) % seg_len
    last = lane == seg_len - 1
    decay = DISCOUNT * (1.0 - e_ref[...])
    total = r_ref[...] + jnp.where(last, decay * tail_ref[...], 0.0)
    decay = jnp.where(last, 0.0, decay)
    reach = 1
    while reach < seg_len:
        total = total + decay * pltpu.roll(total, LANES - reach, axis=1)
        decay = decay * pltpu.roll(decay, LANES - reach, axis=1)
        reach *= 2
    out_ref[...] = total - v_ref[...]


def advantages(rewards, ends, tails, values):
    segs, seg_len = rewards.shape
    shape = (segs * seg_len // LANES, LANES)
    tails = jnp.broadcast_to(tails.astype(F32)[:, None], rewards.shape)
    return pl.pallas_call(
        functools.partial(advantage_kernel, seg_len),
        in_specs=[VMEM] * 4,
        out_specs=VMEM,
        out_shape=jax.ShapeDtypeStruct(shape, F32),
        name="advantage",
    )(
        rewards.astype(F32).reshape(shape),
        ends.astype(F32).reshape(shape),
        tails.reshape(shape),
        values.reshape(shape),
    )


def gradient_chunk(plan, j, here, sig_ref, n_ref, keep_ref, send_ref):
    y, c, z, x = here
    rows = plan.Y * plan.block
    depth = keep_ref.shape[-1]

    def step(m, carry):
        start = pl.multiple_of(m * depth, depth)
        part = jnp.dot(
            sig_ref[j * 2 * rows : (j + 1) * 2 * rows, :],
            n_ref[:, pl.ds(start, depth)],
            preferred_element_type=F32,
        )
        first, second = part[:rows], part[rows:]
        keep = jnp.where(c == 0, first, second)
        send = jnp.where(c == 0, second, first).astype(BF16)
        dz, dx = (m // plan.X) ^ z, (m % plan.X) ^ x
        for col in range(plan.Y):
            p, q = plan.relative(c, y ^ col, dx)
            keep_ref[p, q, dz] = keep[col * plan.block : (col + 1) * plan.block]
            p, q = plan.relative(1 - c, y ^ col, dx)
            send_ref[p, q, dz] = send[col * plan.block : (col + 1) * plan.block]
        return carry

    lax.fori_loop(0, plan.mp, step, 0)


def signal_kernel(plan, here_ref, w_ref, act_ref, *refs):
    count = plan.J * 2 * plan.Y
    pieces, refs = refs[:count], refs[count:]
    n_hbm, sig_ref, keep_ref, send_ref, wt_ref, n_ref, l_ref, w_sems, n_sem = refs
    y, c, z, x = here = tuple(here_ref[i] for i in range(4))
    depth = keep_ref.shape[-1]
    block = plan.block
    n_copy = pltpu.make_async_copy(n_hbm, n_ref, n_sem)
    n_copy.start()
    copies = []
    for j in range(plan.J):
        for other in range(2):
            core = c ^ other
            for p in range(plan.Y):
                piece = pieces[(j * 2 + other) * plan.Y + p]
                for q in range(plan.X):
                    a, b = plan.relative(core, p, q)
                    for dz in range(plan.Z):
                        row = ((j * 2 + core) * plan.Y + (y ^ a)) * block
                        col = ((z ^ dz) * plan.X + (x ^ b)) * depth
                        copy = pltpu.make_async_copy(
                            piece.at[q, dz],
                            wt_ref.at[pl.ds(pl.multiple_of(row, block), block), pl.ds(pl.multiple_of(col, depth), depth)],
                            w_sems.at[len(copies)],
                        )
                        copy.start()
                        copies.append(copy)
    n_copy.wait()
    for copy in copies:
        copy.wait()
    actions, tokens = sig_ref.shape
    tile = l_ref.shape[1]
    group = 256

    def step(t, carry):
        where = pl.ds(pl.multiple_of(t * tile, tile), tile)
        normed = n_ref[where, :]
        top = None
        for a in range(actions // group):
            part = lax.dot_general(
                wt_ref[a * group : (a + 1) * group, :],
                normed,
                (((1,), (1,)), ((), ())),
                preferred_element_type=F32,
            )
            l_ref[a * group : (a + 1) * group, :] = part
            high = jnp.max(part, axis=0, keepdims=True)
            top = high if top is None else jnp.maximum(top, high)
        mass = jnp.zeros_like(top)
        for a in range(actions // group):
            part = jnp.exp(l_ref[a * group : (a + 1) * group, :] - top)
            l_ref[a * group : (a + 1) * group, :] = part
            mass = mass + jnp.sum(part, axis=0, keepdims=True)
        weight = w_ref[:, where]
        chosen = act_ref[:, where]
        inverse = 1.0 / mass
        for a in range(actions // group):
            row = lax.broadcasted_iota(jnp.int32, (group, tile), 0) + a * group
            chance = l_ref[a * group : (a + 1) * group, :] * inverse
            part = weight * (chance - jnp.where(row == chosen, 1.0, 0.0))
            sig_ref[a * group : (a + 1) * group, where] = part.astype(BF16)
        return carry

    lax.fori_loop(0, tokens // tile, step, 0)
    gradient_chunk(plan, 0, here, sig_ref, n_ref, keep_ref, send_ref)


def gradient_kernel(plan, j, here_ref, sig_ref, n_ref, keep_ref, send_ref):
    gradient_chunk(plan, j, tuple(here_ref[i] for i in range(4)), sig_ref, n_ref, keep_ref, send_ref)


def chunk_shapes(plan, depth):
    shape = (plan.Y, plan.X, plan.Z, plan.block, depth)
    return [jax.ShapeDtypeStruct(shape, F32), jax.ShapeDtypeStruct(shape, BF16)]


def signal_and_gradient(plan, here, weights, actions, pieces, normed, count):
    tokens, width = normed.shape
    depth = width // plan.mp
    sig, keep, send = pl.pallas_call(
        functools.partial(signal_kernel, plan),
        in_specs=[SMEM, VMEM, VMEM] + [ANY] * (len(pieces) + 1),
        out_specs=[VMEM] * 3,
        out_shape=[jax.ShapeDtypeStruct((count, tokens), BF16)] + chunk_shapes(plan, depth),
        scratch_shapes=[
            pltpu.VMEM((count, width), BF16),
            pltpu.VMEM((tokens, width), BF16),
            pltpu.VMEM((count, 256), F32),
            pltpu.SemaphoreType.DMA((len(pieces) * plan.X * plan.Z,)),
            pltpu.SemaphoreType.DMA,
        ],
        compiler_params=pltpu.CompilerParams(vmem_limit_bytes=48 * 2**20),
        cost_estimate=pl.CostEstimate(
            flops=2 * tokens * width * count * (plan.J + 1) // plan.J,
            bytes_accessed=2 * tokens * width + 2 * width * count + 2 * tokens * count,
            transcendentals=tokens * count,
        ),
        name="signal",
    )(here, weights, actions, *pieces, normed)
    chunks = [(keep, send)]
    for j in range(1, plan.J):
        chunks.append(
            pl.pallas_call(
                functools.partial(gradient_kernel, plan, j),
                in_specs=[SMEM, VMEM, VMEM],
                out_specs=[VMEM] * 2,
                out_shape=chunk_shapes(plan, depth),
                compiler_params=pltpu.CompilerParams(vmem_limit_bytes=48 * 2**20),
                cost_estimate=pl.CostEstimate(
                    flops=2 * tokens * width * count // plan.J,
                    bytes_accessed=2 * tokens * width + 2 * tokens * count,
                    transcendentals=0,
                ),
                name="gradient",
            )(here, sig, normed)
        )
    return chunks


def assemble_kernel(plan, here_ref, *refs):
    count = plan.J * 2 * plan.Y
    pieces = refs[:count]
    near, far, actor_ref, update_ref, sems = refs[count:]
    y, c, z, x = (here_ref[i] for i in range(4))
    depth = near.shape[-2]
    block = plan.block
    copies = []

    def copy(source, target):
        moved = pltpu.make_async_copy(source, target, sems.at[len(copies)])
        moved.start()
        copies.append(moved)

    for j in range(plan.J):
        for other in range(2):
            core = c ^ other
            for dy in range(plan.Y):
                col = ((j * 2 + core) * plan.Y + (y ^ dy)) * block
                copy(
                    (far if other else near).at[dy, j],
                    update_ref.at[:, pl.ds(pl.multiple_of(col, block), block)],
                )
            for p in range(plan.Y):
                piece = pieces[(j * 2 + other) * plan.Y + p]
                for q in range(plan.X):
                    a, b = plan.relative(core, p, q)
                    for dz in range(plan.Z):
                        col = ((j * 2 + core) * plan.Y + (y ^ a)) * block
                        row = ((z ^ dz) * plan.X + (x ^ b)) * depth
                        copy(
                            piece.at[q, dz],
                            actor_ref.at[pl.ds(pl.multiple_of(row, depth), depth), pl.ds(pl.multiple_of(col, block), block)],
                        )
    for moved in copies:
        moved.wait()


def assemble(plan, here, pieces, near, far, width, count):
    depth = width // plan.mp
    return pl.pallas_call(
        functools.partial(assemble_kernel, plan),
        in_specs=[SMEM] + [VMEM] * (len(pieces) + 2),
        out_specs=[ANY] * 2,
        out_shape=[
            jax.ShapeDtypeStruct((width, count), BF16),
            jax.ShapeDtypeStruct((depth, count), F32),
        ],
        scratch_shapes=[
            pltpu.SemaphoreType.DMA((len(pieces) * plan.X * plan.Z + plan.J * 2 * plan.Y,)),
        ],
        compiler_params=pltpu.CompilerParams(vmem_limit_bytes=32 * 2**20),
        name="assemble",
    )(here, *pieces, near, far)


def body(
    features,
    rewards,
    tail_value,
    actions,
    episode_ends,
    sample_owner,
    sample_row,
    norm_gain,
    value_weight,
    policy_weight,
    first_moment,
    second_moment,
):
    owners_all, columns = lax.axis_size("replay"), lax.axis_size("mp")
    segs, seg_len, width = features.shape
    depth, count = policy_weight.shape
    samples = sample_row.shape[0]
    plan = Plan(owners_all, columns, count)
    here = plan.here()
    place = (here[1] * plan.Y + here[0]).reshape(1)
    replay = lax.axis_index("replay")

    low = own_shard(plan, place, policy_weight)
    stages = [plan.gather_column(low[j]) for j in range(plan.J)]
    stages[0], norm_gain = lax.optimization_barrier((stages[0], norm_gain))
    pieces = [piece for column in stages for piece in plan.gather_rest(column)]

    normed, values = normalize(features.reshape(segs * seg_len, width), norm_gain, value_weight)
    advantage = advantages(rewards, episode_ends, tail_value, values)

    rows = advantage.shape[0]
    request = (sample_owner[:, 0] * segs + sample_row).astype(F32)
    request = jnp.pad(request[None, :], ((0, 7), (0, LANES - samples)))
    known = jnp.concatenate([advantage, request])
    for axis, size in (("z", plan.Z), ("x", plan.X), ("y", plan.Y), ("c", plan.C)):
        known = jnp.stack([known] + [plan.permute(known, axis, k) for k in range(1, size)])
    lead = (plan.C, plan.Y, plan.X, plan.Z)
    advantage = known[..., :rows, :].reshape(lead + (segs, seg_len))
    request = known[..., rows, :samples].astype(jnp.int32)
    code = (request // segs ^ replay) * segs + request % segs
    marks = jnp.transpose(code, (2, 3, 0, 1, 4)).reshape(plan.X, plan.Z, -1)
    slots = jnp.arange(owners_all * segs, dtype=jnp.int32)
    times = jnp.sum((marks[..., None] == slots).astype(F32), axis=2)
    times = times.reshape(plan.X, plan.Z, plan.Y, plan.C, segs)
    times = jnp.transpose(times, (3, 2, 0, 1, 4))[..., None]

    token_total = owners_all * columns * samples * seg_len
    centered = advantage - jnp.sum(times * advantage) / token_total
    spread = jnp.sum(times * centered * centered) / token_total
    normalized = centered * lax.rsqrt(spread + 1e-05)
    weights = times * jnp.exp(jnp.minimum(normalized, 3.0))
    total_weight = jnp.sum(weights)
    column = jnp.transpose(normalized[:, :, 0, 0], (1, 0, 2, 3)).reshape(owners_all * segs, seg_len)
    local_norm = column[code[0, 0, 0, 0]].reshape(-1)

    chunks = signal_and_gradient(
        plan,
        here,
        weights[0, 0, 0, 0].reshape(1, -1),
        actions.reshape(1, -1),
        pieces,
        normed,
        count,
    )
    updates, fresh = [], []
    for j, (keep, send) in enumerate(chunks):
        base, terms = plan.reduce(keep, send)
        update, low = own_update(
            plan, j, place, total_weight.reshape(1, 1), base, terms, policy_weight, first_moment, second_moment
        )
        updates.append(update)
        fresh += plan.gather_rest(plan.gather_column(low))
    near = jnp.stack(updates)
    near = jnp.stack([near] + [plan.permute(near, "y", k) for k in range(1, plan.Y)])
    far = plan.permute(near, "c", 1)
    actor_policy, update = assemble(plan, here, fresh, near, far, width, count)
    return (local_norm, update, actor_policy)


def solution(mesh):
    return jax.shard_map(
        body,
        mesh=mesh,
        in_specs=(
            P(ALL, None, None),
            P(ALL, None),
            P(ALL),
            P(ALL, None),
            P(ALL, None),
            P(ALL, None),
            P(ALL),
            P(),
            P(),
            P("mp", None),
            P("mp", None),
            P("mp", None),
        ),
        out_specs=(P(ALL), P("mp", None), P()),
        check_vma=False,
    )
```

time: 492 us -> 176 us (0.36)
  waiting for transfers between devices: 260 us -> 50.3 us
  blocking collectives: 130 us -> 0 us
  starting transfers between devices: 17.9 us -> 56.6 us
  Pallas kernels: 0 us -> 38 us
  matrix products: 16 us -> 0 us
  between operations: 15.3 us -> 2.44 us
  other arithmetic: 19 us -> 7.4 us
  local copies, waits for them, and re-layouts: 31.4 us -> 20.9 us
    psum x1 -> x0, waiting for transfers between devices: 138 us -> none  [body(): summed = lax.psum(full_grad, ('replay', 'mp'))]
    psum x3 -> x0, blocking collectives: 123 us -> none  [the longest x1 41.6 us: body(): lax.psum(jnp.sum(multiplicity * centered * centered), ('replay', 'mp'))]
    all_gather x2 -> x0, waiting for transfers between devices: 73.6 us -> none  [the longest x1 73.6 us: body(): actor_policy = lax.all_gather(actor_low, 'mp', axis=0, tiled=True)]
    ppermute x0 -> x48, starting transfers between devices: none -> 56.6 us  [permute(): return lax.ppermute(value, ALL, pairs)]
    ppermute x0 -> x48, waiting for transfers between devices: none -> 50.3 us  [permute(): return lax.ppermute(value, ALL, pairs)]
    all_to_all x5 -> x0, waiting for transfers between devices: 48 us -> none  [the longest x1 44.3 us: body(): lax.all_to_all(features[asked_safe], 'replay', split_axis=0, concat_axis=...]
    pallas_call x0 -> x8, Pallas kernels: none -> 38 us  [the longest x1 16.1 us: signal_and_gradient(): pl.pallas_call(functools.partial(signal_kernel, plan), in_specs=[SMEM, VM...]
    all_to_all x5 -> x0, starting transfers between devices: 17.8 us -> none  [the longest x1 4.85 us: body(): lax.all_to_all(features[asked_safe], 'replay', split_axis=0, concat_axis=...]
  transfers between devices with their start and end apart: 8 -> 48, of which waited for: 6 -> 19; matrix products, arithmetic and copies ran while one was open for 7% -> 9% of each run, Pallas kernels for 0% -> 6%
where the time goes in v1:
time: 176 us
  starting transfers between devices  56.6 us (32%)
  waiting for transfers between devices  50.3 us (29%)
  Pallas kernels  38 us (22%)
  local copies, waits for them, and re-layouts  20.9 us (12%)
  other arithmetic  7.4 us (4%)
  between operations  2.44 us (1%)
    ppermute x48, starting transfers between devices, permute(): return lax.ppermute(value, ALL, pairs)  56.6 us
    ppermute x48, waiting for transfers between devices, permute(): return lax.ppermute(value, ALL, pairs)  50.3 us
    pallas_call x1, Pallas kernels, signal_and_gradient(): pl.pallas_call(functools.partial(signal_kernel, plan), in_specs=[SMEM, VM...  16.1 us
    unnamed x40, local copies, waits for them, and re-layouts  10.6 us
    pallas_call x1, Pallas kernels, signal_and_gradient(): pl.pallas_call(functools.partial(gradient_kernel, plan, j), in_specs=[SME...  5.95 us
    pallas_call x2, Pallas kernels, own_update(): pl.pallas_call(functools.partial(update_kernel, len(terms)), grid_spec=pl...  5.38 us
    pallas_call x1, Pallas kernels, assemble(): pl.pallas_call(functools.partial(assemble_kernel, plan), in_specs=[SMEM]...  4.45 us
  transfers between devices with their start and end apart: 48, of which 19 were waited for; matrix products, arithmetic and copies ran while one was open for 9% of the time, Pallas kernels for 6%

profile of v1, /device:TPU:0, one launch (start us, length us, event | category | flops | bytes accessed | tf_op | source)
XLA Modules:
  0.0 175.6 jit_solution(1806661016589501146)
XLA Ops:
  0.7 1.8 %shard.1 = bf16[2,128,256]{2,1,0:T(8,128)(2,1)} custom-call(s32[1]{0:T(128)} %bitcast.1.place_ref, f32[256,1024]{1,0:T(8,128)} %refs_3_.3), custom_call_target="tpu_custom_call" | custom-call | tf_op jit(solution)/shard_map/shard/pallas_call | solution.py:85
  3.3 5.1 %collective-permute-start.2 = (bf16[128,256]{1,0:T(8,128)(2,1)S(1)}, bf16[128,256]{1,0:T(8,128)(2,1)S(1)}, u32[]{:S(2)}, u32[]{:S(2)}) collective-permute-start(bf16[128,256]{1,0:T(8,128)(2,1)S(1)} %get-tuple-element.54), channel_id=1, source_target_pairs={{0,6},{1,7},{2,4},{3,5},{4,2},{5,3},{6,0},{7,1},{8,14},{9,15},{10,... | collective-permute-start | bytes 196616 | tf_op jit(solution)/shard_map/ppermute | solution.py:44
  9.8 1.4 reshape.99.r_ref
  14.2 2.2 %copy-done = bf16[32,32,2048]{2,1,0:T(8,128)(2,1)S(1)} copy-done((bf16[32,32,2048]{2,1,0:T(8,128)(2,1)S(1)}, bf16[32,32,2048]{2,1,0:T(8,128)(2,1)}, u32[]{:S(2)}) %copy-start) | copy-done | bytes 4194328
  16.3 2.7 %normalize.1 = (bf16[1024,2048]{1,0:T(8,128)(2,1)S(1)}, f32[16,1024]{1,0:T(8,128)S(1)}) custom-call(bf16[1024,2048]{1,0:T(8,128)(2,1)S(1)} %bitcast.128, f32[1,2048]{1,0:T(1,128)S(1)} %bitcast.129, bf16[16,2048]{1,0:T(8,128)(2,1)S(1)} %broadcast_in_dim.28.value_ref), custom_call_target="tpu_custom_call" | custom-call | flops 20971520 | bytes 8388608 | tf_op jit(solution)/shard_map/normalize/pallas_call | solution.py:146
  19.0 2.0 %copy-done.2 = bf16[1024,2048]{1,0:T(8,128)(2,1)} copy-done((bf16[1024,2048]{1,0:T(8,128)(2,1)}, bf16[1024,2048]{1,0:T(8,128)(2,1)S(1)}, u32[]{:S(2)}) %copy-start.2) | copy-done | bytes 4194328
  21.6 1.7 advantage.1
  24.0 2.3 %collective-permute-start.4 = (f32[16,128]{1,0:T(8,128)S(1)}, f32[16,128]{1,0:T(8,128)S(1)}, u32[]{:S(2)}, u32[]{:S(2)}) collective-permute-start(f32[16,128]{1,0:T(8,128)S(1)} %get-tuple-element.64), channel_id=1, source_target_pairs={{0,4},{1,5},{2,6},{3,7},{4,0},{5,1},{6,2},{7,3},{8,12},{9,13},{10,... | collective-permute-start | bytes 24584 | tf_op jit(solution)/shard_map/ppermute | solution.py:44
  26.2 2.0 %collective-permute-start.3 = (f32[16,128]{1,0:T(8,128)S(1)}, f32[16,128]{1,0:T(8,128)S(1)}, u32[]{:S(2)}, u32[]{:S(2)}) collective-permute-start(f32[16,128]{1,0:T(8,128)S(1)} %get-tuple-element.64), channel_id=1, source_target_pairs={{0,2},{1,3},{2,0},{3,1},{4,6},{5,7},{6,4},{7,5},{8,10},{9,11},{10,... | collective-permute-start | bytes 24584 | tf_op jit(solution)/shard_map/ppermute | solution.py:44
  28.4 3.7 %collective-permute-start.15 = (bf16[128,256]{1,0:T(8,128)(2,1)S(1)}, bf16[128,256]{1,0:T(8,128)(2,1)S(1)}, u32[]{:S(2)}, u32[]{:S(2)}) collective-permute-start(bf16[128,256]{1,0:T(8,128)(2,1)S(1)} %get-tuple-element.55), channel_id=1, source_target_pairs={{0,6},{1,7},{2,4},{3,5},{4,2},{5,3},{6,0},{7,1},{8,14},{9,15},{10,... | collective-permute-start | bytes 196616 | tf_op jit(solution)/shard_map/ppermute | solution.py:44
  32.8 1.0 collective-permute-done.5
  33.8 1.4 collective-permute-start.6
  35.2 2.1 %collective-permute-done.14 = bf16[128,256]{1,0:T(8,128)(2,1)S(1)} collective-permute-done((bf16[128,256]{1,0:T(8,128)(2,1)S(1)}, bf16[128,256]{1,0:T(8,128)(2,1)S(1)}, u32[]{:S(2)}, u32[]{:S(2)}) %collective-permute-start.14) | collective-permute-done | bytes 65568 | tf_op jit(solution)/shard_map/ppermute | solution.py:44
  37.3 1.6 collective-permute-start.16
  39.4 1.7 collective-permute-start.7
  41.3 3.3 %collective-permute-done.7 = f32[2,4,16,128]{3,2,1,0:T(8,128)S(1)} collective-permute-done((f32[2,4,16,128]{3,2,1,0:T(8,128)S(1)}, f32[2,4,16,128]{3,2,1,0:T(8,128)S(1)}, u32[]{:S(2)}, u32[]{:S(2)}) %collective-permute-start.7) | collective-permute-done | bytes 65568 | tf_op jit(solution)/shard_map/ppermute | solution.py:44
  44.6 1.2 collective-permute-start.8
  46.6 1.7 collective-permute-start.10
  51.6 4.3 %collective-permute-done.10.refs_1_ = bf16[2,4,128,256]{3,2,1,0:T(8,128)(2,1)S(1)} collective-permute-done((bf16[2,4,128,256]{3,2,1,0:T(8,128)(2,1)S(1)}, bf16[2,4,128,256]{3,2,1,0:T(8,128)(2,1)S(1)}, u32[]{:S(2)}, u32[]{:S(2)}) %collective-permute-start.10) | collective-permute-done | bytes 524320 | tf_op jit(solution)/shard_map/ppermute | solution.py:44
  55.9 5.6 %collective-permute-done.17.refs_5_ = bf16[2,4,128,256]{3,2,1,0:T(8,128)(2,1)S(1)} collective-permute-done((bf16[2,4,128,256]{3,2,1,0:T(8,128)(2,1)S(1)}, bf16[2,4,128,256]{3,2,1,0:T(8,128)(2,1)S(1)}, u32[]{:S(2)}, u32[]{:S(2)}) %collective-permute-start.17) | collective-permute-done | bytes 524320 | tf_op jit(solution)/shard_map/ppermute | solution.py:44
  68.3 16.1 %signal.1 = (bf16[1024,1024]{1,0:T(8,128)(2,1)}, f32[2,2,4,128,256]{4,3,2,1,0:T(8,128)}, bf16[2,2,4,128,256]{4,3,2,1,0:T(8,128)(2,1)S(1)}) custom-call(s32[4]{0:T(128)S(1)} %pad_add_fusion.here_ref, f32[1,1024]{1,0:T(1,128)S(1)} %reshape_squeeze.7.w_ref, s32[1,1024]{1,0:T(1,128)S(1)} %reshape.97.act_ref, ...), custom_call_target="tpu_custom_call" | custom-call | flops 6442450944 | bytes 10485760 | tf_op jit(solution)/shard_map/signal/pallas_call | solution.py:308
  84.9 1.6 copy-done.7
  86.5 6.0 %gradient.1 = (f32[2,2,4,128,256]{4,3,2,1,0:T(8,128)S(1)}, bf16[2,2,4,128,256]{4,3,2,1,0:T(8,128)(2,1)S(1)}) custom-call(s32[4]{0:T(128)S(1)} %pad_add_fusion.here_ref, bf16[1024,1024]{1,0:T(8,128)(2,1)S(1)} %copy-done.7, bf16[1024,2048]{1,0:T(8,128)(2,1)} %copy-done.2), custom_call_target="tpu_custom_call" | custom-call | flops 2147483648 | bytes 6291456 | tf_op jit(solution)/shard_map/gradient/pallas_call | solution.py:331
  92.9 1.6 collective-permute-start.21
  95.5 1.7 collective-permute-start.34
  97.1 5.0 %collective-permute-done.21 = bf16[2,4,128,256]{3,2,1,0:T(8,128)(2,1)S(1)} collective-permute-done((bf16[2,4,128,256]{3,2,1,0:T(8,128)(2,1)S(1)}, bf16[2,4,128,256]{3,2,1,0:T(8,128)(2,1)S(1)}, u32[]{:S(2)}, u32[]{:S(2)}) %collective-permute-start.21) | collective-permute-done | bytes 524320 | tf_op jit(solution)/shard_map/ppermute | solution.py:44
  102.3 1.6 collective-permute-start.22
  103.9 6.7 %collective-permute-done.34 = bf16[2,4,128,256]{3,2,1,0:T(8,128)(2,1)S(1)} collective-permute-done((bf16[2,4,128,256]{3,2,1,0:T(8,128)(2,1)S(1)}, bf16[2,4,128,256]{3,2,1,0:T(8,128)(2,1)S(1)}, u32[]{:S(2)}, u32[]{:S(2)}) %collective-permute-start.34) | collective-permute-done | bytes 524320 | tf_op jit(solution)/shard_map/ppermute | solution.py:44
  110.7 1.6 collective-permute-start.35
  112.4 1.8 %collective-permute-start.25 = (bf16[128,256]{1,0:T(8,128)(2,1)S(1)}, bf16[128,256]{1,0:T(8,128)(2,1)S(1)}, u32[]{:S(2)}, u32[]{:S(2)}) collective-permute-start(bf16[128,256]{1,0:T(8,128)(2,1)S(1)} %get-tuple-element.48), channel_id=1, source_target_pairs={{0,6},{1,7},{2,4},{3,5},{4,2},{5,3},{6,0},{7,1},{8,14},{9,15},{10,... | collective-permute-start | bytes 196616 | tf_op jit(solution)/shard_map/ppermute | solution.py:44
  114.5 2.4 %collective-permute-start.23 = (bf16[128,256]{1,0:T(8,128)(2,1)S(1)}, bf16[128,256]{1,0:T(8,128)(2,1)S(1)}, u32[]{:S(2)}, u32[]{:S(2)}) collective-permute-start(bf16[128,256]{1,0:T(8,128)(2,1)S(1)} %get-tuple-element.50), channel_id=1, source_target_pairs={{0,2},{1,3},{2,0},{3,1},{4,6},{5,7},{6,4},{7,5},{8,10},{9,11},{10,... | collective-permute-start | bytes 196616 | tf_op jit(solution)/shard_map/ppermute | solution.py:44
  117.3 1.9 %collective-permute-start.38 = (bf16[128,256]{1,0:T(8,128)(2,1)S(1)}, bf16[128,256]{1,0:T(8,128)(2,1)S(1)}, u32[]{:S(2)}, u32[]{:S(2)}) collective-permute-start(bf16[128,256]{1,0:T(8,128)(2,1)S(1)} %get-tuple-element.43), channel_id=1, source_target_pairs={{0,6},{1,7},{2,4},{3,5},{4,2},{5,3},{6,0},{7,1},{8,14},{9,15},{10,... | collective-permute-start | bytes 196616 | tf_op jit(solution)/shard_map/ppermute | solution.py:44
  120.0 2.4 %collective-permute-start.36 = (bf16[128,256]{1,0:T(8,128)(2,1)S(1)}, bf16[128,256]{1,0:T(8,128)(2,1)S(1)}, u32[]{:S(2)}, u32[]{:S(2)}) collective-permute-start(bf16[128,256]{1,0:T(8,128)(2,1)S(1)} %get-tuple-element.45), channel_id=1, source_target_pairs={{0,2},{1,3},{2,0},{3,1},{4,6},{5,7},{6,4},{7,5},{8,10},{9,11},{10,... | collective-permute-start | bytes 196616 | tf_op jit(solution)/shard_map/ppermute | solution.py:44
  123.1 2.7 %update.2 = (f32[256,128]{1,0:T(8,128)}, bf16[256,128]{1,0:T(8,128)(2,1)}) custom-call(s32[1]{0:T(128)} %bitcast.1.place_ref, f32[1,1]{1,0:T(1,128)} %bitcast.32.mass_ref, f32[128,256]{1,0:T(8,128)} %slice_bitcast_fusion.5.base_ref, bf16[128,256]{1,0:T(8,128)(2,1)} %copy-done.17, bf16[128,256]{1,0:T(8,128)(2,1)} %copy-done.15, bf16[128,256]{1,0:T(8,128)(2,1)} %copy-done.14, ...), custom_call_target="tpu_custom_call" | custom-call | tf_op jit(solution)/shard_map/update/pallas_call | solution.py:117
  125.8 1.8 %collective-permute-start.28 = (bf16[256,128]{1,0:T(8,128)(2,1)}, bf16[256,128]{1,0:T(8,128)(2,1)S(1)}, u32[]{:S(2)}, u32[]{:S(2)}) collective-permute-start(bf16[256,128]{1,0:T(8,128)(2,1)} %get-tuple-element.24), channel_id=1, source_target_pairs={{0,6},{1,7},{2,4},{3,5},{4,2},{5,3},{6,0},{7,1},{8,14},{9,15},{10,... | collective-permute-start | bytes 196616 | tf_op jit(solution)/shard_map/ppermute | solution.py:44
  127.6 2.6 %collective-permute-start.26 = (bf16[256,128]{1,0:T(8,128)(2,1)}, bf16[256,128]{1,0:T(8,128)(2,1)S(1)}, u32[]{:S(2)}, u32[]{:S(2)}) collective-permute-start(bf16[256,128]{1,0:T(8,128)(2,1)} %get-tuple-element.24), channel_id=1, source_target_pairs={{0,2},{1,3},{2,0},{3,1},{4,6},{5,7},{6,4},{7,5},{8,10},{9,11},{10,... | collective-permute-start | bytes 196616 | tf_op jit(solution)/shard_map/ppermute | solution.py:44
  132.1 2.7 %update.3 = (f32[256,128]{1,0:T(8,128)}, bf16[256,128]{1,0:T(8,128)(2,1)}) custom-call(s32[1]{0:T(128)} %bitcast.1.place_ref, f32[1,1]{1,0:T(1,128)} %bitcast.32.mass_ref, f32[128,256]{1,0:T(8,128)} %slice_bitcast_fusion.4.base_ref, bf16[128,256]{1,0:T(8,128)(2,1)} %copy-done.16, bf16[128,256]{1,0:T(8,128)(2,1)} %copy-done.13, bf16[128,256]{1,0:T(8,128)(2,1)} %copy-done.12, ...), custom_call_target="tpu_custom_call" | custom-call | tf_op jit(solution)/shard_map/update/pallas_call | solution.py:117
  134.8 1.9 %collective-permute-start.41 = (bf16[256,128]{1,0:T(8,128)(2,1)}, bf16[256,128]{1,0:T(8,128)(2,1)S(1)}, u32[]{:S(2)}, u32[]{:S(2)}) collective-permute-start(bf16[256,128]{1,0:T(8,128)(2,1)} %get-tuple-element.28), channel_id=1, source_target_pairs={{0,6},{1,7},{2,4},{3,5},{4,2},{5,3},{6,0},{7,1},{8,14},{9,15},{10,... | collective-permute-start | bytes 196616 | tf_op jit(solution)/shard_map/ppermute | solution.py:44
  136.6 2.6 %collective-permute-start.39 = (bf16[256,128]{1,0:T(8,128)(2,1)}, bf16[256,128]{1,0:T(8,128)(2,1)S(1)}, u32[]{:S(2)}, u32[]{:S(2)}) collective-permute-start(bf16[256,128]{1,0:T(8,128)(2,1)} %get-tuple-element.28), channel_id=1, source_target_pairs={{0,2},{1,3},{2,0},{3,1},{4,6},{5,7},{6,4},{7,5},{8,10},{9,11},{10,... | collective-permute-start | bytes 196616 | tf_op jit(solution)/shard_map/ppermute | solution.py:44
  139.3 1.6 collective-permute-start.29
  141.1 1.4 collective-permute-done.40
  143.4 1.6 collective-permute-start.42
  145.0 3.3 %collective-permute-done.29 = bf16[4,256,128]{2,1,0:T(8,128)(2,1)S(1)} collective-permute-done((bf16[4,256,128]{2,1,0:T(8,128)(2,1)S(1)}, bf16[4,256,128]{2,1,0:T(8,128)(2,1)S(1)}, u32[]{:S(2)}, u32[]{:S(2)}) %collective-permute-start.29) | collective-permute-done | bytes 262176 | tf_op jit(solution)/shard_map/ppermute | solution.py:44
  148.3 1.6 collective-permute-start.30
  149.9 4.0 %collective-permute-done.42 = bf16[4,256,128]{2,1,0:T(8,128)(2,1)S(1)} collective-permute-done((bf16[4,256,128]{2,1,0:T(8,128)(2,1)S(1)}, bf16[4,256,128]{2,1,0:T(8,128)(2,1)S(1)}, u32[]{:S(2)}, u32[]{:S(2)}) %collective-permute-start.42) | collective-permute-done | bytes 262176 | tf_op jit(solution)/shard_map/ppermute | solution.py:44
  153.9 1.6 collective-permute-start.43
  157.0 9.0 %collective-permute-done.46 = f32[2,256,128]{2,1,0:T(8,128)S(1)} collective-permute-done((f32[2,256,128]{2,1,0:T(8,128)S(1)}, f32[2,256,128]{2,1,0:T(8,128)S(1)}, u32[]{:S(2)}, u32[]{:S(2)}) %collective-permute-start.46) | collective-permute-done | bytes 262176 | tf_op jit(solution)/shard_map/ppermute | solution.py:44
  171.1 4.4 %assemble.1 = (bf16[2048,1024]{1,0:T(8,128)(2,1)}, f32[256,1024]{1,0:T(8,128)}) custom-call(s32[4]{0:T(128)S(1)} %pad_add_fusion.here_ref, bf16[2,4,256,128]{3,2,1,0:T(8,128)(2,1)S(1)} %pad_maximum_fusion.2.refs_0_, bf16[2,4,256,128]{3,2,1,0:T(8,128)(2,1)S(1)} %collective-permute-done.30.refs_1_, bf16[2,4,256,128]{3,2,1,0:T(8,128)(2,1)} %collective-permute-done.31.refs_2_, ...), custom_call_target="tpu_custom_call" | custom-call | tf_op jit(solution)/shard_map/assemble/pallas_call | solution.py:388
  (159 shorter events, 31.6 us)
Async XLA Ops:
  3.3 10.7 %collective-permute-start.2 = (bf16[128,256]{1,0:T(8,128)(2,1)S(1)}, bf16[128,256]{1,0:T(8,128)(2,1)S(1)}, u32[]{:S(2)}, u32[]{:S(2)}) collective-permute-start(bf16[128,256]{1,0:T(8,128)(2,1)S(1)} %get-tuple-element.54), channel_id=1, source_target_pairs={{0,6},{1,7},{2,4},{3,5},{4,2},{5,3},{6,0},{7,1},{8,14},{9,15},{10,... | collective-permute-start | bytes 196616 | tf_op jit(solution)/shard_map/ppermute | solution.py:44
  8.5 5.6 %collective-permute-start.1 = (bf16[128,256]{1,0:T(8,128)(2,1)S(1)}, bf16[128,256]{1,0:T(8,128)(2,1)S(1)}, u32[]{:S(2)}, u32[]{:S(2)}) collective-permute-start(bf16[128,256]{1,0:T(8,128)(2,1)S(1)} %get-tuple-element.54), channel_id=1, source_target_pairs={{0,4},{1,5},{2,6},{3,7},{4,0},{5,1},{6,2},{7,3},{8,12},{9,13},{10,... | collective-permute-start | bytes 196616 | tf_op jit(solution)/shard_map/ppermute | solution.py:44
  8.5 5.6 %collective-permute-start = (bf16[128,256]{1,0:T(8,128)(2,1)S(1)}, bf16[128,256]{1,0:T(8,128)(2,1)S(1)}, u32[]{:S(2)}, u32[]{:S(2)}) collective-permute-start(bf16[128,256]{1,0:T(8,128)(2,1)S(1)} %get-tuple-element.54), channel_id=1, source_target_pairs={{0,2},{1,3},{2,0},{3,1},{4,6},{5,7},{6,4},{7,5},{8,10},{9,11},{10,... | collective-permute-start | bytes 196616 | tf_op jit(solution)/shard_map/ppermute | solution.py:44
  24.0 8.1 %collective-permute-start.4 = (f32[16,128]{1,0:T(8,128)S(1)}, f32[16,128]{1,0:T(8,128)S(1)}, u32[]{:S(2)}, u32[]{:S(2)}) collective-permute-start(f32[16,128]{1,0:T(8,128)S(1)} %get-tuple-element.64), channel_id=1, source_target_pairs={{0,4},{1,5},{2,6},{3,7},{4,0},{5,1},{6,2},{7,3},{8,12},{9,13},{10,... | collective-permute-start | bytes 24584 | tf_op jit(solution)/shard_map/ppermute | solution.py:44
  26.2 6.5 %collective-permute-start.3 = (f32[16,128]{1,0:T(8,128)S(1)}, f32[16,128]{1,0:T(8,128)S(1)}, u32[]{:S(2)}, u32[]{:S(2)}) collective-permute-start(f32[16,128]{1,0:T(8,128)S(1)} %get-tuple-element.64), channel_id=1, source_target_pairs={{0,2},{1,3},{2,0},{3,1},{4,6},{5,7},{6,4},{7,5},{8,10},{9,11},{10,... | collective-permute-start | bytes 24584 | tf_op jit(solution)/shard_map/ppermute | solution.py:44
  28.3 5.6 %collective-permute-start.5 = (f32[16,128]{1,0:T(8,128)S(1)}, f32[16,128]{1,0:T(8,128)S(1)}, u32[]{:S(2)}, u32[]{:S(2)}) collective-permute-start(f32[16,128]{1,0:T(8,128)S(1)} %get-tuple-element.64), channel_id=1, source_target_pairs={{0,6},{1,7},{2,4},{3,5},{4,2},{5,3},{6,0},{7,1},{8,14},{9,15},{10,... | collective-permute-start | bytes 24584 | tf_op jit(solution)/shard_map/ppermute | solution.py:44
  28.4 6.8 %collective-permute-start.15 = (bf16[128,256]{1,0:T(8,128)(2,1)S(1)}, bf16[128,256]{1,0:T(8,128)(2,1)S(1)}, u32[]{:S(2)}, u32[]{:S(2)}) collective-permute-start(bf16[128,256]{1,0:T(8,128)(2,1)S(1)} %get-tuple-element.55), channel_id=1, source_target_pairs={{0,6},{1,7},{2,4},{3,5},{4,2},{5,3},{6,0},{7,1},{8,14},{9,15},{10,... | collective-permute-start | bytes 196616 | tf_op jit(solution)/shard_map/ppermute | solution.py:44
  32.1 5.2 %collective-permute-start.14 = (bf16[128,256]{1,0:T(8,128)(2,1)S(1)}, bf16[128,256]{1,0:T(8,128)(2,1)S(1)}, u32[]{:S(2)}, u32[]{:S(2)}) collective-permute-start(bf16[128,256]{1,0:T(8,128)(2,1)S(1)} %get-tuple-element.55), channel_id=1, source_target_pairs={{0,4},{1,5},{2,6},{3,7},{4,0},{5,1},{6,2},{7,3},{8,12},{9,13},{10,... | collective-permute-start | bytes 196616 | tf_op jit(solution)/shard_map/ppermute | solution.py:44
  32.1 5.2 %collective-permute-start.13 = (bf16[128,256]{1,0:T(8,128)(2,1)S(1)}, bf16[128,256]{1,0:T(8,128)(2,1)S(1)}, u32[]{:S(2)}, u32[]{:S(2)}) collective-permute-start(bf16[128,256]{1,0:T(8,128)(2,1)S(1)} %get-tuple-element.55), channel_id=1, source_target_pairs={{0,2},{1,3},{2,0},{3,1},{4,6},{5,7},{6,4},{7,5},{8,10},{9,11},{10,... | collective-permute-start | bytes 196616 | tf_op jit(solution)/shard_map/ppermute | solution.py:44
  33.8 5.6 %collective-permute-start.6 = (f32[4,16,128]{2,1,0:T(8,128)S(1)}, f32[4,16,128]{2,1,0:T(8,128)S(1)}, u32[]{:S(2)}, u32[]{:S(2)}) collective-permute-start(f32[4,16,128]{2,1,0:T(8,128)S(1)} %get-tuple-element.62), channel_id=1, source_target_pairs={{0,1},{1,0},{2,3},{3,2},{4,5},{5,4},{6,7},{7,6},{8,9},{9,8},{10,11... | collective-permute-start | bytes 98312 | tf_op jit(solution)/shard_map/ppermute | solution.py:44
  37.3 11.0 %collective-permute-start.16 = (bf16[4,128,256]{2,1,0:T(8,128)(2,1)S(1)}, bf16[4,128,256]{2,1,0:T(8,128)(2,1)S(1)}, u32[]{:S(2)}, u32[]{:S(2)}) collective-permute-start(bf16[4,128,256]{2,1,0:T(8,128)(2,1)S(1)} %get-tuple-element.52), channel_id=1, source_target_pairs={{0,1},{1,0},{2,3},{3,2},{4,5},{5,4},{6,7},{7,6},{8,24},{9,25},{10,... | collective-permute-start | bytes 786440 | tf_op jit(solution)/shard_map/ppermute | solution.py:44
  39.0 7.6 %collective-permute-start.9 = (bf16[4,128,256]{2,1,0:T(8,128)(2,1)S(1)}, bf16[4,128,256]{2,1,0:T(8,128)(2,1)S(1)}, u32[]{:S(2)}, u32[]{:S(2)}) collective-permute-start(bf16[4,128,256]{2,1,0:T(8,128)(2,1)S(1)} %pad_maximum_fusion.5), channel_id=1, source_target_pairs={{0,1},{1,0},{2,3},{3,2},{4,5},{5,4},{6,7},{7,6},{8,24},{9,25},{10,... | collective-permute-start | bytes 786440 | tf_op jit(solution)/shard_map/ppermute | solution.py:44
  39.4 5.1 %collective-permute-start.7 = (f32[2,4,16,128]{3,2,1,0:T(8,128)S(1)}, f32[2,4,16,128]{3,2,1,0:T(8,128)S(1)}, u32[]{:S(2)}, u32[]{:S(2)}) collective-permute-start(f32[2,4,16,128]{3,2,1,0:T(8,128)S(1)} %get-tuple-element.60), channel_id=1, source_target_pairs={{0,16},{1,17},{2,18},{3,19},{4,20},{5,21},{6,22},{7,23},{8,24},{9,... | collective-permute-start | bytes 196616 | tf_op jit(solution)/shard_map/ppermute | solution.py:44
  44.6 4.3 %collective-permute-start.8 = (f32[2,2,4,16,128]{4,3,2,1,0:T(8,128)S(1)}, f32[2,2,4,16,128]{4,3,2,1,0:T(8,128)S(1)}, u32[]{:S(2)}, u32[]{:S(2)}) collective-permute-start(f32[2,2,4,16,128]{4,3,2,1,0:T(8,128)S(1)} %get-tuple-element.58), channel_id=1, source_target_pairs={{0,8},{1,9},{2,10},{3,11},{4,12},{5,13},{6,14},{7,15},{8,0},{9,1},... | collective-permute-start | bytes 393224 | tf_op jit(solution)/shard_map/ppermute | solution.py:44
  46.6 9.2 %collective-permute-start.10 = (bf16[2,4,128,256]{3,2,1,0:T(8,128)(2,1)S(1)}, bf16[2,4,128,256]{3,2,1,0:T(8,128)(2,1)S(1)}, u32[]{:S(2)}, u32[]{:S(2)}) collective-permute-start(bf16[2,4,128,256]{3,2,1,0:T(8,128)(2,1)S(1)} %pad_maximum_fusion.refs_0_), channel_id=1, source_target_pairs={{0,16},{1,17},{2,18},{3,19},{4,20},{5,21},{6,22},{7,23},{8,9},{9,8... | collective-permute-start | bytes 1572872 | tf_op jit(solution)/shard_map/ppermute | solution.py:44
  48.3 13.2 %collective-permute-start.17 = (bf16[2,4,128,256]{3,2,1,0:T(8,128)(2,1)S(1)}, bf16[2,4,128,256]{3,2,1,0:T(8,128)(2,1)S(1)}, u32[]{:S(2)}, u32[]{:S(2)}) collective-permute-start(bf16[2,4,128,256]{3,2,1,0:T(8,128)(2,1)S(1)} %pad_maximum_fusion.1.refs_4_), channel_id=1, source_target_pairs={{0,16},{1,17},{2,18},{3,19},{4,20},{5,21},{6,22},{7,23},{8,9},{9,8... | collective-permute-start | bytes 1572872 | tf_op jit(solution)/shard_map/ppermute | solution.py:44
  51.0 14.3 %collective-permute-start.11 = (bf16[2,4,128,256]{3,2,1,0:T(8,128)(2,1)S(1)}, bf16[2,4,128,256]{3,2,1,0:T(8,128)(2,1)S(1)}, u32[]{:S(2)}, u32[]{:S(2)}) collective-permute-start(bf16[2,4,128,256]{3,2,1,0:T(8,128)(2,1)S(1)} %pad_maximum_fusion.refs_0_), channel_id=1, source_target_pairs={{0,8},{1,9},{2,10},{3,11},{4,12},{5,13},{6,14},{7,15},{8,0},{9,1},... | collective-permute-start | bytes 1572872 | tf_op jit(solution)/shard_map/ppermute | solution.py:44
  51.1 15.1 %collective-permute-start.18 = (bf16[2,4,128,256]{3,2,1,0:T(8,128)(2,1)S(1)}, bf16[2,4,128,256]{3,2,1,0:T(8,128)(2,1)}, u32[]{:S(2)}, u32[]{:S(2)}) collective-permute-start(bf16[2,4,128,256]{3,2,1,0:T(8,128)(2,1)S(1)} %pad_maximum_fusion.1.refs_4_), channel_id=1, source_target_pairs={{0,8},{1,9},{2,10},{3,11},{4,12},{5,13},{6,14},{7,15},{8,0},{9,1},... | collective-permute-start | bytes 1572872 | tf_op jit(solution)/shard_map/ppermute | solution.py:44
  55.9 10.3 %collective-permute-start.12 = (bf16[2,4,128,256]{3,2,1,0:T(8,128)(2,1)S(1)}, bf16[2,4,128,256]{3,2,1,0:T(8,128)(2,1)}, u32[]{:S(2)}, u32[]{:S(2)}) collective-permute-start(bf16[2,4,128,256]{3,2,1,0:T(8,128)(2,1)S(1)} %collective-permute-done.10.refs_1_), channel_id=1, source_target_pairs={{0,8},{1,9},{2,10},{3,11},{4,12},{5,13},{6,14},{7,15},{8,0},{9,1},... | collective-permute-start | bytes 1572872 | tf_op jit(solution)/shard_map/ppermute | solution.py:44
  61.5 4.7 %collective-permute-start.19 = (bf16[2,4,128,256]{3,2,1,0:T(8,128)(2,1)S(1)}, bf16[2,4,128,256]{3,2,1,0:T(8,128)(2,1)}, u32[]{:S(2)}, u32[]{:S(2)}) collective-permute-start(bf16[2,4,128,256]{3,2,1,0:T(8,128)(2,1)S(1)} %collective-permute-done.17.refs_5_), channel_id=1, source_target_pairs={{0,8},{1,9},{2,10},{3,11},{4,12},{5,13},{6,14},{7,15},{8,0},{9,1},... | collective-permute-start | bytes 1572872 | tf_op jit(solution)/shard_map/ppermute | solution.py:44
  84.4 8.2 %collective-permute-start.20 = (bf16[2,2,4,128,256]{4,3,2,1,0:T(8,128)(2,1)S(1)}, bf16[2,2,4,128,256]{4,3,2,1,0:T(8,128)(2,1)S(1)}, u32[]{:S(2)}, u32[]{:S(2)}) collective-permute-start(bf16[2,2,4,128,256]{4,3,2,1,0:T(8,128)(2,1)S(1)} %get-tuple-element.23), channel_id=1, source_target_pairs={{0,8},{1,9},{2,10},{3,11},{4,12},{5,13},{6,14},{7,15},{8,0},{9,1},... | collective-permute-start | bytes 3145736 | tf_op jit(solution)/shard_map/ppermute | solution.py:44
  92.4 2.7 %collective-permute-start.33 = (bf16[2,2,4,128,256]{4,3,2,1,0:T(8,128)(2,1)S(1)}, bf16[2,2,4,128,256]{4,3,2,1,0:T(8,128)(2,1)S(1)}, u32[]{:S(2)}, u32[]{:S(2)}) collective-permute-start(bf16[2,2,4,128,256]{4,3,2,1,0:T(8,128)(2,1)S(1)} %get-tuple-element.27), channel_id=1, source_target_pairs={{0,8},{1,9},{2,10},{3,11},{4,12},{5,13},{6,14},{7,15},{8,0},{9,1},... | collective-permute-start | bytes 3145736 | tf_op jit(solution)/shard_map/ppermute | solution.py:44
  92.9 9.2 %collective-permute-start.21 = (bf16[2,4,128,256]{3,2,1,0:T(8,128)(2,1)S(1)}, bf16[2,4,128,256]{3,2,1,0:T(8,128)(2,1)S(1)}, u32[]{:S(2)}, u32[]{:S(2)}) collective-permute-start(bf16[2,4,128,256]{3,2,1,0:T(8,128)(2,1)S(1)} %fusion.2), channel_id=1, source_target_pairs={{0,16},{1,17},{2,18},{3,19},{4,20},{5,21},{6,22},{7,23},{8,9},{9,8... | collective-permute-start | bytes 1572872 | tf_op jit(solution)/shard_map/ppermute | solution.py:44
  95.5 15.1 %collective-permute-start.34 = (bf16[2,4,128,256]{3,2,1,0:T(8,128)(2,1)S(1)}, bf16[2,4,128,256]{3,2,1,0:T(8,128)(2,1)S(1)}, u32[]{:S(2)}, u32[]{:S(2)}) collective-permute-start(bf16[2,4,128,256]{3,2,1,0:T(8,128)(2,1)S(1)} %fusion.3), channel_id=1, source_target_pairs={{0,16},{1,17},{2,18},{3,19},{4,20},{5,21},{6,22},{7,23},{8,9},{9,8... | collective-permute-start | bytes 1572872 | tf_op jit(solution)/shard_map/ppermute | solution.py:44
  102.3 10.0 %collective-permute-start.22 = (bf16[4,128,256]{2,1,0:T(8,128)(2,1)S(1)}, bf16[4,128,256]{2,1,0:T(8,128)(2,1)S(1)}, u32[]{:S(2)}, u32[]{:S(2)}) collective-permute-start(bf16[4,128,256]{2,1,0:T(8,128)(2,1)S(1)} %fusion.6), channel_id=1, source_target_pairs={{0,1},{1,0},{2,3},{3,2},{4,5},{5,4},{6,7},{7,6},{8,24},{9,25},{10,... | collective-permute-start | bytes 786440 | tf_op jit(solution)/shard_map/ppermute | solution.py:44
  110.7 6.4 %collective-permute-start.35 = (bf16[4,128,256]{2,1,0:T(8,128)(2,1)S(1)}, bf16[4,128,256]{2,1,0:T(8,128)(2,1)S(1)}, u32[]{:S(2)}, u32[]{:S(2)}) collective-permute-start(bf16[4,128,256]{2,1,0:T(8,128)(2,1)S(1)} %fusion.7), channel_id=1, source_target_pairs={{0,1},{1,0},{2,3},{3,2},{4,5},{5,4},{6,7},{7,6},{8,24},{9,25},{10,... | collective-permute-start | bytes 786440 | tf_op jit(solution)/shard_map/ppermute | solution.py:44
  112.4 7.6 %collective-permute-start.25 = (bf16[128,256]{1,0:T(8,128)(2,1)S(1)}, bf16[128,256]{1,0:T(8,128)(2,1)S(1)}, u32[]{:S(2)}, u32[]{:S(2)}) collective-permute-start(bf16[128,256]{1,0:T(8,128)(2,1)S(1)} %get-tuple-element.48), channel_id=1, source_target_pairs={{0,6},{1,7},{2,4},{3,5},{4,2},{5,3},{6,0},{7,1},{8,14},{9,15},{10,... | collective-permute-start | bytes 196616 | tf_op jit(solution)/shard_map/ppermute | solution.py:44
  114.3 8.1 %collective-permute-start.24 = (bf16[128,256]{1,0:T(8,128)(2,1)S(1)}, bf16[128,256]{1,0:T(8,128)(2,1)S(1)}, u32[]{:S(2)}, u32[]{:S(2)}) collective-permute-start(bf16[128,256]{1,0:T(8,128)(2,1)S(1)} %get-tuple-element.49), channel_id=1, source_target_pairs={{0,4},{1,5},{2,6},{3,7},{4,0},{5,1},{6,2},{7,3},{8,12},{9,13},{10,... | collective-permute-start | bytes 196616 | tf_op jit(solution)/shard_map/ppermute | solution.py:44
  114.5 7.9 %collective-permute-start.23 = (bf16[128,256]{1,0:T(8,128)(2,1)S(1)}, bf16[128,256]{1,0:T(8,128)(2,1)S(1)}, u32[]{:S(2)}, u32[]{:S(2)}) collective-permute-start(bf16[128,256]{1,0:T(8,128)(2,1)S(1)} %get-tuple-element.50), channel_id=1, source_target_pairs={{0,2},{1,3},{2,0},{3,1},{4,6},{5,7},{6,4},{7,5},{8,10},{9,11},{10,... | collective-permute-start | bytes 196616 | tf_op jit(solution)/shard_map/ppermute | solution.py:44
  117.3 10.3 %collective-permute-start.38 = (bf16[128,256]{1,0:T(8,128)(2,1)S(1)}, bf16[128,256]{1,0:T(8,128)(2,1)S(1)}, u32[]{:S(2)}, u32[]{:S(2)}) collective-permute-start(bf16[128,256]{1,0:T(8,128)(2,1)S(1)} %get-tuple-element.43), channel_id=1, source_target_pairs={{0,6},{1,7},{2,4},{3,5},{4,2},{5,3},{6,0},{7,1},{8,14},{9,15},{10,... | collective-permute-start | bytes 196616 | tf_op jit(solution)/shard_map/ppermute | solution.py:44
  119.8 11.0 %collective-permute-start.37 = (bf16[128,256]{1,0:T(8,128)(2,1)S(1)}, bf16[128,256]{1,0:T(8,128)(2,1)S(1)}, u32[]{:S(2)}, u32[]{:S(2)}) collective-permute-start(bf16[128,256]{1,0:T(8,128)(2,1)S(1)} %get-tuple-element.44), channel_id=1, source_target_pairs={{0,4},{1,5},{2,6},{3,7},{4,0},{5,1},{6,2},{7,3},{8,12},{9,13},{10,... | collective-permute-start | bytes 196616 | tf_op jit(solution)/shard_map/ppermute | solution.py:44
  120.0 10.8 %collective-permute-start.36 = (bf16[128,256]{1,0:T(8,128)(2,1)S(1)}, bf16[128,256]{1,0:T(8,128)(2,1)S(1)}, u32[]{:S(2)}, u32[]{:S(2)}) collective-permute-start(bf16[128,256]{1,0:T(8,128)(2,1)S(1)} %get-tuple-element.45), channel_id=1, source_target_pairs={{0,2},{1,3},{2,0},{3,1},{4,6},{5,7},{6,4},{7,5},{8,10},{9,11},{10,... | collective-permute-start | bytes 196616 | tf_op jit(solution)/shard_map/ppermute | solution.py:44
  125.8 10.9 %collective-permute-start.28 = (bf16[256,128]{1,0:T(8,128)(2,1)}, bf16[256,128]{1,0:T(8,128)(2,1)S(1)}, u32[]{:S(2)}, u32[]{:S(2)}) collective-permute-start(bf16[256,128]{1,0:T(8,128)(2,1)} %get-tuple-element.24), channel_id=1, source_target_pairs={{0,6},{1,7},{2,4},{3,5},{4,2},{5,3},{6,0},{7,1},{8,14},{9,15},{10,... | collective-permute-start | bytes 196616 | tf_op jit(solution)/shard_map/ppermute | solution.py:44
  127.6 11.6 %collective-permute-start.27 = (bf16[256,128]{1,0:T(8,128)(2,1)}, bf16[256,128]{1,0:T(8,128)(2,1)S(1)}, u32[]{:S(2)}, u32[]{:S(2)}) collective-permute-start(bf16[256,128]{1,0:T(8,128)(2,1)} %get-tuple-element.24), channel_id=1, source_target_pairs={{0,4},{1,5},{2,6},{3,7},{4,0},{5,1},{6,2},{7,3},{8,12},{9,13},{10,... | collective-permute-start | bytes 196616 | tf_op jit(solution)/shard_map/ppermute | solution.py:44
  127.6 11.6 %collective-permute-start.26 = (bf16[256,128]{1,0:T(8,128)(2,1)}, bf16[256,128]{1,0:T(8,128)(2,1)S(1)}, u32[]{:S(2)}, u32[]{:S(2)}) collective-permute-start(bf16[256,128]{1,0:T(8,128)(2,1)} %get-tuple-element.24), channel_id=1, source_target_pairs={{0,2},{1,3},{2,0},{3,1},{4,6},{5,7},{6,4},{7,5},{8,10},{9,11},{10,... | collective-permute-start | bytes 196616 | tf_op jit(solution)/shard_map/ppermute | solution.py:44
  134.8 6.3 %collective-permute-start.41 = (bf16[256,128]{1,0:T(8,128)(2,1)}, bf16[256,128]{1,0:T(8,128)(2,1)S(1)}, u32[]{:S(2)}, u32[]{:S(2)}) collective-permute-start(bf16[256,128]{1,0:T(8,128)(2,1)} %get-tuple-element.28), channel_id=1, source_target_pairs={{0,6},{1,7},{2,4},{3,5},{4,2},{5,3},{6,0},{7,1},{8,14},{9,15},{10,... | collective-permute-start | bytes 196616 | tf_op jit(solution)/shard_map/ppermute | solution.py:44
  136.6 5.9 %collective-permute-start.40 = (bf16[256,128]{1,0:T(8,128)(2,1)}, bf16[256,128]{1,0:T(8,128)(2,1)S(1)}, u32[]{:S(2)}, u32[]{:S(2)}) collective-permute-start(bf16[256,128]{1,0:T(8,128)(2,1)} %get-tuple-element.28), channel_id=1, source_target_pairs={{0,4},{1,5},{2,6},{3,7},{4,0},{5,1},{6,2},{7,3},{8,12},{9,13},{10,... | collective-permute-start | bytes 196616 | tf_op jit(solution)/shard_map/ppermute | solution.py:44
  136.6 5.9 %collective-permute-start.39 = (bf16[256,128]{1,0:T(8,128)(2,1)}, bf16[256,128]{1,0:T(8,128)(2,1)S(1)}, u32[]{:S(2)}, u32[]{:S(2)}) collective-permute-start(bf16[256,128]{1,0:T(8,128)(2,1)} %get-tuple-element.28), channel_id=1, source_target_pairs={{0,2},{1,3},{2,0},{3,1},{4,6},{5,7},{6,4},{7,5},{8,10},{9,11},{10,... | collective-permute-start | bytes 196616 | tf_op jit(solution)/shard_map/ppermute | solution.py:44
  139.3 9.0 %collective-permute-start.29 = (bf16[4,256,128]{2,1,0:T(8,128)(2,1)S(1)}, bf16[4,256,128]{2,1,0:T(8,128)(2,1)S(1)}, u32[]{:S(2)}, u32[]{:S(2)}) collective-permute-start(bf16[4,256,128]{2,1,0:T(8,128)(2,1)S(1)} %get-tuple-element.47), channel_id=1, source_target_pairs={{0,1},{1,0},{2,3},{3,2},{4,5},{5,4},{6,7},{7,6},{8,24},{9,25},{10,... | collective-permute-start | bytes 786440 | tf_op jit(solution)/shard_map/ppermute | solution.py:44
  143.4 10.5 %collective-permute-start.42 = (bf16[4,256,128]{2,1,0:T(8,128)(2,1)S(1)}, bf16[4,256,128]{2,1,0:T(8,128)(2,1)S(1)}, u32[]{:S(2)}, u32[]{:S(2)}) collective-permute-start(bf16[4,256,128]{2,1,0:T(8,128)(2,1)S(1)} %get-tuple-element.42), channel_id=1, source_target_pairs={{0,1},{1,0},{2,3},{3,2},{4,5},{5,4},{6,7},{7,6},{8,24},{9,25},{10,... | collective-permute-start | bytes 786440 | tf_op jit(solution)/shard_map/ppermute | solution.py:44
  148.3 18.4 %collective-permute-start.30 = (bf16[2,4,256,128]{3,2,1,0:T(8,128)(2,1)S(1)}, bf16[2,4,256,128]{3,2,1,0:T(8,128)(2,1)S(1)}, u32[]{:S(2)}, u32[]{:S(2)}) collective-permute-start(bf16[2,4,256,128]{3,2,1,0:T(8,128)(2,1)S(1)} %pad_maximum_fusion.2.refs_0_), channel_id=1, source_target_pairs={{0,16},{1,17},{2,18},{3,19},{4,20},{5,21},{6,22},{7,23},{8,9},{9,8... | collective-permute-start | bytes 1572872 | tf_op jit(solution)/shard_map/ppermute | solution.py:44
  153.9 13.2 %collective-permute-start.43 = (bf16[2,4,256,128]{3,2,1,0:T(8,128)(2,1)S(1)}, bf16[2,4,256,128]{3,2,1,0:T(8,128)(2,1)S(1)}, u32[]{:S(2)}, u32[]{:S(2)}) collective-permute-start(bf16[2,4,256,128]{3,2,1,0:T(8,128)(2,1)S(1)} %pad_maximum_fusion.3.refs_4_), channel_id=1, source_target_pairs={{0,16},{1,17},{2,18},{3,19},{4,20},{5,21},{6,22},{7,23},{8,9},{9,8... | collective-permute-start | bytes 1572872 | tf_op jit(solution)/shard_map/ppermute | solution.py:44
  155.5 10.4 %collective-permute-start.46 = (f32[2,256,128]{2,1,0:T(8,128)S(1)}, f32[2,256,128]{2,1,0:T(8,128)S(1)}, u32[]{:S(2)}, u32[]{:S(2)}) collective-permute-start(f32[2,256,128]{2,1,0:T(8,128)S(1)} %get-tuple-element.40), channel_id=1, source_target_pairs={{0,16},{1,17},{2,18},{3,19},{4,20},{5,21},{6,22},{7,23},{8,24},{9,... | collective-permute-start | bytes 786440 | tf_op jit(solution)/shard_map/ppermute | solution.py:44
  166.0 2.5 %collective-permute-start.47 = (f32[2,2,256,128]{3,2,1,0:T(8,128)S(1)}, f32[2,2,256,128]{3,2,1,0:T(8,128)S(1)}, u32[]{:S(2)}, u32[]{:S(2)}) collective-permute-start(f32[2,2,256,128]{3,2,1,0:T(8,128)S(1)} %pad_maximum_fusion.4.refs_8_), channel_id=1, source_target_pairs={{0,8},{1,9},{2,10},{3,11},{4,12},{5,13},{6,14},{7,15},{8,0},{9,1},... | collective-permute-start | bytes 1572872 | tf_op jit(solution)/shard_map/ppermute | solution.py:44
  166.1 2.8 %collective-permute-start.31 = (bf16[2,4,256,128]{3,2,1,0:T(8,128)(2,1)S(1)}, bf16[2,4,256,128]{3,2,1,0:T(8,128)(2,1)}, u32[]{:S(2)}, u32[]{:S(2)}) collective-permute-start(bf16[2,4,256,128]{3,2,1,0:T(8,128)(2,1)S(1)} %pad_maximum_fusion.2.refs_0_), channel_id=1, source_target_pairs={{0,8},{1,9},{2,10},{3,11},{4,12},{5,13},{6,14},{7,15},{8,0},{9,1},... | collective-permute-start | bytes 1572872 | tf_op jit(solution)/shard_map/ppermute | solution.py:44
  166.6 3.0 %collective-permute-start.44 = (bf16[2,4,256,128]{3,2,1,0:T(8,128)(2,1)S(1)}, bf16[2,4,256,128]{3,2,1,0:T(8,128)(2,1)}, u32[]{:S(2)}, u32[]{:S(2)}) collective-permute-start(bf16[2,4,256,128]{3,2,1,0:T(8,128)(2,1)S(1)} %pad_maximum_fusion.3.refs_4_), channel_id=1, source_target_pairs={{0,8},{1,9},{2,10},{3,11},{4,12},{5,13},{6,14},{7,15},{8,0},{9,1},... | collective-permute-start | bytes 1572872 | tf_op jit(solution)/shard_map/ppermute | solution.py:44
  166.7 3.7 %collective-permute-start.32 = (bf16[2,4,256,128]{3,2,1,0:T(8,128)(2,1)S(1)}, bf16[2,4,256,128]{3,2,1,0:T(8,128)(2,1)}, u32[]{:S(2)}, u32[]{:S(2)}) collective-permute-start(bf16[2,4,256,128]{3,2,1,0:T(8,128)(2,1)S(1)} %collective-permute-done.30.refs_1_), channel_id=1, source_target_pairs={{0,8},{1,9},{2,10},{3,11},{4,12},{5,13},{6,14},{7,15},{8,0},{9,1},... | collective-permute-start | bytes 1572872 | tf_op jit(solution)/shard_map/ppermute | solution.py:44
  167.1 4.0 %collective-permute-start.45 = (bf16[2,4,256,128]{3,2,1,0:T(8,128)(2,1)S(1)}, bf16[2,4,256,128]{3,2,1,0:T(8,128)(2,1)}, u32[]{:S(2)}, u32[]{:S(2)}) collective-permute-start(bf16[2,4,256,128]{3,2,1,0:T(8,128)(2,1)S(1)} %collective-permute-done.43.refs_5_), channel_id=1, source_target_pairs={{0,8},{1,9},{2,10},{3,11},{4,12},{5,13},{6,14},{7,15},{8,0},{9,1},... | collective-permute-start | bytes 1572872 | tf_op jit(solution)/shard_map/ppermute | solution.py:44
  (20 other events, 134.4 us)

commit v2 on v1

v2 whole, which is shorter than its diff:
```python
import functools

import jax
import jax.numpy as jnp
from jax import lax
from jax.experimental import pallas as pl
from jax.experimental.pallas import tpu as pltpu
from jax.sharding import PartitionSpec as P

DISCOUNT = 0.97
STEP_RATE = 0.002
ALL = ("replay", "mp")
LANES = 128
BF16 = jnp.bfloat16
F32 = jnp.float32
VMEM = pl.BlockSpec(memory_space=pltpu.VMEM)
SMEM = pl.BlockSpec(memory_space=pltpu.SMEM)
ANY = pl.BlockSpec(memory_space=pl.ANY)
ROOM = pltpu.CompilerParams(vmem_limit_bytes=32 * 2**20)


class Plan:
    def __init__(self, replay, mp, actions):
        self.C = 2
        self.Y = replay // self.C
        self.Z = 4
        self.X = mp // self.Z
        self.mp = mp
        self.swap = self.X == self.Y
        self.block = LANES
        self.J = max(1, actions // (self.C * self.Y * self.block))

    def permute(self, value, axis, k):
        pairs = []
        for y in range(self.Y):
            for c in range(self.C):
                for z in range(self.Z):
                    for x in range(self.X):
                        along = axis
                        if axis in ("p", "q"):
                            along = "y" if (axis == "p") == (c == 0 or not self.swap) else "x"
                        to = dict(y=y, c=c, z=z, x=x)
                        to[along] ^= k
                        pairs.append((self.index(y, c, z, x), self.index(**to)))
        return lax.ppermute(value, ALL, pairs)

    def index(self, y, c, z, x):
        return (y * self.C + c) * self.mp + z * self.X + x

    def here(self):
        replay, mp = lax.axis_index("replay"), lax.axis_index("mp")
        return jnp.stack([replay // self.C, replay % self.C, mp // self.X, mp % self.X]).astype(jnp.int32)

    def relative(self, core, dy, dx):
        if not self.swap:
            return dy, dx
        return jnp.where(core == 0, dy, dx), jnp.where(core == 0, dx, dy)

    def gather_column(self, block):
        return [block] + [self.permute(block, "z", k) for k in range(1, self.Z)]

    def gather_rest(self, column):
        column = jnp.stack(column)
        plane = jnp.stack([column] + [self.permute(column, "q", k) for k in range(1, self.X)])
        mine = [plane] + [self.permute(plane, "p", k) for k in range(1, self.Y)]
        return mine + [self.permute(piece, "c", 1) for piece in mine]

    def reduce(self, keep, send):
        total = keep + self.permute(send, "c", 1).astype(F32)
        for axis in ("p", "q"):
            low = total[1:].astype(BF16)
            total = total[0]
            for k in range(1, low.shape[0] + 1):
                total = total + self.permute(low[k - 1], axis, k).astype(F32)
        return total[0], [total[k].astype(BF16) for k in range(1, self.Z)]

    def reduce_column(self, low):
        return [self.permute(low[k - 1], "z", k) for k in range(1, self.Z)]


def shard_kernel(plan, place_ref, w_hbm, *refs):
    outs, stage, sems = refs[: plan.J], refs[plan.J], refs[plan.J + 1]
    block = plan.block
    copies = []
    for j in range(plan.J):
        start = pl.multiple_of((j * 2 * plan.Y + place_ref[0]) * block, block)
        copy = pltpu.make_async_copy(w_hbm.at[:, pl.ds(start, block)], stage.at[j], sems.at[j])
        copy.start()
        copies.append(copy)
    for j in range(plan.J):
        copies[j].wait()
        outs[j][...] = stage[j].T.astype(BF16)


def own_shard(plan, place, policy_weight):
    depth = policy_weight.shape[0]
    block = plan.block
    return pl.pallas_call(
        functools.partial(shard_kernel, plan),
        in_specs=[SMEM, ANY],
        out_specs=[VMEM] * plan.J,
        out_shape=[jax.ShapeDtypeStruct((block, depth), BF16)] * plan.J,
        scratch_shapes=[pltpu.VMEM((plan.J, depth, block), F32), pltpu.SemaphoreType.DMA((plan.J,))],
        name="shard",
    )(place, policy_weight)


def update_kernel(count, place_ref, mass_ref, base_ref, *refs):
    terms, (w_ref, m_ref, v_ref, update_ref, low_ref) = refs[:count], refs[count:]
    total = base_ref[...]
    for term in terms:
        total = total + term[...].astype(F32)
    gradient = total.T / mass_ref[0, 0]
    first_new = 0.9 * m_ref[...] + 0.1 * gradient
    second_new = 0.95 * v_ref[...] + 0.05 * gradient * gradient
    update = first_new / (jnp.sqrt(second_new) + 1e-08)
    update_ref[...] = update
    low_ref[...] = (w_ref[...] - STEP_RATE * update).astype(BF16)


def own_update(plan, j, place, mass, base, terms, policy_weight, first_moment, second_moment):
    depth = policy_weight.shape[0]
    block = plan.block
    whole = pl.BlockSpec((block, depth), lambda i, place: (0, 0))
    own = pl.BlockSpec((depth, block), lambda i, place: (0, j * 2 * plan.Y + place[0]))
    out = pl.BlockSpec((depth, block), lambda i, place: (0, 0))
    return pl.pallas_call(
        functools.partial(update_kernel, len(terms)),
        grid_spec=pltpu.PrefetchScalarGridSpec(
            num_scalar_prefetch=1,
            grid=(1,),
            in_specs=[SMEM, whole] + [whole] * len(terms) + [own] * 3,
            out_specs=[out, out],
        ),
        out_shape=[
            jax.ShapeDtypeStruct((depth, block), F32),
            jax.ShapeDtypeStruct((depth, block), BF16),
        ],
        name="update",
    )(place, mass, base, *terms, policy_weight, first_moment, second_moment)


def spread_rows(rows, lanes):
    n, steps = rows.shape
    lane = lax.broadcasted_iota(jnp.int32, (steps, lanes), 1)
    pick = (lane % steps == lax.broadcasted_iota(jnp.int32, (steps, lanes), 0)).astype(F32).astype(BF16)
    wide = jnp.dot(rows.astype(BF16), pick, preferred_element_type=F32)
    lane = lax.broadcasted_iota(jnp.int32, (n, lanes), 1)
    own = lane // steps == lax.broadcasted_iota(jnp.int32, (n, lanes), 0)
    return jnp.sum(jnp.where(own, wide, 0.0), axis=0, keepdims=True)


def norm_kernel(x_ref, gain_ref, value_ref, r_ref, e_ref, tail_ref, ask_ref, low_ref, out_ref, block_ref, val_ref):
    wide = x_ref[...].astype(F32)
    mean_square = jnp.mean(wide * wide, axis=-1, keepdims=True)
    normed = (wide * lax.rsqrt(mean_square + 1e-05) * gain_ref[...]).astype(BF16)
    out_ref[...] = normed
    tile = normed.shape[0]
    step = pl.program_id(0)
    val_ref[:, pl.ds(pl.multiple_of(step * tile, tile), tile)] = lax.dot_general(
        value_ref[...], normed, (((1,), (1,)), ((), ())), preferred_element_type=F32
    )

    @pl.when(step == pl.num_programs(0) - 1)
    def _():
        segs, seg_len = r_ref.shape
        lanes = segs * seg_len
        lane = lax.broadcasted_iota(jnp.int32, (1, lanes), 1)
        last = lane % seg_len == seg_len - 1
        ends = spread_rows(e_ref[...].astype(F32), lanes)
        tails = spread_rows(jnp.broadcast_to(tail_ref[...].astype(F32), (segs, seg_len)), lanes)
        decay = DISCOUNT * (1.0 - ends)
        total = spread_rows(r_ref[...], lanes) + jnp.where(last, decay * tails, 0.0)
        decay = jnp.where(last, 0.0, decay)
        reach = 1
        while reach < seg_len:
            total = total + decay * pltpu.roll(total, lanes - reach, axis=1)
            decay = decay * pltpu.roll(decay, lanes - reach, axis=1)
            reach *= 2
        rest = total - val_ref[0:1, :]
        block, depth = low_ref.shape
        rows = []
        for _ in range(3):
            term = rest.astype(BF16).astype(F32)
            rest = rest - term
            rows += [term[:, i : i + depth] for i in range(0, lanes, depth)]
        rows.append(ask_ref[...])
        rows.append(jnp.zeros((block_ref.shape[0] - block - len(rows), depth), F32))
        block_ref[:block, :] = low_ref[...]
        block_ref[block:, :] = jnp.concatenate(rows, axis=0).astype(BF16)


def payload_rows(lanes, depth):
    return -(-(3 * lanes // depth + 1) // 16) * 16


def normalize(rows, norm_gain, value_weight, rewards, ends, tails, asked, low):
    tokens, width = rows.shape
    tile = 256
    block, depth = low.shape
    segs = tails.shape[0]
    high = block + payload_rows(tokens, depth)
    asked = jnp.pad(asked.astype(F32)[None, :], ((0, 0), (0, depth - asked.shape[0])))

    def whole(shape):
        return pl.BlockSpec(shape, lambda i: (0, 0))

    return pl.pallas_call(
        norm_kernel,
        grid=(tokens // tile,),
        in_specs=[
            pl.BlockSpec((tile, width), lambda i: (i, 0)),
            whole((1, width)),
            whole((16, width)),
            whole(rewards.shape),
            whole(ends.shape),
            whole((segs, 1)),
            whole((1, depth)),
            whole(low.shape),
        ],
        out_specs=[pl.BlockSpec((tile, width), lambda i: (i, 0)), whole((high, depth))],
        out_shape=[
            jax.ShapeDtypeStruct((tokens, width), BF16),
            jax.ShapeDtypeStruct((high, depth), BF16),
        ],
        scratch_shapes=[pltpu.VMEM((16, tokens), F32)],
        compiler_params=ROOM,
        cost_estimate=pl.CostEstimate(
            flops=10 * tokens * width, bytes_accessed=4 * tokens * width, transcendentals=0
        ),
        name="normalize",
    )(
        rows,
        norm_gain.reshape(1, width),
        jnp.broadcast_to(value_weight[None, :], (16, width)),
        rewards,
        ends,
        tails.reshape(segs, 1),
        asked,
        low,
    )


def weight_kernel(plan, segs, samples, total, here_ref, *refs):
    pieces, (weight_ref, mass_ref, norm_ref, known_ref) = refs[: 2 * plan.Y], refs[2 * plan.Y :]
    lanes = weight_ref.shape[1]
    steps = lanes // segs
    owners = plan.C * plan.Y
    c = here_ref[1]
    me = here_ref[0] * plan.C + c
    depth = pieces[0].shape[-1]
    parts = lanes // depth
    for other in range(2):
        for dy in range(plan.Y):
            for dx in range(plan.X):
                for dz in range(plan.Z):
                    row = (other * plan.Y + dy) * plan.mp + dx * plan.Z + dz
                    sent = pieces[other * plan.Y + dy][dx, dz, plan.block :, :].astype(F32)
                    if plan.swap and dy != dx:
                        turned = pieces[other * plan.Y + dx][dy, dz, plan.block :, :].astype(F32)
                        sent = jnp.where(c == other, sent, turned)
                    value = (sent[:parts] + sent[parts : 2 * parts]) + sent[2 * parts : 3 * parts]
                    for i in range(parts):
                        known_ref[row : row + 1, i * depth : (i + 1) * depth] = value[i : i + 1]
                    known_ref[row : row + 1, lanes : lanes + depth] = sent[3 * parts : 3 * parts + 1]
    asked = known_ref[:, lanes:].astype(jnp.int32)
    owner = (asked // segs) ^ me
    slot = ((owner % plan.C) * plan.Y + owner // plan.C) * segs + asked % segs
    code = lax.broadcasted_iota(jnp.int32, (plan.mp, owners * segs), 1)
    times = jnp.zeros((plan.mp, owners * segs), F32)
    for b in range(owners):
        for i in range(samples):
            wanted = slot[b * plan.mp : (b + 1) * plan.mp, i : i + 1]
            times = times + jnp.where(code == wanted, 1.0, 0.0)
    times = times.astype(BF16)
    row = lax.broadcasted_iota(jnp.int32, (owners * segs, lanes), 0)
    lane = lax.broadcasted_iota(jnp.int32, (owners * segs, lanes), 1)
    spread_times = []
    for o in range(owners):
        pick = (row == o * segs + lane // steps).astype(F32).astype(BF16)
        spread_times.append(jnp.dot(times, pick, preferred_element_type=F32))
    times = jnp.concatenate(spread_times, axis=0)
    advantage = known_ref[:, :lanes]
    centered = advantage - jnp.sum(times * advantage) / total
    spread = jnp.sum(times * centered * centered) / total
    normalized = centered * lax.rsqrt(spread + 1e-05)
    weights = times * jnp.exp(jnp.minimum(normalized, 3.0))
    weight_ref[...] = weights[0:1, :]
    mass_ref[0, 0] = jnp.sum(weights)
    for o in range(owners):
        norm_ref[o : o + 1, :] = normalized[o * plan.mp : o * plan.mp + 1, :]


def step_weights(plan, here, pieces, segs, samples, lanes, total):
    owners = plan.C * plan.Y
    depth = pieces[0].shape[-1]
    return pl.pallas_call(
        functools.partial(weight_kernel, plan, segs, samples, total),
        in_specs=[SMEM] + [VMEM] * len(pieces),
        out_specs=[VMEM, SMEM, VMEM],
        out_shape=[
            jax.ShapeDtypeStruct((1, lanes), F32),
            jax.ShapeDtypeStruct((1, 1), F32),
            jax.ShapeDtypeStruct((owners, lanes), F32),
        ],
        scratch_shapes=[pltpu.VMEM((owners * plan.mp, lanes + depth), F32)],
        compiler_params=ROOM,
        name="weights",
    )(here, *pieces)


def gradient_chunk(plan, here, sig_ref, n_ref, keep_ref, send_ref):
    y, c, z, x = here
    rows = plan.Y * plan.block
    depth = keep_ref.shape[-1]
    span = plan.X * depth

    def step(plane, carry):
        part = jnp.dot(
            sig_ref[: 2 * rows, :],
            n_ref[:, pl.ds(pl.multiple_of(plane * span, span), span)],
            preferred_element_type=F32,
        )
        keep = jnp.where(c == 0, part[:rows], part[rows:])
        send = jnp.where(c == 0, part[rows:], part[:rows]).astype(BF16)
        dz = plane ^ z
        for line in range(plan.X):
            for col in range(plan.Y):
                where = (slice(col * plan.block, (col + 1) * plan.block), slice(line * depth, (line + 1) * depth))
                p, q = plan.relative(c, y ^ col, x ^ line)
                keep_ref[p, q, dz] = keep[where]
                p, q = plan.relative(1 - c, y ^ col, x ^ line)
                send_ref[p, q, dz] = send[where]
        return carry

    lax.fori_loop(0, plan.Z, step, 0)


def fetch_policy(plan, here, j, pieces, wt_ref, sems):
    y, c, z, x = here
    block = plan.block
    depth = pieces[0].shape[-1]
    copies = []
    for other in range(2):
        core = c ^ other
        for p in range(plan.Y):
            piece = pieces[other * plan.Y + p]
            for q in range(plan.X):
                a, b = plan.relative(core, p, q)
                for dz in range(plan.Z):
                    row = (core * plan.Y + (y ^ a)) * block
                    col = ((z ^ dz) * plan.X + (x ^ b)) * depth
                    copy = pltpu.make_async_copy(
                        piece.at[q, dz, 0:block],
                        wt_ref.at[
                            pl.ds(pl.multiple_of(row, block), block),
                            pl.ds(pl.multiple_of(col, depth), depth),
                        ],
                        sems.at[len(copies)],
                    )
                    copy.start()
                    copies.append(copy)
    return copies


TILE = 256


def chunk_logits(wt_ref, n_ref, l_ref, first_row, top_ref):
    rows = wt_ref.shape[0]

    def step(t, carry):
        part = lax.dot_general(
            wt_ref[...],
            n_ref[pl.ds(pl.multiple_of(t * TILE, TILE), TILE), :],
            (((1,), (1,)), ((), ())),
            preferred_element_type=F32,
        )
        l_ref[t, first_row : first_row + rows, :] = part
        top_ref[t] = jnp.max(part, axis=0, keepdims=True)
        return carry

    lax.fori_loop(0, l_ref.shape[0], step, 0)


def logits_kernel(plan, here_ref, *refs):
    pieces, refs = refs[: 2 * plan.Y], refs[2 * plan.Y :]
    n_ref, l_ref, top_ref, wt_ref, w_sems = refs
    here = tuple(here_ref[i] for i in range(4))
    for copy in fetch_policy(plan, here, 0, pieces, wt_ref, w_sems):
        copy.wait()
    chunk_logits(wt_ref, n_ref, l_ref, 0, top_ref)


def signals(known, l_ref, sig_refs, w_ref, act_ref, top_ref):
    group = 64
    tiles, actions, _ = l_ref.shape
    rows = sig_refs[0].shape[0]

    def step(t, carry):
        top = top_ref[t]
        for j in range(len(known) // 2):
            top = jnp.maximum(top, known[2 * j + 1][t])
        where = pl.ds(pl.multiple_of(t * TILE, TILE), TILE)
        mass = jnp.zeros((8, TILE), F32)
        for a in range(0, actions, group):
            j, first = a // rows, a % rows
            source = known[2 * j][t, first : first + group, :] if 2 * j < len(known) else l_ref[t, a : a + group, :]
            part = jnp.exp(source - top)
            l_ref[t, a : a + group, :] = part
            mass = mass + jnp.sum(part.reshape(group // 8, 8, TILE), axis=0)
        mass = jnp.sum(mass, axis=0, keepdims=True)
        weight = w_ref[:, where]
        chosen = act_ref[:, where]
        scale = weight / mass
        for a in range(0, actions, group):
            row = lax.broadcasted_iota(jnp.int32, (group, TILE), 0) + a
            part = l_ref[t, a : a + group, :] * scale
            part = part - jnp.where(row == chosen, weight, 0.0)
            sig_refs[a // rows][a % rows : a % rows + group, where] = part.astype(BF16)
        return carry

    lax.fori_loop(0, tiles, step, 0)


def signal_kernel(plan, here_ref, w_ref, act_ref, *refs):
    pieces, refs = refs[: 2 * plan.Y], refs[2 * plan.Y :]
    n_ref, refs = refs[0], refs[1:]
    early = plan.J - 1
    known, refs = refs[: 2 * early], refs[2 * early :]
    rest, refs = refs[:early], refs[early:]
    keep_ref, send_ref, wt_ref, l_ref, top_ref, sig_ref, w_sems = refs
    here = tuple(here_ref[i] for i in range(4))
    for copy in fetch_policy(plan, here, early, pieces, wt_ref, w_sems):
        copy.wait()
    chunk_logits(wt_ref, n_ref, l_ref, early * wt_ref.shape[0], top_ref)
    signals(known, l_ref, (sig_ref,) + tuple(rest), w_ref, act_ref, top_ref)
    gradient_chunk(plan, here, sig_ref, n_ref, keep_ref, send_ref)


def gradient_kernel(plan, here_ref, sig_ref, n_ref, keep_ref, send_ref):
    here = tuple(here_ref[i] for i in range(4))
    gradient_chunk(plan, here, sig_ref, n_ref, keep_ref, send_ref)


def chunk_shapes(plan, depth):
    shape = (plan.Y, plan.X, plan.Z, plan.block, depth)
    return [jax.ShapeDtypeStruct(shape, F32), jax.ShapeDtypeStruct(shape, BF16)]


def early_logits(plan, here, pieces, normed, count):
    tokens, width = normed.shape
    rows = count // plan.J
    return pl.pallas_call(
        functools.partial(logits_kernel, plan),
        in_specs=[SMEM] + [VMEM] * (len(pieces) + 1),
        out_specs=[VMEM, VMEM],
        out_shape=[
            jax.ShapeDtypeStruct((tokens // TILE, rows, TILE), F32),
            jax.ShapeDtypeStruct((tokens // TILE, 1, TILE), F32),
        ],
        scratch_shapes=[
            pltpu.VMEM((rows, width), BF16),
            pltpu.SemaphoreType.DMA((len(pieces) * plan.X * plan.Z,)),
        ],
        compiler_params=ROOM,
        cost_estimate=pl.CostEstimate(
            flops=2 * tokens * width * rows,
            bytes_accessed=2 * tokens * width + 2 * width * rows + 4 * tokens * rows,
            transcendentals=0,
        ),
        name="logits",
    )(here, *pieces, normed)


def signal_and_gradient(plan, here, weights, actions, pieces, normed, count):
    tokens, width = normed.shape
    depth = width // plan.mp
    rows = count // plan.J
    known = []
    for piece in pieces[:-1]:
        known += early_logits(plan, here, piece, normed, count)
    last = pieces[-1]
    signal = jax.ShapeDtypeStruct((rows, tokens), BF16)
    *rest, keep, send = pl.pallas_call(
        functools.partial(signal_kernel, plan),
        in_specs=[SMEM, VMEM, VMEM] + [VMEM] * (len(last) + 1 + len(known)),
        out_specs=[VMEM] * (plan.J + 1),
        out_shape=[signal] * (plan.J - 1) + chunk_shapes(plan, depth),
        scratch_shapes=[
            pltpu.VMEM((rows, width), BF16),
            pltpu.VMEM((tokens // TILE, count, TILE), F32),
            pltpu.VMEM((tokens // TILE, 1, TILE), F32),
            pltpu.VMEM((rows, tokens), BF16),
            pltpu.SemaphoreType.DMA((len(last) * plan.X * plan.Z,)),
        ],
        compiler_params=ROOM,
        cost_estimate=pl.CostEstimate(
            flops=4 * tokens * width * rows,
            bytes_accessed=2 * tokens * width + 2 * width * count + 6 * tokens * count,
            transcendentals=tokens * count,
        ),
        name="signal",
    )(here, weights, actions, *last, normed, *known)
    chunks = [(keep, send)]
    for later in rest:
        chunks.append(
            pl.pallas_call(
                functools.partial(gradient_kernel, plan),
                in_specs=[SMEM, VMEM, VMEM],
                out_specs=[VMEM] * 2,
                out_shape=chunk_shapes(plan, depth),
                compiler_params=ROOM,
                cost_estimate=pl.CostEstimate(
                    flops=2 * tokens * width * rows,
                    bytes_accessed=2 * tokens * width + 2 * tokens * count,
                    transcendentals=0,
                ),
                name="gradient",
            )(here, later, normed)
        )
    return chunks


def assemble_kernel(plan, j, here_ref, *refs):
    count = 2 * plan.Y
    pieces, refs = refs[:count], refs[count:]
    near, far = refs[:2]
    actor_ref, update_ref, sems = refs[-3:]
    y, c, z, x = (here_ref[i] for i in range(4))
    depth = near.shape[-2]
    block = plan.block
    copies = []

    def copy(source, target):
        moved = pltpu.make_async_copy(source, target, sems.at[len(copies)])
        moved.start()
        copies.append(moved)

    for other in range(2):
        core = c ^ other
        for dy in range(plan.Y):
            col = ((j * 2 + core) * plan.Y + (y ^ dy)) * block
            copy(
                (far if other else near).at[dy],
                update_ref.at[:, pl.ds(pl.multiple_of(col, block), block)],
            )
        for p in range(plan.Y):
            piece = pieces[other * plan.Y + p]
            for q in range(plan.X):
                a, b = plan.relative(core, p, q)
                for dz in range(plan.Z):
                    col = ((j * 2 + core) * plan.Y + (y ^ a)) * block
                    row = ((z ^ dz) * plan.X + (x ^ b)) * depth
                    copy(
                        piece.at[q, dz],
                        actor_ref.at[
                            pl.ds(pl.multiple_of(row, depth), depth),
                            pl.ds(pl.multiple_of(col, block), block),
                        ],
                    )
    for moved in copies:
        moved.wait()


def assemble(plan, j, here, pieces, near, far, before, width, count):
    depth = width // plan.mp
    taken = len(pieces) + 3
    return pl.pallas_call(
        functools.partial(assemble_kernel, plan, j),
        in_specs=[SMEM] + [VMEM] * (len(pieces) + 2) + [ANY] * len(before),
        out_specs=[ANY] * 2,
        out_shape=[
            jax.ShapeDtypeStruct((width, count), BF16),
            jax.ShapeDtypeStruct((depth, count), F32),
        ],
        scratch_shapes=[
            pltpu.SemaphoreType.DMA((len(pieces) * plan.X * plan.Z + 2 * plan.Y,)),
        ],
        input_output_aliases={taken + i: i for i in range(len(before))},
        compiler_params=pltpu.CompilerParams(vmem_limit_bytes=32 * 2**20),
        name="assemble",
    )(here, *pieces, near, far, *before)


def body(
    features,
    rewards,
    tail_value,
    actions,
    episode_ends,
    sample_owner,
    sample_row,
    norm_gain,
    value_weight,
    policy_weight,
    first_moment,
    second_moment,
):
    owners_all, columns = lax.axis_size("replay"), lax.axis_size("mp")
    segs, seg_len, width = features.shape
    depth, count = policy_weight.shape
    samples = sample_row.shape[0]
    plan = Plan(owners_all, columns, count)
    here = plan.here()
    place = (here[1] * plan.Y + here[0]).reshape(1)
    replay = lax.axis_index("replay")

    low = own_shard(plan, place, policy_weight)
    stages = [plan.gather_column(block) for block in low[:-1]]
    if stages:
        norm_gain = lax.optimization_barrier((norm_gain, stages[0][1]))[0]

    asked = sample_owner[:, 0] * segs + sample_row
    normed, block = normalize(
        features.reshape(segs * seg_len, width),
        norm_gain,
        value_weight,
        rewards,
        episode_ends,
        tail_value,
        asked,
        low[-1],
    )
    stages.append(plan.gather_column(block))
    pieces = [plan.gather_rest(column) for column in stages]
    token_total = owners_all * columns * samples * seg_len
    weights, total_weight, column = step_weights(plan, here, pieces[-1], segs, samples, segs * seg_len, token_total)
    owner = (asked // segs) ^ replay
    slot = ((owner % plan.C) * plan.Y + owner // plan.C) * segs + asked % segs
    local_norm = column.reshape(owners_all * segs, seg_len)[slot].reshape(-1)

    chunks = signal_and_gradient(plan, here, weights, actions.reshape(1, -1), pieces, normed, count)
    outs, terms = (), None
    for j, (keep, send) in enumerate(chunks):
        base, low = plan.reduce(keep, send)
        if terms is not None:
            low, terms = lax.optimization_barrier((low, terms))
        terms = plan.reduce_column(low)
        update, low = own_update(
            plan, j, place, total_weight, base, terms, policy_weight, first_moment, second_moment
        )
        near = jnp.stack([update] + [plan.permute(update, "y", k) for k in range(1, plan.Y)])
        column, near = lax.optimization_barrier((plan.gather_column(low), near))
        far = plan.permute(near, "c", 1)
        outs = assemble(plan, j, here, plan.gather_rest(column), near, far, outs, width, count)
    actor_policy, update = outs
    return (local_norm, update, actor_policy)


def solution(mesh):
    return jax.shard_map(
        body,
        mesh=mesh,
        in_specs=(
            P(ALL, None, None),
            P(ALL, None),
            P(ALL),
            P(ALL, None),
            P(ALL, None),
            P(ALL, None),
            P(ALL),
            P(),
            P(),
            P("mp", None),
            P("mp", None),
            P("mp", None),
        ),
        out_specs=(P(ALL), P("mp", None), P()),
        check_vma=False,
    )
```

time: 176 us -> 158 us (0.90)
  starting transfers between devices: 56.6 us -> 50.5 us
  local copies, waits for them, and re-layouts: 20.9 us -> 16 us
  other arithmetic: 7.4 us -> 3.86 us
  Pallas kernels: 38 us -> 35.1 us
    pallas_call x1, Pallas kernels: 16.1 us -> 8.56 us  [signal_and_gradient(): pl.pallas_call(functools.partial(signal_kernel, plan), in_specs=[SMEM, VM...]
    ppermute x48 -> x44, starting transfers between devices: 56.6 us -> 50.5 us  [permute(): return lax.ppermute(value, ALL, pairs)]
    pallas_call x4 -> x6, Pallas kernels: 13.8 us -> 17.9 us  [the longest x2 5.47 us: assemble(): pl.pallas_call(functools.partial(assemble_kernel, plan, j), in_specs=[SME...]
    reduce_sum x4 -> x0, other arithmetic: 2.18 us -> none  [the longest x1 0.68 us: body(): spread = jnp.sum(times * centered * centered) / token_total]
    ppermute x48 -> x44, waiting for transfers between devices: 50.3 us -> 51 us  [permute(): return lax.ppermute(value, ALL, pairs)]
  transfers between devices with their start and end apart: 48 -> 44, of which waited for: 19 -> 15; matrix products, arithmetic and copies ran while one was open for 9% -> 5% of each run, Pallas kernels for 6% -> 13%
where the time goes in v2:
time: 158 us; the launch traced here: 157 us
  waiting for transfers between devices  51 us (32%)
  starting transfers between devices  50.5 us (32%)
  Pallas kernels  35.1 us (22%)
  local copies, waits for them, and re-layouts  16 us (10%)
  other arithmetic  3.86 us (2%)
    ppermute x44, waiting for transfers between devices, permute(): return lax.ppermute(value, ALL, pairs)  51 us
    ppermute x44, starting transfers between devices, permute(): return lax.ppermute(value, ALL, pairs)  50.5 us
    unnamed x40, local copies, waits for them, and re-layouts  11.6 us
    pallas_call x1, Pallas kernels, signal_and_gradient(): pl.pallas_call(functools.partial(signal_kernel, plan), in_specs=[SMEM, VM...  8.56 us
    pallas_call x2, Pallas kernels, assemble(): pl.pallas_call(functools.partial(assemble_kernel, plan, j), in_specs=[SME...  5.47 us
    pallas_call x2, Pallas kernels, own_update(): pl.pallas_call(functools.partial(update_kernel, len(terms)), grid_spec=pl...  5.39 us
    pallas_call x1, Pallas kernels, early_logits(): pl.pallas_call(functools.partial(logits_kernel, plan), in_specs=[SMEM] +...  5.04 us
    pallas_call x1, Pallas kernels, signal_and_gradient(): pl.pallas_call(functools.partial(gradient_kernel, plan), in_specs=[SMEM,...  3.51 us
  transfers between devices with their start and end apart: 44, of which 15 were waited for; matrix products, arithmetic and copies ran while one was open for 5% of the time, Pallas kernels for 13%

profile of v2, /device:TPU:0, one launch (start us, length us, event | category | flops | bytes accessed | tf_op | source)
XLA Modules:
  0.0 157.4 jit_solution(6797700488207154187)
XLA Ops:
  0.7 1.8 %shard.1 = (bf16[128,256]{1,0:T(8,128)(2,1)}, bf16[128,256]{1,0:T(8,128)(2,1)}) custom-call(s32[1]{0:T(128)} %bitcast.5.place_ref, f32[256,1024]{1,0:T(8,128)} %refs_3_.3), custom_call_target="tpu_custom_call" | custom-call | tf_op jit(solution)/shard_map/shard/pallas_call | solution.py:98
  2.4 5.1 %collective-permute-start.9 = (bf16[128,256]{1,0:T(8,128)(2,1)}, bf16[128,256]{1,0:T(8,128)(2,1)S(1)}, u32[]{:S(2)}, u32[]{:S(2)}) collective-permute-start(bf16[128,256]{1,0:T(8,128)(2,1)} %get-tuple-element.39), channel_id=1, source_target_pairs={{0,6},{1,7},{2,4},{3,5},{4,2},{5,3},{6,0},{7,1},{8,14},{9,15},{10,... | collective-permute-start | bytes 196616 | tf_op jit(solution)/shard_map/ppermute | solution.py:45
  9.6 2.4 %collective-permute-done = bf16[128,256]{1,0:T(8,128)(2,1)S(1)} collective-permute-done((bf16[128,256]{1,0:T(8,128)(2,1)}, bf16[128,256]{1,0:T(8,128)(2,1)S(1)}, u32[]{:S(2)}, u32[]{:S(2)}) %collective-permute-start) | collective-permute-done | bytes 65568 | tf_op jit(solution)/shard_map/ppermute | solution.py:45
  12.8 2.2 %copy-done = bf16[32,32,2048]{2,1,0:T(8,128)(2,1)S(1)} copy-done((bf16[32,32,2048]{2,1,0:T(8,128)(2,1)S(1)}, bf16[32,32,2048]{2,1,0:T(8,128)(2,1)}, u32[]{:S(2)}) %copy-start) | copy-done | bytes 4194328
  17.9 3.3 %normalize.1 = (bf16[1024,2048]{1,0:T(8,128)(2,1)S(1)}, bf16[144,256]{1,0:T(8,128)(2,1)S(1)}) custom-call(bf16[1024,2048]{1,0:T(8,128)(2,1)S(1)} %bitcast.90, f32[1,2048]{1,0:T(1,128)S(1)} %bitcast.92, bf16[16,2048]{1,0:T(8,128)(2,1)S(1)} %broadcast_in_dim.12.value_ref, bf16[32,32]{1,0:T(8,128)(2,1)S(1)} %copy-done.6, s32[32,32]{1,0:T(8,128)S(1)} %copy-done.4, ...), custom_call_target="tpu_custom_call" | custom-call | flops 20971520 | bytes 8388608 | tf_op jit(solution)/shard_map/normalize/pallas_call | solution.py:208
  21.2 2.0 %copy-done.7 = bf16[1024,2048]{1,0:T(8,128)(2,1)} copy-done((bf16[1024,2048]{1,0:T(8,128)(2,1)}, bf16[1024,2048]{1,0:T(8,128)(2,1)S(1)}, u32[]{:S(2)}) %copy-start.7) | copy-done | bytes 4194328
  23.2 3.2 %collective-permute-start.3 = (bf16[144,256]{1,0:T(8,128)(2,1)S(1)}, bf16[144,256]{1,0:T(8,128)(2,1)S(1)}, u32[]{:S(2)}, u32[]{:S(2)}) collective-permute-start(bf16[144,256]{1,0:T(8,128)(2,1)S(1)} %get-tuple-element.42), channel_id=1, source_target_pairs={{0,6},{1,7},{2,4},{3,5},{4,2},{5,3},{6,0},{7,1},{8,14},{9,15},{10,... | collective-permute-start | bytes 221192 | tf_op jit(solution)/shard_map/ppermute | solution.py:45
  27.6 1.6 %collective-permute-start.10 = (bf16[4,128,256]{2,1,0:T(8,128)(2,1)S(1)}, bf16[4,128,256]{2,1,0:T(8,128)(2,1)S(1)}, u32[]{:S(2)}, u32[]{:S(2)}) collective-permute-start(bf16[4,128,256]{2,1,0:T(8,128)(2,1)S(1)} %get-tuple-element.92), channel_id=1, source_target_pairs={{0,1},{1,0},{2,3},{3,2},{4,5},{5,4},{6,7},{7,6},{8,24},{9,25},{10,... | collective-permute-start | bytes 786440 | tf_op jit(solution)/shard_map/ppermute | solution.py:45
  29.4 3.2 %collective-permute-done.2 = bf16[144,256]{1,0:T(8,128)(2,1)S(1)} collective-permute-done((bf16[144,256]{1,0:T(8,128)(2,1)S(1)}, bf16[144,256]{1,0:T(8,128)(2,1)S(1)}, u32[]{:S(2)}, u32[]{:S(2)}) %collective-permute-start.2) | collective-permute-done | bytes 73760 | tf_op jit(solution)/shard_map/ppermute | solution.py:45
  32.7 1.6 collective-permute-start.4
  34.3 1.6 %collective-permute-start.11 = (bf16[2,4,128,256]{3,2,1,0:T(8,128)(2,1)S(1)}, bf16[2,4,128,256]{3,2,1,0:T(8,128)(2,1)S(1)}, u32[]{:S(2)}, u32[]{:S(2)}) collective-permute-start(bf16[2,4,128,256]{3,2,1,0:T(8,128)(2,1)S(1)} %pad_maximum_fusion.1.refs_0_), channel_id=1, source_target_pairs={{0,16},{1,17},{2,18},{3,19},{4,20},{5,21},{6,22},{7,23},{8,9},{9,8... | collective-permute-start | bytes 1572872 | tf_op jit(solution)/shard_map/ppermute | solution.py:45
  35.9 6.7 %collective-permute-done.4 = bf16[4,144,256]{2,1,0:T(8,128)(2,1)S(1)} collective-permute-done((bf16[4,144,256]{2,1,0:T(8,128)(2,1)S(1)}, bf16[4,144,256]{2,1,0:T(8,128)(2,1)S(1)}, u32[]{:S(2)}, u32[]{:S(2)}) %collective-permute-start.4) | collective-permute-done | bytes 294944 | tf_op jit(solution)/shard_map/ppermute | solution.py:45
  42.7 1.6 %collective-permute-start.5 = (bf16[2,4,144,256]{3,2,1,0:T(8,128)(2,1)S(1)}, bf16[2,4,144,256]{3,2,1,0:T(8,128)(2,1)S(1)}, u32[]{:S(2)}, u32[]{:S(2)}) collective-permute-start(bf16[2,4,144,256]{3,2,1,0:T(8,128)(2,1)S(1)} %pad_maximum_fusion.refs_0_), channel_id=1, source_target_pairs={{0,16},{1,17},{2,18},{3,19},{4,20},{5,21},{6,22},{7,23},{8,9},{9,8... | collective-permute-start | bytes 1769480 | tf_op jit(solution)/shard_map/ppermute | solution.py:45
  44.8 7.8 %collective-permute-done.5.refs_1_ = bf16[2,4,144,256]{3,2,1,0:T(8,128)(2,1)S(1)} collective-permute-done((bf16[2,4,144,256]{3,2,1,0:T(8,128)(2,1)S(1)}, bf16[2,4,144,256]{3,2,1,0:T(8,128)(2,1)S(1)}, u32[]{:S(2)}, u32[]{:S(2)}) %collective-permute-start.5) | collective-permute-done | bytes 589856 | tf_op jit(solution)/shard_map/ppermute | solution.py:45
  52.8 2.2 %copy-done.8 = bf16[1024,2048]{1,0:T(8,128)(2,1)S(1)} copy-done((bf16[1024,2048]{1,0:T(8,128)(2,1)S(1)}, bf16[1024,2048]{1,0:T(8,128)(2,1)}, u32[]{:S(2)}) %copy-start.8) | copy-done | bytes 4194328
  55.0 5.0 %logits.1 = (f32[4,512,256]{2,1,0:T(8,128)S(1)}, f32[4,1,256]{2,1,0:T(1,128)S(1)}) custom-call(s32[4]{0:T(128)S(1)} %pad_add_fusion.here_ref, bf16[2,4,128,256]{3,2,1,0:T(8,128)(2,1)S(1)} %pad_maximum_fusion.1.refs_0_, bf16[2,4,128,256]{3,2,1,0:T(8,128)(2,1)S(1)} %collective-permute-done.11.refs_1_, ...), custom_call_target="tpu_custom_call" | custom-call | flops 2147483648 | bytes 8388608 | tf_op jit(solution)/shard_map/logits/pallas_call | solution.py:454
  60.1 2.1 %weights.1 = (f32[1,1024]{1,0:T(1,128)S(1)}, f32[1,1]{1,0:T(1,128)}, f32[4,1024]{1,0:T(4,128)S(1)}) custom-call(s32[4]{0:T(128)S(1)} %pad_add_fusion.here_ref, bf16[2,4,144,256]{3,2,1,0:T(8,128)(2,1)S(1)} %pad_maximum_fusion.refs_0_, bf16[2,4,144,256]{3,2,1,0:T(8,128)(2,1)S(1)} %collective-permute-done.5.refs_1_, ...), custom_call_target="tpu_custom_call" | custom-call | tf_op jit(solution)/shard_map/weights/pallas_call | solution.py:297
  62.2 8.6 %signal.1 = (bf16[512,1024]{1,0:T(8,128)(2,1)S(1)}, f32[2,2,4,128,256]{4,3,2,1,0:T(8,128)S(1)}, bf16[2,2,4,128,256]{4,3,2,1,0:T(8,128)(2,1)S(1)}) custom-call(s32[4]{0:T(128)S(1)} %pad_add_fusion.here_ref, f32[1,1024]{1,0:T(1,128)S(1)} %get-tuple-element.45.w_ref, s32[1,1024]{1,0:T(1,128)S(1)} %reshape.42.act_ref, ...), custom_call_target="tpu_custom_call" | custom-call | flops 4294967296 | bytes 14680064 | tf_op jit(solution)/shard_map/signal/pallas_call | solution.py:485
  71.3 3.5 %gradient.1 = (f32[2,2,4,128,256]{4,3,2,1,0:T(8,128)S(1)}, bf16[2,2,4,128,256]{4,3,2,1,0:T(8,128)(2,1)S(1)}) custom-call(s32[4]{0:T(128)S(1)} %pad_add_fusion.here_ref, bf16[512,1024]{1,0:T(8,128)(2,1)S(1)} %get-tuple-element.49.sig_ref, bf16[1024,2048]{1,0:T(8,128)(2,1)S(1)} %copy-done.9), custom_call_target="tpu_custom_call" | custom-call | flops 2147483648 | bytes 6291456 | tf_op jit(solution)/shard_map/gradient/pallas_call | solution.py:508
  75.3 1.6 %collective-permute-start.18 = (bf16[2,4,128,256]{3,2,1,0:T(8,128)(2,1)S(1)}, bf16[2,4,128,256]{3,2,1,0:T(8,128)(2,1)S(1)}, u32[]{:S(2)}, u32[]{:S(2)}) collective-permute-start(bf16[2,4,128,256]{3,2,1,0:T(8,128)(2,1)S(1)} %fusion.3), channel_id=1, source_target_pairs={{0,16},{1,17},{2,18},{3,19},{4,20},{5,21},{6,22},{7,23},{8,9},{9,8... | collective-permute-start | bytes 1572872 | tf_op jit(solution)/shard_map/ppermute | solution.py:45
  77.8 1.6 %collective-permute-start.15 = (bf16[2,4,128,256]{3,2,1,0:T(8,128)(2,1)S(1)}, bf16[2,4,128,256]{3,2,1,0:T(8,128)(2,1)S(1)}, u32[]{:S(2)}, u32[]{:S(2)}) collective-permute-start(bf16[2,4,128,256]{3,2,1,0:T(8,128)(2,1)S(1)} %fusion.2), channel_id=1, source_target_pairs={{0,16},{1,17},{2,18},{3,19},{4,20},{5,21},{6,22},{7,23},{8,9},{9,8... | collective-permute-start | bytes 1572872 | tf_op jit(solution)/shard_map/ppermute | solution.py:45
  79.5 5.0 %collective-permute-done.18 = bf16[2,4,128,256]{3,2,1,0:T(8,128)(2,1)S(1)} collective-permute-done((bf16[2,4,128,256]{3,2,1,0:T(8,128)(2,1)S(1)}, bf16[2,4,128,256]{3,2,1,0:T(8,128)(2,1)S(1)}, u32[]{:S(2)}, u32[]{:S(2)}) %collective-permute-start.18) | collective-permute-done | bytes 524320 | tf_op jit(solution)/shard_map/ppermute | solution.py:45
  84.7 1.6 collective-permute-start.19
  86.2 6.7 %collective-permute-done.15 = bf16[2,4,128,256]{3,2,1,0:T(8,128)(2,1)S(1)} collective-permute-done((bf16[2,4,128,256]{3,2,1,0:T(8,128)(2,1)S(1)}, bf16[2,4,128,256]{3,2,1,0:T(8,128)(2,1)S(1)}, u32[]{:S(2)}, u32[]{:S(2)}) %collective-permute-start.15) | collective-permute-done | bytes 524320 | tf_op jit(solution)/shard_map/ppermute | solution.py:45
  93.1 1.6 collective-permute-start.16
  94.8 2.2 %collective-permute-start.22 = (bf16[128,256]{1,0:T(8,128)(2,1)S(1)}, bf16[128,256]{1,0:T(8,128)(2,1)S(1)}, u32[]{:S(2)}, u32[]{:S(2)}) collective-permute-start(bf16[128,256]{1,0:T(8,128)(2,1)S(1)} %get-tuple-element.85), channel_id=1, source_target_pairs={{0,6},{1,7},{2,4},{3,5},{4,2},{5,3},{6,0},{7,1},{8,14},{9,15},{10,... | collective-permute-start | bytes 196616 | tf_op jit(solution)/shard_map/ppermute | solution.py:45
  97.0 2.3 %collective-permute-start.20 = (bf16[128,256]{1,0:T(8,128)(2,1)S(1)}, bf16[128,256]{1,0:T(8,128)(2,1)S(1)}, u32[]{:S(2)}, u32[]{:S(2)}) collective-permute-start(bf16[128,256]{1,0:T(8,128)(2,1)S(1)} %get-tuple-element.87), channel_id=1, source_target_pairs={{0,2},{1,3},{2,0},{3,1},{4,6},{5,7},{6,4},{7,5},{8,10},{9,11},{10,... | collective-permute-start | bytes 196616 | tf_op jit(solution)/shard_map/ppermute | solution.py:45
  100.9 1.4 collective-permute-done.21.refs_1_
  102.3 1.8 %collective-permute-start.23 = (bf16[128,256]{1,0:T(8,128)(2,1)S(1)}, bf16[128,256]{1,0:T(8,128)(2,1)S(1)}, u32[]{:S(2)}, u32[]{:S(2)}) collective-permute-start(bf16[128,256]{1,0:T(8,128)(2,1)S(1)} %get-tuple-element.54), channel_id=1, source_target_pairs={{0,2},{1,3},{2,0},{3,1},{4,6},{5,7},{6,4},{7,5},{8,10},{9,11},{10,... | collective-permute-start | bytes 196616 | tf_op jit(solution)/shard_map/ppermute | solution.py:45
  104.1 1.0 collective-permute-start.24
  105.1 1.7 %collective-permute-start.25 = (bf16[128,256]{1,0:T(8,128)(2,1)S(1)}, bf16[128,256]{1,0:T(8,128)(2,1)S(1)}, u32[]{:S(2)}, u32[]{:S(2)}) collective-permute-start(bf16[128,256]{1,0:T(8,128)(2,1)S(1)} %get-tuple-element.56), channel_id=1, source_target_pairs={{0,6},{1,7},{2,4},{3,5},{4,2},{5,3},{6,0},{7,1},{8,14},{9,15},{10,... | collective-permute-start | bytes 196616 | tf_op jit(solution)/shard_map/ppermute | solution.py:45
  106.8 2.7 %update.3 = (f32[256,128]{1,0:T(8,128)}, bf16[256,128]{1,0:T(8,128)(2,1)}) custom-call(s32[1]{0:T(128)} %bitcast.5.place_ref, f32[1,1]{1,0:T(1,128)} %get-tuple-element.44.mass_ref, f32[128,256]{1,0:T(8,128)} %slice_bitcast_fusion.4.base_ref, bf16[128,256]{1,0:T(8,128)(2,1)} %copy-done.17, bf16[128,256]{1,0:T(8,128)(2,1)} %copy-done.15, ...), custom_call_target="tpu_custom_call" | custom-call | tf_op jit(solution)/shard_map/update/pallas_call | solution.py:127
  109.5 1.6 collective-permute-start.38
  111.7 2.2 %collective-permute-start.37 = (bf16[256,128]{1,0:T(8,128)(2,1)}, bf16[256,128]{1,0:T(8,128)(2,1)S(1)}, u32[]{:S(2)}, u32[]{:S(2)}) collective-permute-start(bf16[256,128]{1,0:T(8,128)(2,1)} %get-tuple-element.66), channel_id=1, source_target_pairs={{0,6},{1,7},{2,4},{3,5},{4,2},{5,3},{6,0},{7,1},{8,14},{9,15},{10,... | collective-permute-start | bytes 196616 | tf_op jit(solution)/shard_map/ppermute | solution.py:45
  114.0 2.1 %collective-permute-start.35 = (bf16[256,128]{1,0:T(8,128)(2,1)}, bf16[256,128]{1,0:T(8,128)(2,1)S(1)}, u32[]{:S(2)}, u32[]{:S(2)}) collective-permute-start(bf16[256,128]{1,0:T(8,128)(2,1)} %get-tuple-element.66), channel_id=1, source_target_pairs={{0,2},{1,3},{2,0},{3,1},{4,6},{5,7},{6,4},{7,5},{8,10},{9,11},{10,... | collective-permute-start | bytes 196616 | tf_op jit(solution)/shard_map/ppermute | solution.py:45
  116.7 2.7 %update.2 = (f32[256,128]{1,0:T(8,128)}, bf16[256,128]{1,0:T(8,128)(2,1)}) custom-call(s32[1]{0:T(128)} %bitcast.5.place_ref, f32[1,1]{1,0:T(1,128)} %get-tuple-element.44.mass_ref, f32[128,256]{1,0:T(8,128)} %slice_bitcast_fusion.5.base_ref, bf16[128,256]{1,0:T(8,128)(2,1)} %copy-done.14, bf16[128,256]{1,0:T(8,128)(2,1)} %copy-done.16, ...), custom_call_target="tpu_custom_call" | custom-call | tf_op jit(solution)/shard_map/update/pallas_call | solution.py:127
  119.4 2.2 %collective-permute-start.28 = (bf16[256,128]{1,0:T(8,128)(2,1)}, bf16[256,128]{1,0:T(8,128)(2,1)S(1)}, u32[]{:S(2)}, u32[]{:S(2)}) collective-permute-start(bf16[256,128]{1,0:T(8,128)(2,1)} %get-tuple-element.59), channel_id=1, source_target_pairs={{0,6},{1,7},{2,4},{3,5},{4,2},{5,3},{6,0},{7,1},{8,14},{9,15},{10,... | collective-permute-start | bytes 196616 | tf_op jit(solution)/shard_map/ppermute | solution.py:45
  122.1 2.2 %collective-permute-start.26 = (bf16[256,128]{1,0:T(8,128)(2,1)}, bf16[256,128]{1,0:T(8,128)(2,1)S(1)}, u32[]{:S(2)}, u32[]{:S(2)}) collective-permute-start(bf16[256,128]{1,0:T(8,128)(2,1)} %get-tuple-element.59), channel_id=1, source_target_pairs={{0,2},{1,3},{2,0},{3,1},{4,6},{5,7},{6,4},{7,5},{8,10},{9,11},{10,... | collective-permute-start | bytes 196616 | tf_op jit(solution)/shard_map/ppermute | solution.py:45
  124.4 1.1 collective-permute-start.39
  125.6 2.4 %collective-permute-done.29 = f32[256,128]{1,0:T(8,128)S(1)} collective-permute-done((f32[256,128]{1,0:T(8,128)}, f32[256,128]{1,0:T(8,128)S(1)}, u32[]{:S(2)}, u32[]{:S(2)}) %collective-permute-start.29) | collective-permute-done | bytes 131104 | tf_op jit(solution)/shard_map/ppermute | solution.py:45
  130.6 1.9 %collective-permute-done.39 = bf16[4,256,128]{2,1,0:T(8,128)(2,1)S(1)} collective-permute-done((bf16[4,256,128]{2,1,0:T(8,128)(2,1)S(1)}, bf16[4,256,128]{2,1,0:T(8,128)(2,1)S(1)}, u32[]{:S(2)}, u32[]{:S(2)}) %collective-permute-start.39) | collective-permute-done | bytes 262176 | tf_op jit(solution)/shard_map/ppermute | solution.py:45
  132.5 2.1 %collective-permute-start.40 = (bf16[2,4,256,128]{3,2,1,0:T(8,128)(2,1)S(1)}, bf16[2,4,256,128]{3,2,1,0:T(8,128)(2,1)}, u32[]{:S(2)}, u32[]{:S(2)}) collective-permute-start(bf16[2,4,256,128]{3,2,1,0:T(8,128)(2,1)S(1)} %pad_maximum_fusion.3.refs_0_), channel_id=1, source_target_pairs={{0,16},{1,17},{2,18},{3,19},{4,20},{5,21},{6,22},{7,23},{8,9},{9,8... | collective-permute-start | bytes 1572872 | tf_op jit(solution)/shard_map/ppermute | solution.py:45
  134.7 4.4 %collective-permute-done.30 = bf16[4,256,128]{2,1,0:T(8,128)(2,1)S(1)} collective-permute-done((bf16[4,256,128]{2,1,0:T(8,128)(2,1)S(1)}, bf16[4,256,128]{2,1,0:T(8,128)(2,1)S(1)}, u32[]{:S(2)}, u32[]{:S(2)}) %collective-permute-start.30) | collective-permute-done | bytes 262176 | tf_op jit(solution)/shard_map/ppermute | solution.py:45
  139.1 1.1 collective-permute-start.31
  140.8 1.1 collective-permute-done.40.refs_1_
  142.4 6.0 %collective-permute-done.31.refs_1_ = bf16[2,4,256,128]{3,2,1,0:T(8,128)(2,1)S(1)} collective-permute-done((bf16[2,4,256,128]{3,2,1,0:T(8,128)(2,1)S(1)}, bf16[2,4,256,128]{3,2,1,0:T(8,128)(2,1)S(1)}, u32[]{:S(2)}, u32[]{:S(2)}) %collective-permute-start.31) | collective-permute-done | bytes 524320 | tf_op jit(solution)/shard_map/ppermute | solution.py:45
  151.9 3.1 %assemble.2 = (bf16[2048,1024]{1,0:T(8,128)(2,1)}, f32[256,1024]{1,0:T(8,128)}) custom-call(s32[4]{0:T(128)S(1)} %pad_add_fusion.here_ref, bf16[2,4,256,128]{3,2,1,0:T(8,128)(2,1)S(1)} %pad_maximum_fusion.3.refs_0_, bf16[2,4,256,128]{3,2,1,0:T(8,128)(2,1)} %collective-permute-done.40.refs_1_, bf16[2,4,256,128]{3,2,1,0:T(8,128)(2,1)} %collective-permute-done.41.refs_2_, ...), custom_call_target="tpu_custom_call" | custom-call | tf_op jit(solution)/shard_map/assemble/pallas_call | solution.py:569
  155.1 2.3 %assemble.3 = (bf16[2048,1024]{1,0:T(8,128)(2,1)}, f32[256,1024]{1,0:T(8,128)}) custom-call(s32[4]{0:T(128)S(1)} %pad_add_fusion.here_ref, bf16[2,4,256,128]{3,2,1,0:T(8,128)(2,1)S(1)} %pad_maximum_fusion.2.refs_0_, bf16[2,4,256,128]{3,2,1,0:T(8,128)(2,1)S(1)} %collective-permute-done.31.refs_1_, ...), custom_call_target="tpu_custom_call", output_to_operand_aliasing={{0}: (7, {}), {1}: (8, {})} | custom-call | tf_op jit(solution)/shard_map/assemble/pallas_call | solution.py:569
  (124 shorter events, 21.3 us)
Async XLA Ops:
  2.4 25.2 %collective-permute-start.9 = (bf16[128,256]{1,0:T(8,128)(2,1)}, bf16[128,256]{1,0:T(8,128)(2,1)S(1)}, u32[]{:S(2)}, u32[]{:S(2)}) collective-permute-start(bf16[128,256]{1,0:T(8,128)(2,1)} %get-tuple-element.39), channel_id=1, source_target_pairs={{0,6},{1,7},{2,4},{3,5},{4,2},{5,3},{6,0},{7,1},{8,14},{9,15},{10,... | collective-permute-start | bytes 196616 | tf_op jit(solution)/shard_map/ppermute | solution.py:45
  7.5 20.0 %collective-permute-start.8 = (bf16[128,256]{1,0:T(8,128)(2,1)}, bf16[128,256]{1,0:T(8,128)(2,1)S(1)}, u32[]{:S(2)}, u32[]{:S(2)}) collective-permute-start(bf16[128,256]{1,0:T(8,128)(2,1)} %get-tuple-element.39), channel_id=1, source_target_pairs={{0,4},{1,5},{2,6},{3,7},{4,0},{5,1},{6,2},{7,3},{8,12},{9,13},{10,... | collective-permute-start | bytes 196616 | tf_op jit(solution)/shard_map/ppermute | solution.py:45
  7.5 4.5 %collective-permute-start = (bf16[128,256]{1,0:T(8,128)(2,1)}, bf16[128,256]{1,0:T(8,128)(2,1)S(1)}, u32[]{:S(2)}, u32[]{:S(2)}) collective-permute-start(bf16[128,256]{1,0:T(8,128)(2,1)} %get-tuple-element.39), channel_id=1, source_target_pairs={{0,2},{1,3},{2,0},{3,1},{4,6},{5,7},{6,4},{7,5},{8,10},{9,11},{10,... | collective-permute-start | bytes 196616 | tf_op jit(solution)/shard_map/ppermute | solution.py:45
  17.9 9.7 %copy-start.13 = (bf16[128,256]{1,0:T(8,128)(2,1)S(1)}, bf16[128,256]{1,0:T(8,128)(2,1)}, u32[]{:S(2)}) copy-start(bf16[128,256]{1,0:T(8,128)(2,1)} %get-tuple-element.39) | copy-start | bytes 196612
  23.2 29.5 %copy-start.19 = (s32[32,32]{1,0:T(8,128)S(1)}, s32[32,32]{1,0:T(8,128)}, u32[]{:S(2)}) copy-start(s32[32,32]{1,0:T(8,128)} %param.15) | copy-start | bytes 12292
  23.2 6.2 %collective-permute-start.3 = (bf16[144,256]{1,0:T(8,128)(2,1)S(1)}, bf16[144,256]{1,0:T(8,128)(2,1)S(1)}, u32[]{:S(2)}, u32[]{:S(2)}) collective-permute-start(bf16[144,256]{1,0:T(8,128)(2,1)S(1)} %get-tuple-element.42), channel_id=1, source_target_pairs={{0,6},{1,7},{2,4},{3,5},{4,2},{5,3},{6,0},{7,1},{8,14},{9,15},{10,... | collective-permute-start | bytes 221192 | tf_op jit(solution)/shard_map/ppermute | solution.py:45
  26.4 6.2 %collective-permute-start.2 = (bf16[144,256]{1,0:T(8,128)(2,1)S(1)}, bf16[144,256]{1,0:T(8,128)(2,1)S(1)}, u32[]{:S(2)}, u32[]{:S(2)}) collective-permute-start(bf16[144,256]{1,0:T(8,128)(2,1)S(1)} %get-tuple-element.42), channel_id=1, source_target_pairs={{0,4},{1,5},{2,6},{3,7},{4,0},{5,1},{6,2},{7,3},{8,12},{9,13},{10,... | collective-permute-start | bytes 221192 | tf_op jit(solution)/shard_map/ppermute | solution.py:45
  27.0 5.6 %collective-permute-start.1 = (bf16[144,256]{1,0:T(8,128)(2,1)S(1)}, bf16[144,256]{1,0:T(8,128)(2,1)S(1)}, u32[]{:S(2)}, u32[]{:S(2)}) collective-permute-start(bf16[144,256]{1,0:T(8,128)(2,1)S(1)} %get-tuple-element.42), channel_id=1, source_target_pairs={{0,2},{1,3},{2,0},{3,1},{4,6},{5,7},{6,4},{7,5},{8,10},{9,11},{10,... | collective-permute-start | bytes 221192 | tf_op jit(solution)/shard_map/ppermute | solution.py:45
  27.6 6.6 %collective-permute-start.10 = (bf16[4,128,256]{2,1,0:T(8,128)(2,1)S(1)}, bf16[4,128,256]{2,1,0:T(8,128)(2,1)S(1)}, u32[]{:S(2)}, u32[]{:S(2)}) collective-permute-start(bf16[4,128,256]{2,1,0:T(8,128)(2,1)S(1)} %get-tuple-element.92), channel_id=1, source_target_pairs={{0,1},{1,0},{2,3},{3,2},{4,5},{5,4},{6,7},{7,6},{8,24},{9,25},{10,... | collective-permute-start | bytes 786440 | tf_op jit(solution)/shard_map/ppermute | solution.py:45
  32.7 9.9 %collective-permute-start.4 = (bf16[4,144,256]{2,1,0:T(8,128)(2,1)S(1)}, bf16[4,144,256]{2,1,0:T(8,128)(2,1)S(1)}, u32[]{:S(2)}, u32[]{:S(2)}) collective-permute-start(bf16[4,144,256]{2,1,0:T(8,128)(2,1)S(1)} %get-tuple-element.80), channel_id=1, source_target_pairs={{0,1},{1,0},{2,3},{3,2},{4,5},{5,4},{6,7},{7,6},{8,24},{9,25},{10,... | collective-permute-start | bytes 884744 | tf_op jit(solution)/shard_map/ppermute | solution.py:45
  34.3 10.0 %collective-permute-start.11 = (bf16[2,4,128,256]{3,2,1,0:T(8,128)(2,1)S(1)}, bf16[2,4,128,256]{3,2,1,0:T(8,128)(2,1)S(1)}, u32[]{:S(2)}, u32[]{:S(2)}) collective-permute-start(bf16[2,4,128,256]{3,2,1,0:T(8,128)(2,1)S(1)} %pad_maximum_fusion.1.refs_0_), channel_id=1, source_target_pairs={{0,16},{1,17},{2,18},{3,19},{4,20},{5,21},{6,22},{7,23},{8,9},{9,8... | collective-permute-start | bytes 1572872 | tf_op jit(solution)/shard_map/ppermute | solution.py:45
  42.7 9.9 %collective-permute-start.5 = (bf16[2,4,144,256]{3,2,1,0:T(8,128)(2,1)S(1)}, bf16[2,4,144,256]{3,2,1,0:T(8,128)(2,1)S(1)}, u32[]{:S(2)}, u32[]{:S(2)}) collective-permute-start(bf16[2,4,144,256]{3,2,1,0:T(8,128)(2,1)S(1)} %pad_maximum_fusion.refs_0_), channel_id=1, source_target_pairs={{0,16},{1,17},{2,18},{3,19},{4,20},{5,21},{6,22},{7,23},{8,9},{9,8... | collective-permute-start | bytes 1769480 | tf_op jit(solution)/shard_map/ppermute | solution.py:45
  44.3 8.5 %collective-permute-start.12 = (bf16[2,4,128,256]{3,2,1,0:T(8,128)(2,1)S(1)}, bf16[2,4,128,256]{3,2,1,0:T(8,128)(2,1)}, u32[]{:S(2)}, u32[]{:S(2)}) collective-permute-start(bf16[2,4,128,256]{3,2,1,0:T(8,128)(2,1)S(1)} %pad_maximum_fusion.1.refs_0_), channel_id=1, source_target_pairs={{0,8},{1,9},{2,10},{3,11},{4,12},{5,13},{6,14},{7,15},{8,0},{9,1},... | collective-permute-start | bytes 1572872 | tf_op jit(solution)/shard_map/ppermute | solution.py:45
  44.3 8.5 %collective-permute-start.13 = (bf16[2,4,128,256]{3,2,1,0:T(8,128)(2,1)S(1)}, bf16[2,4,128,256]{3,2,1,0:T(8,128)(2,1)}, u32[]{:S(2)}, u32[]{:S(2)}) collective-permute-start(bf16[2,4,128,256]{3,2,1,0:T(8,128)(2,1)S(1)} %collective-permute-done.11.refs_1_), channel_id=1, source_target_pairs={{0,8},{1,9},{2,10},{3,11},{4,12},{5,13},{6,14},{7,15},{8,0},{9,1},... | collective-permute-start | bytes 1572872 | tf_op jit(solution)/shard_map/ppermute | solution.py:45
  44.8 15.2 %collective-permute-start.6 = (bf16[2,4,144,256]{3,2,1,0:T(8,128)(2,1)S(1)}, bf16[2,4,144,256]{3,2,1,0:T(8,128)(2,1)S(1)}, u32[]{:S(2)}, u32[]{:S(2)}) collective-permute-start(bf16[2,4,144,256]{3,2,1,0:T(8,128)(2,1)S(1)} %pad_maximum_fusion.refs_0_), channel_id=1, source_target_pairs={{0,8},{1,9},{2,10},{3,11},{4,12},{5,13},{6,14},{7,15},{8,0},{9,1},... | collective-permute-start | bytes 1769480 | tf_op jit(solution)/shard_map/ppermute | solution.py:45
  52.6 7.4 %collective-permute-start.7 = (bf16[2,4,144,256]{3,2,1,0:T(8,128)(2,1)S(1)}, bf16[2,4,144,256]{3,2,1,0:T(8,128)(2,1)S(1)}, u32[]{:S(2)}, u32[]{:S(2)}) collective-permute-start(bf16[2,4,144,256]{3,2,1,0:T(8,128)(2,1)S(1)} %collective-permute-done.5.refs_1_), channel_id=1, source_target_pairs={{0,8},{1,9},{2,10},{3,11},{4,12},{5,13},{6,14},{7,15},{8,0},{9,1},... | collective-permute-start | bytes 1769480 | tf_op jit(solution)/shard_map/ppermute | solution.py:45
  70.7 4.2 %collective-permute-start.17 = (bf16[2,2,4,128,256]{4,3,2,1,0:T(8,128)(2,1)S(1)}, bf16[2,2,4,128,256]{4,3,2,1,0:T(8,128)(2,1)S(1)}, u32[]{:S(2)}, u32[]{:S(2)}) collective-permute-start(bf16[2,2,4,128,256]{4,3,2,1,0:T(8,128)(2,1)S(1)} %get-tuple-element.53), channel_id=1, source_target_pairs={{0,8},{1,9},{2,10},{3,11},{4,12},{5,13},{6,14},{7,15},{8,0},{9,1},... | collective-permute-start | bytes 3145736 | tf_op jit(solution)/shard_map/ppermute | solution.py:45
  74.8 2.7 %collective-permute-start.14 = (bf16[2,2,4,128,256]{4,3,2,1,0:T(8,128)(2,1)S(1)}, bf16[2,2,4,128,256]{4,3,2,1,0:T(8,128)(2,1)S(1)}, u32[]{:S(2)}, u32[]{:S(2)}) collective-permute-start(bf16[2,2,4,128,256]{4,3,2,1,0:T(8,128)(2,1)S(1)} %get-tuple-element.51), channel_id=1, source_target_pairs={{0,8},{1,9},{2,10},{3,11},{4,12},{5,13},{6,14},{7,15},{8,0},{9,1},... | collective-permute-start | bytes 3145736 | tf_op jit(solution)/shard_map/ppermute | solution.py:45
  75.3 9.2 %collective-permute-start.18 = (bf16[2,4,128,256]{3,2,1,0:T(8,128)(2,1)S(1)}, bf16[2,4,128,256]{3,2,1,0:T(8,128)(2,1)S(1)}, u32[]{:S(2)}, u32[]{:S(2)}) collective-permute-start(bf16[2,4,128,256]{3,2,1,0:T(8,128)(2,1)S(1)} %fusion.3), channel_id=1, source_target_pairs={{0,16},{1,17},{2,18},{3,19},{4,20},{5,21},{6,22},{7,23},{8,9},{9,8... | collective-permute-start | bytes 1572872 | tf_op jit(solution)/shard_map/ppermute | solution.py:45
  77.8 15.1 %collective-permute-start.15 = (bf16[2,4,128,256]{3,2,1,0:T(8,128)(2,1)S(1)}, bf16[2,4,128,256]{3,2,1,0:T(8,128)(2,1)S(1)}, u32[]{:S(2)}, u32[]{:S(2)}) collective-permute-start(bf16[2,4,128,256]{3,2,1,0:T(8,128)(2,1)S(1)} %fusion.2), channel_id=1, source_target_pairs={{0,16},{1,17},{2,18},{3,19},{4,20},{5,21},{6,22},{7,23},{8,9},{9,8... | collective-permute-start | bytes 1572872 | tf_op jit(solution)/shard_map/ppermute | solution.py:45
  84.7 10.0 %collective-permute-start.19 = (bf16[4,128,256]{2,1,0:T(8,128)(2,1)S(1)}, bf16[4,128,256]{2,1,0:T(8,128)(2,1)S(1)}, u32[]{:S(2)}, u32[]{:S(2)}) collective-permute-start(bf16[4,128,256]{2,1,0:T(8,128)(2,1)S(1)} %fusion.7), channel_id=1, source_target_pairs={{0,1},{1,0},{2,3},{3,2},{4,5},{5,4},{6,7},{7,6},{8,24},{9,25},{10,... | collective-permute-start | bytes 786440 | tf_op jit(solution)/shard_map/ppermute | solution.py:45
  93.1 6.8 %collective-permute-start.16 = (bf16[4,128,256]{2,1,0:T(8,128)(2,1)S(1)}, bf16[4,128,256]{2,1,0:T(8,128)(2,1)S(1)}, u32[]{:S(2)}, u32[]{:S(2)}) collective-permute-start(bf16[4,128,256]{2,1,0:T(8,128)(2,1)S(1)} %fusion.6), channel_id=1, source_target_pairs={{0,1},{1,0},{2,3},{3,2},{4,5},{5,4},{6,7},{7,6},{8,24},{9,25},{10,... | collective-permute-start | bytes 786440 | tf_op jit(solution)/shard_map/ppermute | solution.py:45
  94.8 6.1 %collective-permute-start.22 = (bf16[128,256]{1,0:T(8,128)(2,1)S(1)}, bf16[128,256]{1,0:T(8,128)(2,1)S(1)}, u32[]{:S(2)}, u32[]{:S(2)}) collective-permute-start(bf16[128,256]{1,0:T(8,128)(2,1)S(1)} %get-tuple-element.85), channel_id=1, source_target_pairs={{0,6},{1,7},{2,4},{3,5},{4,2},{5,3},{6,0},{7,1},{8,14},{9,15},{10,... | collective-permute-start | bytes 196616 | tf_op jit(solution)/shard_map/ppermute | solution.py:45
  97.0 5.3 %collective-permute-start.21 = (bf16[128,256]{1,0:T(8,128)(2,1)S(1)}, bf16[128,256]{1,0:T(8,128)(2,1)S(1)}, u32[]{:S(2)}, u32[]{:S(2)}) collective-permute-start(bf16[128,256]{1,0:T(8,128)(2,1)S(1)} %get-tuple-element.86), channel_id=1, source_target_pairs={{0,4},{1,5},{2,6},{3,7},{4,0},{5,1},{6,2},{7,3},{8,12},{9,13},{10,... | collective-permute-start | bytes 196616 | tf_op jit(solution)/shard_map/ppermute | solution.py:45
  97.0 5.3 %collective-permute-start.20 = (bf16[128,256]{1,0:T(8,128)(2,1)S(1)}, bf16[128,256]{1,0:T(8,128)(2,1)S(1)}, u32[]{:S(2)}, u32[]{:S(2)}) collective-permute-start(bf16[128,256]{1,0:T(8,128)(2,1)S(1)} %get-tuple-element.87), channel_id=1, source_target_pairs={{0,2},{1,3},{2,0},{3,1},{4,6},{5,7},{6,4},{7,5},{8,10},{9,11},{10,... | collective-permute-start | bytes 196616 | tf_op jit(solution)/shard_map/ppermute | solution.py:45
  102.3 11.6 %collective-permute-start.23 = (bf16[128,256]{1,0:T(8,128)(2,1)S(1)}, bf16[128,256]{1,0:T(8,128)(2,1)S(1)}, u32[]{:S(2)}, u32[]{:S(2)}) collective-permute-start(bf16[128,256]{1,0:T(8,128)(2,1)S(1)} %get-tuple-element.54), channel_id=1, source_target_pairs={{0,2},{1,3},{2,0},{3,1},{4,6},{5,7},{6,4},{7,5},{8,10},{9,11},{10,... | collective-permute-start | bytes 196616 | tf_op jit(solution)/shard_map/ppermute | solution.py:45
  104.1 9.9 %collective-permute-start.24 = (bf16[128,256]{1,0:T(8,128)(2,1)S(1)}, bf16[128,256]{1,0:T(8,128)(2,1)S(1)}, u32[]{:S(2)}, u32[]{:S(2)}) collective-permute-start(bf16[128,256]{1,0:T(8,128)(2,1)S(1)} %get-tuple-element.55), channel_id=1, source_target_pairs={{0,4},{1,5},{2,6},{3,7},{4,0},{5,1},{6,2},{7,3},{8,12},{9,13},{10,... | collective-permute-start | bytes 196616 | tf_op jit(solution)/shard_map/ppermute | solution.py:45
  105.1 11.1 %collective-permute-start.25 = (bf16[128,256]{1,0:T(8,128)(2,1)S(1)}, bf16[128,256]{1,0:T(8,128)(2,1)S(1)}, u32[]{:S(2)}, u32[]{:S(2)}) collective-permute-start(bf16[128,256]{1,0:T(8,128)(2,1)S(1)} %get-tuple-element.56), channel_id=1, source_target_pairs={{0,6},{1,7},{2,4},{3,5},{4,2},{5,3},{6,0},{7,1},{8,14},{9,15},{10,... | collective-permute-start | bytes 196616 | tf_op jit(solution)/shard_map/ppermute | solution.py:45
  109.5 12.5 %copy-start.10 = (f32[256,128]{1,0:T(8,128)S(1)}, f32[256,128]{1,0:T(8,128)}, u32[]{:S(2)}) copy-start(f32[256,128]{1,0:T(8,128)} %get-tuple-element.65) | copy-start | bytes 393220
  109.5 12.1 %collective-permute-start.38 = (f32[256,128]{1,0:T(8,128)}, f32[256,128]{1,0:T(8,128)S(1)}, u32[]{:S(2)}, u32[]{:S(2)}) collective-permute-start(f32[256,128]{1,0:T(8,128)} %get-tuple-element.65), channel_id=1, source_target_pairs={{0,16},{1,17},{2,18},{3,19},{4,20},{5,21},{6,22},{7,23},{8,24},{9,... | collective-permute-start | bytes 393224 | tf_op jit(solution)/shard_map/ppermute | solution.py:45
  111.0 13.3 %copy-start.11 = (bf16[256,128]{1,0:T(8,128)(2,1)S(1)}, bf16[256,128]{1,0:T(8,128)(2,1)}, u32[]{:S(2)}) copy-start(bf16[256,128]{1,0:T(8,128)(2,1)} %get-tuple-element.66) | copy-start | bytes 196612
  111.7 10.3 %collective-permute-start.37 = (bf16[256,128]{1,0:T(8,128)(2,1)}, bf16[256,128]{1,0:T(8,128)(2,1)S(1)}, u32[]{:S(2)}, u32[]{:S(2)}) collective-permute-start(bf16[256,128]{1,0:T(8,128)(2,1)} %get-tuple-element.66), channel_id=1, source_target_pairs={{0,6},{1,7},{2,4},{3,5},{4,2},{5,3},{6,0},{7,1},{8,14},{9,15},{10,... | collective-permute-start | bytes 196616 | tf_op jit(solution)/shard_map/ppermute | solution.py:45
  113.9 8.3 %collective-permute-start.36 = (bf16[256,128]{1,0:T(8,128)(2,1)}, bf16[256,128]{1,0:T(8,128)(2,1)S(1)}, u32[]{:S(2)}, u32[]{:S(2)}) collective-permute-start(bf16[256,128]{1,0:T(8,128)(2,1)} %get-tuple-element.66), channel_id=1, source_target_pairs={{0,4},{1,5},{2,6},{3,7},{4,0},{5,1},{6,2},{7,3},{8,12},{9,13},{10,... | collective-permute-start | bytes 196616 | tf_op jit(solution)/shard_map/ppermute | solution.py:45
  114.0 10.4 %collective-permute-start.35 = (bf16[256,128]{1,0:T(8,128)(2,1)}, bf16[256,128]{1,0:T(8,128)(2,1)S(1)}, u32[]{:S(2)}, u32[]{:S(2)}) collective-permute-start(bf16[256,128]{1,0:T(8,128)(2,1)} %get-tuple-element.66), channel_id=1, source_target_pairs={{0,2},{1,3},{2,0},{3,1},{4,6},{5,7},{6,4},{7,5},{8,10},{9,11},{10,... | collective-permute-start | bytes 196616 | tf_op jit(solution)/shard_map/ppermute | solution.py:45
  119.4 9.4 %collective-permute-start.28 = (bf16[256,128]{1,0:T(8,128)(2,1)}, bf16[256,128]{1,0:T(8,128)(2,1)S(1)}, u32[]{:S(2)}, u32[]{:S(2)}) collective-permute-start(bf16[256,128]{1,0:T(8,128)(2,1)} %get-tuple-element.59), channel_id=1, source_target_pairs={{0,6},{1,7},{2,4},{3,5},{4,2},{5,3},{6,0},{7,1},{8,14},{9,15},{10,... | collective-permute-start | bytes 196616 | tf_op jit(solution)/shard_map/ppermute | solution.py:45
  121.6 6.3 %collective-permute-start.29 = (f32[256,128]{1,0:T(8,128)}, f32[256,128]{1,0:T(8,128)S(1)}, u32[]{:S(2)}, u32[]{:S(2)}) collective-permute-start(f32[256,128]{1,0:T(8,128)} %get-tuple-element.58), channel_id=1, source_target_pairs={{0,16},{1,17},{2,18},{3,19},{4,20},{5,21},{6,22},{7,23},{8,24},{9,... | collective-permute-start | bytes 393224 | tf_op jit(solution)/shard_map/ppermute | solution.py:45
  122.1 6.8 %collective-permute-start.27 = (bf16[256,128]{1,0:T(8,128)(2,1)}, bf16[256,128]{1,0:T(8,128)(2,1)S(1)}, u32[]{:S(2)}, u32[]{:S(2)}) collective-permute-start(bf16[256,128]{1,0:T(8,128)(2,1)} %get-tuple-element.59), channel_id=1, source_target_pairs={{0,4},{1,5},{2,6},{3,7},{4,0},{5,1},{6,2},{7,3},{8,12},{9,13},{10,... | collective-permute-start | bytes 196616 | tf_op jit(solution)/shard_map/ppermute | solution.py:45
  122.1 6.7 %collective-permute-start.26 = (bf16[256,128]{1,0:T(8,128)(2,1)}, bf16[256,128]{1,0:T(8,128)(2,1)S(1)}, u32[]{:S(2)}, u32[]{:S(2)}) collective-permute-start(bf16[256,128]{1,0:T(8,128)(2,1)} %get-tuple-element.59), channel_id=1, source_target_pairs={{0,2},{1,3},{2,0},{3,1},{4,6},{5,7},{6,4},{7,5},{8,10},{9,11},{10,... | collective-permute-start | bytes 196616 | tf_op jit(solution)/shard_map/ppermute | solution.py:45
  124.4 8.0 %collective-permute-start.39 = (bf16[4,256,128]{2,1,0:T(8,128)(2,1)S(1)}, bf16[4,256,128]{2,1,0:T(8,128)(2,1)S(1)}, u32[]{:S(2)}, u32[]{:S(2)}) collective-permute-start(bf16[4,256,128]{2,1,0:T(8,128)(2,1)S(1)} %get-tuple-element.82), channel_id=1, source_target_pairs={{0,1},{1,0},{2,3},{3,2},{4,5},{5,4},{6,7},{7,6},{8,24},{9,25},{10,... | collective-permute-start | bytes 786440 | tf_op jit(solution)/shard_map/ppermute | solution.py:45
  129.8 9.3 %collective-permute-start.30 = (bf16[4,256,128]{2,1,0:T(8,128)(2,1)S(1)}, bf16[4,256,128]{2,1,0:T(8,128)(2,1)S(1)}, u32[]{:S(2)}, u32[]{:S(2)}) collective-permute-start(bf16[4,256,128]{2,1,0:T(8,128)(2,1)S(1)} %get-tuple-element.84), channel_id=1, source_target_pairs={{0,1},{1,0},{2,3},{3,2},{4,5},{5,4},{6,7},{7,6},{8,24},{9,25},{10,... | collective-permute-start | bytes 786440 | tf_op jit(solution)/shard_map/ppermute | solution.py:45
  132.5 9.4 %collective-permute-start.40 = (bf16[2,4,256,128]{3,2,1,0:T(8,128)(2,1)S(1)}, bf16[2,4,256,128]{3,2,1,0:T(8,128)(2,1)}, u32[]{:S(2)}, u32[]{:S(2)}) collective-permute-start(bf16[2,4,256,128]{3,2,1,0:T(8,128)(2,1)S(1)} %pad_maximum_fusion.3.refs_0_), channel_id=1, source_target_pairs={{0,16},{1,17},{2,18},{3,19},{4,20},{5,21},{6,22},{7,23},{8,9},{9,8... | collective-permute-start | bytes 1572872 | tf_op jit(solution)/shard_map/ppermute | solution.py:45
  139.1 9.2 %collective-permute-start.31 = (bf16[2,4,256,128]{3,2,1,0:T(8,128)(2,1)S(1)}, bf16[2,4,256,128]{3,2,1,0:T(8,128)(2,1)S(1)}, u32[]{:S(2)}, u32[]{:S(2)}) collective-permute-start(bf16[2,4,256,128]{3,2,1,0:T(8,128)(2,1)S(1)} %pad_maximum_fusion.2.refs_0_), channel_id=1, source_target_pairs={{0,16},{1,17},{2,18},{3,19},{4,20},{5,21},{6,22},{7,23},{8,9},{9,8... | collective-permute-start | bytes 1572872 | tf_op jit(solution)/shard_map/ppermute | solution.py:45
  140.3 8.1 %collective-permute-start.43 = (f32[2,256,128]{2,1,0:T(8,128)S(1)}, f32[2,256,128]{2,1,0:T(8,128)S(1)}, u32[]{:S(2)}, u32[]{:S(2)}) collective-permute-start(f32[2,256,128]{2,1,0:T(8,128)S(1)} %pad_maximum_fusion.8.refs_4_), channel_id=1, source_target_pairs={{0,8},{1,9},{2,10},{3,11},{4,12},{5,13},{6,14},{7,15},{8,0},{9,1},... | collective-permute-start | bytes 786440 | tf_op jit(solution)/shard_map/ppermute | solution.py:45
  140.3 10.7 %collective-permute-start.41 = (bf16[2,4,256,128]{3,2,1,0:T(8,128)(2,1)S(1)}, bf16[2,4,256,128]{3,2,1,0:T(8,128)(2,1)}, u32[]{:S(2)}, u32[]{:S(2)}) collective-permute-start(bf16[2,4,256,128]{3,2,1,0:T(8,128)(2,1)S(1)} %pad_maximum_fusion.3.refs_0_), channel_id=1, source_target_pairs={{0,8},{1,9},{2,10},{3,11},{4,12},{5,13},{6,14},{7,15},{8,0},{9,1},... | collective-permute-start | bytes 1572872 | tf_op jit(solution)/shard_map/ppermute | solution.py:45
  141.9 9.0 %collective-permute-start.42 = (bf16[2,4,256,128]{3,2,1,0:T(8,128)(2,1)}, bf16[2,4,256,128]{3,2,1,0:T(8,128)(2,1)}, u32[]{:S(2)}, u32[]{:S(2)}) collective-permute-start(bf16[2,4,256,128]{3,2,1,0:T(8,128)(2,1)} %collective-permute-done.40.refs_1_), channel_id=1, source_target_pairs={{0,8},{1,9},{2,10},{3,11},{4,12},{5,13},{6,14},{7,15},{8,0},{9,1},... | collective-permute-start | bytes 1572872 | tf_op jit(solution)/shard_map/ppermute | solution.py:45
  141.9 13.2 %collective-permute-start.32 = (bf16[2,4,256,128]{3,2,1,0:T(8,128)(2,1)S(1)}, bf16[2,4,256,128]{3,2,1,0:T(8,128)(2,1)S(1)}, u32[]{:S(2)}, u32[]{:S(2)}) collective-permute-start(bf16[2,4,256,128]{3,2,1,0:T(8,128)(2,1)S(1)} %pad_maximum_fusion.2.refs_0_), channel_id=1, source_target_pairs={{0,8},{1,9},{2,10},{3,11},{4,12},{5,13},{6,14},{7,15},{8,0},{9,1},... | collective-permute-start | bytes 1572872 | tf_op jit(solution)/shard_map/ppermute | solution.py:45
  148.4 6.7 %collective-permute-start.33 = (bf16[2,4,256,128]{3,2,1,0:T(8,128)(2,1)S(1)}, bf16[2,4,256,128]{3,2,1,0:T(8,128)(2,1)S(1)}, u32[]{:S(2)}, u32[]{:S(2)}) collective-permute-start(bf16[2,4,256,128]{3,2,1,0:T(8,128)(2,1)S(1)} %collective-permute-done.31.refs_1_), channel_id=1, source_target_pairs={{0,8},{1,9},{2,10},{3,11},{4,12},{5,13},{6,14},{7,15},{8,0},{9,1},... | collective-permute-start | bytes 1572872 | tf_op jit(solution)/shard_map/ppermute | solution.py:45
  149.1 6.0 %collective-permute-start.34 = (f32[2,256,128]{2,1,0:T(8,128)S(1)}, f32[2,256,128]{2,1,0:T(8,128)S(1)}, u32[]{:S(2)}, u32[]{:S(2)}) collective-permute-start(f32[2,256,128]{2,1,0:T(8,128)S(1)} %pad_maximum_fusion.6.refs_4_), channel_id=1, source_target_pairs={{0,8},{1,9},{2,10},{3,11},{4,12},{5,13},{6,14},{7,15},{8,0},{9,1},... | collective-permute-start | bytes 786440 | tf_op jit(solution)/shard_map/ppermute | solution.py:45
  (16 other events, 37.9 us)

commit v3 on v2

--- a/solution.py
+++ b/solution.py
@@ -16,7 +16,12 @@
 VMEM = pl.BlockSpec(memory_space=pltpu.VMEM)
 SMEM = pl.BlockSpec(memory_space=pltpu.SMEM)
 ANY = pl.BlockSpec(memory_space=pl.ANY)
+HBM = pl.BlockSpec(memory_space=pltpu.HBM)
 ROOM = pltpu.CompilerParams(vmem_limit_bytes=32 * 2**20)
+
+
+def after(value, *others):
+    return lax.optimization_barrier((value, others))[0]
 
 
 class Plan:
@@ -59,10 +64,14 @@
     def gather_column(self, block):
         return [block] + [self.permute(block, "z", k) for k in range(1, self.Z)]
 
-    def gather_rest(self, column):
+    def gather_plane(self, column):
         column = jnp.stack(column)
-        plane = jnp.stack([column] + [self.permute(column, "q", k) for k in range(1, self.X)])
-        mine = [plane] + [self.permute(plane, "p", k) for k in range(1, self.Y)]
+        return jnp.stack([column] + [self.permute(column, "q", k) for k in range(1, self.X)])
+
+    def gather_near(self, plane):
+        return [plane] + [self.permute(plane, "p", k) for k in range(1, self.Y)]
+
+    def gather_far(self, mine):
         return mine + [self.permute(piece, "c", 1) for piece in mine]
 
     def reduce(self, keep, send):
@@ -72,7 +81,7 @@
             total = total[0]
             for k in range(1, low.shape[0] + 1):
                 total = total + self.permute(low[k - 1], axis, k).astype(F32)
-        return total[0], [total[k].astype(BF16) for k in range(1, self.Z)]
+        return total, [total[k].astype(BF16) for k in range(1, self.Z)]
 
     def reduce_column(self, low):
         return [self.permute(low[k - 1], "z", k) for k in range(1, self.Z)]
@@ -105,37 +114,32 @@
     )(place, policy_weight)
 
 
-def update_kernel(count, place_ref, mass_ref, base_ref, *refs):
+def update_kernel(count, block, first, place_ref, mass_ref, base_ref, *refs):
     terms, (w_ref, m_ref, v_ref, update_ref, low_ref) = refs[:count], refs[count:]
-    total = base_ref[...]
+    own = (slice(None), pl.ds(pl.multiple_of((first + place_ref[0]) * block, block), block))
+    total = base_ref[0]
     for term in terms:
         total = total + term[...].astype(F32)
     gradient = total.T / mass_ref[0, 0]
-    first_new = 0.9 * m_ref[...] + 0.1 * gradient
-    second_new = 0.95 * v_ref[...] + 0.05 * gradient * gradient
+    first_new = 0.9 * m_ref[own] + 0.1 * gradient
+    second_new = 0.95 * v_ref[own] + 0.05 * gradient * gradient
     update = first_new / (jnp.sqrt(second_new) + 1e-08)
     update_ref[...] = update
-    low_ref[...] = (w_ref[...] - STEP_RATE * update).astype(BF16)
+    low_ref[...] = (w_ref[own] - STEP_RATE * update).astype(BF16)
 
 
 def own_update(plan, j, place, mass, base, terms, policy_weight, first_moment, second_moment):
     depth = policy_weight.shape[0]
     block = plan.block
-    whole = pl.BlockSpec((block, depth), lambda i, place: (0, 0))
-    own = pl.BlockSpec((depth, block), lambda i, place: (0, j * 2 * plan.Y + place[0]))
-    out = pl.BlockSpec((depth, block), lambda i, place: (0, 0))
     return pl.pallas_call(
-        functools.partial(update_kernel, len(terms)),
-        grid_spec=pltpu.PrefetchScalarGridSpec(
-            num_scalar_prefetch=1,
-            grid=(1,),
-            in_specs=[SMEM, whole] + [whole] * len(terms) + [own] * 3,
-            out_specs=[out, out],
-        ),
+        functools.partial(update_kernel, len(terms), block, j * 2 * plan.Y),
+        in_specs=[SMEM, SMEM] + [VMEM] * (len(terms) + 4),
+        out_specs=[VMEM, VMEM],
         out_shape=[
             jax.ShapeDtypeStruct((depth, block), F32),
             jax.ShapeDtypeStruct((depth, block), BF16),
         ],
+        compiler_params=pltpu.CompilerParams(vmem_limit_bytes=16 * 2**20),
         name="update",
     )(place, mass, base, *terms, policy_weight, first_moment, second_moment)
 
@@ -241,13 +245,12 @@
     )
 
 
-def weight_kernel(plan, segs, samples, total, here_ref, *refs):
-    pieces, (weight_ref, mass_ref, norm_ref, known_ref) = refs[: 2 * plan.Y], refs[2 * plan.Y :]
+def step_weights(plan, here, segs, samples, total, pieces, weight_ref, mass_ref, norm_ref, known_ref):
     lanes = weight_ref.shape[1]
     steps = lanes // segs
     owners = plan.C * plan.Y
-    c = here_ref[1]
-    me = here_ref[0] * plan.C + c
+    c = here[1]
+    me = here[0] * plan.C + c
     depth = pieces[0].shape[-1]
     parts = lanes // depth
     for other in range(2):
@@ -291,24 +294,6 @@
         norm_ref[o : o + 1, :] = normalized[o * plan.mp : o * plan.mp + 1, :]
 
 
-def step_weights(plan, here, pieces, segs, samples, lanes, total):
-    owners = plan.C * plan.Y
-    depth = pieces[0].shape[-1]
-    return pl.pallas_call(
-        functools.partial(weight_kernel, plan, segs, samples, total),
-        in_specs=[SMEM] + [VMEM] * len(pieces),
-        out_specs=[VMEM, SMEM, VMEM],
-        out_shape=[
-            jax.ShapeDtypeStruct((1, lanes), F32),
-            jax.ShapeDtypeStruct((1, 1), F32),
-            jax.ShapeDtypeStruct((owners, lanes), F32),
-        ],
-        scratch_shapes=[pltpu.VMEM((owners * plan.mp, lanes + depth), F32)],
-        compiler_params=ROOM,
-        name="weights",
-    )(here, *pieces)
-
-
 def gradient_chunk(plan, here, sig_ref, n_ref, keep_ref, send_ref):
     y, c, z, x = here
     rows = plan.Y * plan.block
@@ -387,7 +372,8 @@
     pieces, refs = refs[: 2 * plan.Y], refs[2 * plan.Y :]
     n_ref, l_ref, top_ref, wt_ref, w_sems = refs
     here = tuple(here_ref[i] for i in range(4))
-    for copy in fetch_policy(plan, here, 0, pieces, wt_ref, w_sems):
+    copies = fetch_policy(plan, here, 0, pieces, wt_ref, w_sems)
+    for copy in copies:
         copy.wait()
     chunk_logits(wt_ref, n_ref, l_ref, 0, top_ref)
 
@@ -423,15 +409,18 @@
     lax.fori_loop(0, tiles, step, 0)
 
 
-def signal_kernel(plan, here_ref, w_ref, act_ref, *refs):
+def signal_kernel(plan, segs, samples, total, here_ref, act_ref, *refs):
     pieces, refs = refs[: 2 * plan.Y], refs[2 * plan.Y :]
     n_ref, refs = refs[0], refs[1:]
     early = plan.J - 1
     known, refs = refs[: 2 * early], refs[2 * early :]
+    mass_ref, norm_ref, refs = refs[0], refs[1], refs[2:]
     rest, refs = refs[:early], refs[early:]
-    keep_ref, send_ref, wt_ref, l_ref, top_ref, sig_ref, w_sems = refs
+    keep_ref, send_ref, wt_ref, w_ref, known_ref, l_ref, top_ref, sig_ref, w_sems = refs
     here = tuple(here_ref[i] for i in range(4))
-    for copy in fetch_policy(plan, here, early, pieces, wt_ref, w_sems):
+    copies = fetch_policy(plan, here, early, pieces, wt_ref, w_sems)
+    step_weights(plan, here, segs, samples, total, pieces, w_ref, mass_ref, norm_ref, known_ref)
+    for copy in copies:
         copy.wait()
     chunk_logits(wt_ref, n_ref, l_ref, early * wt_ref.shape[0], top_ref)
     signals(known, l_ref, (sig_ref,) + tuple(rest), w_ref, act_ref, top_ref)
@@ -453,7 +442,7 @@
     rows = count // plan.J
     return pl.pallas_call(
         functools.partial(logits_kernel, plan),
-        in_specs=[SMEM] + [VMEM] * (len(pieces) + 1),
+        in_specs=[SMEM] + [VMEM] * len(pieces) + [VMEM],
         out_specs=[VMEM, VMEM],
         out_shape=[
             jax.ShapeDtypeStruct((tokens // TILE, rows, TILE), F32),
@@ -473,22 +462,27 @@
     )(here, *pieces, normed)
 
 
-def signal_and_gradient(plan, here, weights, actions, pieces, normed, count):
+def signal_and_gradient(plan, here, actions, last, normed, known, count, segs, samples, total):
     tokens, width = normed.shape
     depth = width // plan.mp
     rows = count // plan.J
-    known = []
-    for piece in pieces[:-1]:
-        known += early_logits(plan, here, piece, normed, count)
-    last = pieces[-1]
+    known = [value for pair in known for value in pair]
     signal = jax.ShapeDtypeStruct((rows, tokens), BF16)
-    *rest, keep, send = pl.pallas_call(
-        functools.partial(signal_kernel, plan),
-        in_specs=[SMEM, VMEM, VMEM] + [VMEM] * (len(last) + 1 + len(known)),
-        out_specs=[VMEM] * (plan.J + 1),
-        out_shape=[signal] * (plan.J - 1) + chunk_shapes(plan, depth),
+    owners = plan.C * plan.Y
+    mass, norm, *rest, keep, send = pl.pallas_call(
+        functools.partial(signal_kernel, plan, segs, samples, total),
+        in_specs=[SMEM, VMEM] + [VMEM] * len(last) + [VMEM] + [VMEM] * len(known),
+        out_specs=[SMEM] + [VMEM] * (plan.J + 2),
+        out_shape=[
+            jax.ShapeDtypeStruct((1, 1), F32),
+            jax.ShapeDtypeStruct((owners, tokens), F32),
+        ]
+        + [signal] * (plan.J - 1)
+        + chunk_shapes(plan, depth),
         scratch_shapes=[
             pltpu.VMEM((rows, width), BF16),
+            pltpu.VMEM((1, tokens), F32),
+            pltpu.VMEM((owners * plan.mp, tokens + depth), F32),
             pltpu.VMEM((tokens // TILE, count, TILE), F32),
             pltpu.VMEM((tokens // TILE, 1, TILE), F32),
             pltpu.VMEM((rows, tokens), BF16),
@@ -501,7 +495,7 @@
             transcendentals=tokens * count,
         ),
         name="signal",
-    )(here, weights, actions, *last, normed, *known)
+    )(here, actions, *last, normed, *known)
     chunks = [(keep, send)]
     for later in rest:
         chunks.append(
@@ -519,16 +513,15 @@
                 name="gradient",
             )(here, later, normed)
         )
-    return chunks
-
-
-def assemble_kernel(plan, j, here_ref, *refs):
-    count = 2 * plan.Y
-    pieces, refs = refs[:count], refs[count:]
-    near, far = refs[:2]
+    return mass, norm, chunks
+
+
+def assemble_kernel(plan, here_ref, *refs):
+    count = 2 * plan.Y * plan.J
+    pieces, updates = refs[:count], refs[count : count + 2 * plan.J]
     actor_ref, update_ref, sems = refs[-3:]
     y, c, z, x = (here_ref[i] for i in range(4))
-    depth = near.shape[-2]
+    depth = updates[0].shape[-2]
     block = plan.block
     copies = []
 
@@ -537,50 +530,49 @@
         moved.start()
         copies.append(moved)
 
-    for other in range(2):
-        core = c ^ other
-        for dy in range(plan.Y):
-            col = ((j * 2 + core) * plan.Y + (y ^ dy)) * block
-            copy(
-                (far if other else near).at[dy],
-                update_ref.at[:, pl.ds(pl.multiple_of(col, block), block)],
-            )
-        for p in range(plan.Y):
-            piece = pieces[other * plan.Y + p]
-            for q in range(plan.X):
-                a, b = plan.relative(core, p, q)
-                for dz in range(plan.Z):
-                    col = ((j * 2 + core) * plan.Y + (y ^ a)) * block
-                    row = ((z ^ dz) * plan.X + (x ^ b)) * depth
-                    copy(
-                        piece.at[q, dz],
-                        actor_ref.at[
-                            pl.ds(pl.multiple_of(row, depth), depth),
-                            pl.ds(pl.multiple_of(col, block), block),
-                        ],
-                    )
+    for j in range(plan.J):
+        for other in range(2):
+            core = c ^ other
+            for dy in range(plan.Y):
+                col = ((j * 2 + core) * plan.Y + (y ^ dy)) * block
+                copy(
+                    updates[2 * j + other].at[dy],
+                    update_ref.at[:, pl.ds(pl.multiple_of(col, block), block)],
+                )
+            for p in range(plan.Y):
+                piece = pieces[(j * 2 + other) * plan.Y + p]
+                for q in range(plan.X):
+                    a, b = plan.relative(core, p, q)
+                    for dz in range(plan.Z):
+                        col = ((j * 2 + core) * plan.Y + (y ^ a)) * block
+                        row = ((z ^ dz) * plan.X + (x ^ b)) * depth
+                        copy(
+                            piece.at[q, dz],
+                            actor_ref.at[
+                                pl.ds(pl.multiple_of(row, depth), depth),
+                                pl.ds(pl.multiple_of(col, block), block),
+                            ],
+                        )
     for moved in copies:
         moved.wait()
 
 
-def assemble(plan, j, here, pieces, near, far, before, width, count):
+def assemble(plan, here, pieces, updates, width, count):
     depth = width // plan.mp
-    taken = len(pieces) + 3
     return pl.pallas_call(
-        functools.partial(assemble_kernel, plan, j),
-        in_specs=[SMEM] + [VMEM] * (len(pieces) + 2) + [ANY] * len(before),
+        functools.partial(assemble_kernel, plan),
+        in_specs=[SMEM] + [VMEM] * (len(pieces) + len(updates)),
         out_specs=[ANY] * 2,
         out_shape=[
             jax.ShapeDtypeStruct((width, count), BF16),
             jax.ShapeDtypeStruct((depth, count), F32),
         ],
         scratch_shapes=[
-            pltpu.SemaphoreType.DMA((len(pieces) * plan.X * plan.Z + 2 * plan.Y,)),
-        ],
-        input_output_aliases={taken + i: i for i in range(len(before))},
-        compiler_params=pltpu.CompilerParams(vmem_limit_bytes=32 * 2**20),
+            pltpu.SemaphoreType.DMA((len(pieces) * plan.X * plan.Z + len(updates) * plan.Y,)),
+        ],
+        compiler_params=ROOM,
         name="assemble",
-    )(here, *pieces, near, far, *before)
+    )(here, *pieces, *updates)
 
 
 def body(
@@ -609,7 +601,7 @@
     low = own_shard(plan, place, policy_weight)
     stages = [plan.gather_column(block) for block in low[:-1]]
     if stages:
-        norm_gain = lax.optimization_barrier((norm_gain, stages[0][1]))[0]
+        norm_gain = after(norm_gain, stages[0][1])
 
     asked = sample_owner[:, 0] * segs + sample_row
     normed, block = normalize(
@@ -622,16 +614,22 @@
         asked,
         low[-1],
     )
-    stages.append(plan.gather_column(block))
-    pieces = [plan.gather_rest(column) for column in stages]
+    column = plan.gather_column(block)
+    planes = [plan.gather_plane([after(first[0], block)] + first[1:]) for first in stages]
+    near = [plan.gather_near(after(plane, column[1])) for plane in planes]
+    mine = plan.gather_near(plan.gather_plane(column))
+    pieces = [plan.gather_far(piece) for piece in near]
+    known = [early_logits(plan, here, piece, normed, count) for piece in pieces]
+    pieces.append(plan.gather_far(mine))
+
     token_total = owners_all * columns * samples * seg_len
-    weights, total_weight, column = step_weights(plan, here, pieces[-1], segs, samples, segs * seg_len, token_total)
+    total_weight, column, chunks = signal_and_gradient(
+        plan, here, actions.reshape(1, -1), pieces[-1], normed, known, count, segs, samples, token_total
+    )
     owner = (asked // segs) ^ replay
     slot = ((owner % plan.C) * plan.Y + owner // plan.C) * segs + asked % segs
     local_norm = column.reshape(owners_all * segs, seg_len)[slot].reshape(-1)
-
-    chunks = signal_and_gradient(plan, here, weights, actions.reshape(1, -1), pieces, normed, count)
-    outs, terms = (), None
+    fresh, updates, terms = [], [], None
     for j, (keep, send) in enumerate(chunks):
         base, low = plan.reduce(keep, send)
         if terms is not None:
@@ -642,9 +640,9 @@
         )
         near = jnp.stack([update] + [plan.permute(update, "y", k) for k in range(1, plan.Y)])
         column, near = lax.optimization_barrier((plan.gather_column(low), near))
-        far = plan.permute(near, "c", 1)
-        outs = assemble(plan, j, here, plan.gather_rest(column), near, far, outs, width, count)
-    actor_policy, update = outs
+        updates += [near, plan.permute(near, "c", 1)]
+        fresh += plan.gather_far(plan.gather_near(plan.gather_plane(column)))
+    actor_policy, update = assemble(plan, here, fresh, updates, width, count)
     return (local_norm, update, actor_policy)
 
 

time: 158 us -> 153 us (0.968)
  Pallas kernels: 35.1 us -> 29.6 us
  waiting for transfers between devices: 51 us -> 53.2 us
  starting transfers between devices: 50.5 us -> 52.6 us
  other arithmetic: 3.86 us -> 2.1 us
  local copies, waits for them, and re-layouts: 16 us -> 14.3 us
    pallas_call x6 -> x4, Pallas kernels: 21.5 us -> 16.1 us  [the longest x1 10.1 us: signal_and_gradient(): pl.pallas_call(functools.partial(signal_kernel, plan, segs, samples, tota...]
    ppermute x44, waiting for transfers between devices: 51 us -> 53.2 us  [permute(): return lax.ppermute(value, ALL, pairs)]
    ppermute x44, starting transfers between devices: 50.5 us -> 52.6 us  [permute(): return lax.ppermute(value, ALL, pairs)]
    unnamed x40 -> x28, local copies, waits for them, and re-layouts: 11.6 us -> 11.2 us
  transfers between devices with their start and end apart: 44 -> 44, of which waited for: 15 -> 18; matrix products, arithmetic and copies ran while one was open for 5% -> 3% of each run, Pallas kernels for 13% -> 8%
where the time goes in v3:
time: 153 us
  waiting for transfers between devices  53.2 us (35%)
  starting transfers between devices  52.6 us (34%)
  Pallas kernels  29.6 us (19%)
  local copies, waits for them, and re-layouts  14.3 us (9%)
  other arithmetic  2.1 us (1%)
    ppermute x44, waiting for transfers between devices, permute(): return lax.ppermute(value, ALL, pairs)  53.2 us
    ppermute x44, starting transfers between devices, permute(): return lax.ppermute(value, ALL, pairs)  52.6 us
    unnamed x28, local copies, waits for them, and re-layouts  11.2 us
    pallas_call x1, Pallas kernels, signal_and_gradient(): pl.pallas_call(functools.partial(signal_kernel, plan, segs, samples, tota...  10.1 us
    pallas_call x1, Pallas kernels, early_logits(): pl.pallas_call(functools.partial(logits_kernel, plan), in_specs=[SMEM] +...  5.03 us
    pallas_call x1, Pallas kernels, assemble(): pl.pallas_call(functools.partial(assemble_kernel, plan), in_specs=[SMEM]...  4.36 us
    pallas_call x1, Pallas kernels, signal_and_gradient(): pl.pallas_call(functools.partial(gradient_kernel, plan), in_specs=[SMEM,...  3.5 us
    pallas_call x1, Pallas kernels, normalize(): pl.pallas_call(norm_kernel, grid=(tokens // tile,), in_specs=[pl.BlockSpe...  3.26 us
  transfers between devices with their start and end apart: 44, of which 18 were waited for; matrix products, arithmetic and copies ran while one was open for 3% of the time, Pallas kernels for 8%

profile of v3, /device:TPU:0, one launch (start us, length us, event | category | flops | bytes accessed | tf_op | source)
XLA Modules:
  0.0 152.9 jit_solution(1531536458467509111)
XLA Ops:
  0.7 1.8 %shard.1 = (bf16[128,256]{1,0:T(8,128)(2,1)}, bf16[128,256]{1,0:T(8,128)(2,1)}) custom-call(s32[1]{0:T(128)} %bitcast.5.place_ref, f32[256,1024]{1,0:T(8,128)} %refs_3_.3), custom_call_target="tpu_custom_call" | custom-call | tf_op jit(solution)/shard_map/shard/pallas_call | solution.py:107
  2.4 3.1 %collective-permute-start = (bf16[128,256]{1,0:T(8,128)(2,1)}, bf16[128,256]{1,0:T(8,128)(2,1)S(1)}, u32[]{:S(2)}, u32[]{:S(2)}) collective-permute-start(bf16[128,256]{1,0:T(8,128)(2,1)} %get-tuple-element.43), channel_id=1, source_target_pairs={{0,2},{1,3},{2,0},{3,1},{4,6},{5,7},{6,4},{7,5},{8,10},{9,11},{10,... | collective-permute-start | bytes 196616 | tf_op jit(solution)/shard_map/ppermute | solution.py:50
  5.5 2.6 %collective-permute-start.8 = (bf16[128,256]{1,0:T(8,128)(2,1)}, bf16[128,256]{1,0:T(8,128)(2,1)S(1)}, u32[]{:S(2)}, u32[]{:S(2)}) collective-permute-start(bf16[128,256]{1,0:T(8,128)(2,1)} %get-tuple-element.43), channel_id=1, source_target_pairs={{0,4},{1,5},{2,6},{3,7},{4,0},{5,1},{6,2},{7,3},{8,12},{9,13},{10,... | collective-permute-start | bytes 196616 | tf_op jit(solution)/shard_map/ppermute | solution.py:50
  10.3 2.2 %copy-done.1 = bf16[32,32,2048]{2,1,0:T(8,128)(2,1)S(1)} copy-done((bf16[32,32,2048]{2,1,0:T(8,128)(2,1)S(1)}, bf16[32,32,2048]{2,1,0:T(8,128)(2,1)}, u32[]{:S(2)}) %copy-start.1) | copy-done | bytes 4194328
  15.4 3.3 %normalize.1 = (bf16[1024,2048]{1,0:T(8,128)(2,1)S(1)}, bf16[144,256]{1,0:T(8,128)(2,1)S(1)}) custom-call(bf16[1024,2048]{1,0:T(8,128)(2,1)S(1)} %bitcast.86, f32[1,2048]{1,0:T(1,128)S(1)} %bitcast.92, bf16[16,2048]{1,0:T(8,128)(2,1)S(1)} %broadcast_in_dim.12.value_ref, bf16[32,32]{1,0:T(8,128)(2,1)S(1)} %copy-done.7, s32[32,32]{1,0:T(8,128)S(1)} %copy-done.5, ...), custom_call_target="tpu_custom_call" | custom-call | flops 20971520 | bytes 8388608 | tf_op jit(solution)/shard_map/normalize/pallas_call | solution.py:212
  18.7 2.0 %copy-done.8 = bf16[1024,2048]{1,0:T(8,128)(2,1)} copy-done((bf16[1024,2048]{1,0:T(8,128)(2,1)}, bf16[1024,2048]{1,0:T(8,128)(2,1)S(1)}, u32[]{:S(2)}) %copy-start.8) | copy-done | bytes 4194328
  20.7 0.9 collective-permute-start.1
  21.6 3.5 %collective-permute-start.2 = (bf16[144,256]{1,0:T(8,128)(2,1)S(1)}, bf16[144,256]{1,0:T(8,128)(2,1)S(1)}, u32[]{:S(2)}, u32[]{:S(2)}) collective-permute-start(bf16[144,256]{1,0:T(8,128)(2,1)S(1)} %get-tuple-element.41), channel_id=1, source_target_pairs={{0,4},{1,5},{2,6},{3,7},{4,0},{5,1},{6,2},{7,3},{8,12},{9,13},{10,... | collective-permute-start | bytes 221192 | tf_op jit(solution)/shard_map/ppermute | solution.py:50
  25.2 1.8 %collective-permute-start.10 = (bf16[4,128,256]{2,1,0:T(8,128)(2,1)S(1)}, bf16[4,128,256]{2,1,0:T(8,128)(2,1)S(1)}, u32[]{:S(2)}, u32[]{:S(2)}) collective-permute-start(bf16[4,128,256]{2,1,0:T(8,128)(2,1)S(1)} %get-tuple-element.90), channel_id=1, source_target_pairs={{0,1},{1,0},{2,3},{3,2},{4,5},{5,4},{6,7},{7,6},{8,24},{9,25},{10,... | collective-permute-start | bytes 786440 | tf_op jit(solution)/shard_map/ppermute | solution.py:50
  26.9 2.5 %collective-permute-done.2 = bf16[144,256]{1,0:T(8,128)(2,1)S(1)} collective-permute-done((bf16[144,256]{1,0:T(8,128)(2,1)S(1)}, bf16[144,256]{1,0:T(8,128)(2,1)S(1)}, u32[]{:S(2)}, u32[]{:S(2)}) %collective-permute-start.2) | collective-permute-done | bytes 73760 | tf_op jit(solution)/shard_map/ppermute | solution.py:50
  29.4 1.8 %collective-permute-done.3 = bf16[144,256]{1,0:T(8,128)(2,1)S(1)} collective-permute-done((bf16[144,256]{1,0:T(8,128)(2,1)S(1)}, bf16[144,256]{1,0:T(8,128)(2,1)S(1)}, u32[]{:S(2)}, u32[]{:S(2)}) %collective-permute-start.3) | collective-permute-done | bytes 73760 | tf_op jit(solution)/shard_map/ppermute | solution.py:50
  31.3 1.6 %collective-permute-start.4 = (bf16[4,144,256]{2,1,0:T(8,128)(2,1)S(1)}, bf16[4,144,256]{2,1,0:T(8,128)(2,1)S(1)}, u32[]{:S(2)}, u32[]{:S(2)}) collective-permute-start(bf16[4,144,256]{2,1,0:T(8,128)(2,1)S(1)} %get-tuple-element.78), channel_id=1, source_target_pairs={{0,1},{1,0},{2,3},{3,2},{4,5},{5,4},{6,7},{7,6},{8,24},{9,25},{10,... | collective-permute-start | bytes 884744 | tf_op jit(solution)/shard_map/ppermute | solution.py:50
  32.9 1.6 %collective-permute-start.11 = (bf16[2,4,128,256]{3,2,1,0:T(8,128)(2,1)S(1)}, bf16[2,4,128,256]{3,2,1,0:T(8,128)(2,1)}, u32[]{:S(2)}, u32[]{:S(2)}) collective-permute-start(bf16[2,4,128,256]{3,2,1,0:T(8,128)(2,1)S(1)} %pad_maximum_fusion.1.refs_0_), channel_id=1, source_target_pairs={{0,16},{1,17},{2,18},{3,19},{4,20},{5,21},{6,22},{7,23},{8,9},{9,8... | collective-permute-start | bytes 1572872 | tf_op jit(solution)/shard_map/ppermute | solution.py:50
  34.5 6.8 %collective-permute-done.4 = bf16[4,144,256]{2,1,0:T(8,128)(2,1)S(1)} collective-permute-done((bf16[4,144,256]{2,1,0:T(8,128)(2,1)S(1)}, bf16[4,144,256]{2,1,0:T(8,128)(2,1)S(1)}, u32[]{:S(2)}, u32[]{:S(2)}) %collective-permute-start.4) | collective-permute-done | bytes 294944 | tf_op jit(solution)/shard_map/ppermute | solution.py:50
  41.4 1.6 %collective-permute-start.5 = (bf16[2,4,144,256]{3,2,1,0:T(8,128)(2,1)S(1)}, bf16[2,4,144,256]{3,2,1,0:T(8,128)(2,1)S(1)}, u32[]{:S(2)}, u32[]{:S(2)}) collective-permute-start(bf16[2,4,144,256]{3,2,1,0:T(8,128)(2,1)S(1)} %pad_maximum_fusion.refs_0_), channel_id=1, source_target_pairs={{0,16},{1,17},{2,18},{3,19},{4,20},{5,21},{6,22},{7,23},{8,9},{9,8... | collective-permute-start | bytes 1769480 | tf_op jit(solution)/shard_map/ppermute | solution.py:50
  43.5 7.8 %collective-permute-done.5.refs_1_ = bf16[2,4,144,256]{3,2,1,0:T(8,128)(2,1)S(1)} collective-permute-done((bf16[2,4,144,256]{3,2,1,0:T(8,128)(2,1)S(1)}, bf16[2,4,144,256]{3,2,1,0:T(8,128)(2,1)S(1)}, u32[]{:S(2)}, u32[]{:S(2)}) %collective-permute-start.5) | collective-permute-done | bytes 589856 | tf_op jit(solution)/shard_map/ppermute | solution.py:50
  51.5 2.2 %copy-done.9 = bf16[1024,2048]{1,0:T(8,128)(2,1)S(1)} copy-done((bf16[1024,2048]{1,0:T(8,128)(2,1)S(1)}, bf16[1024,2048]{1,0:T(8,128)(2,1)}, u32[]{:S(2)}) %copy-start.9) | copy-done | bytes 4194328
  53.7 5.0 %logits.1 = (f32[4,512,256]{2,1,0:T(8,128)S(1)}, f32[4,1,256]{2,1,0:T(1,128)S(1)}) custom-call(s32[4]{0:T(128)S(1)} %pad_add_fusion.here_ref, bf16[2,4,128,256]{3,2,1,0:T(8,128)(2,1)S(1)} %pad_maximum_fusion.1.refs_0_, bf16[2,4,128,256]{3,2,1,0:T(8,128)(2,1)} %collective-permute-done.11.refs_1_, bf16[2,4,128,256]{3,2,1,0:T(8,128)(2,1)} %collective-permute-done.12.refs_2_, ...), custom_call_target="tpu_custom_call" | custom-call | flops 2147483648 | bytes 8388608 | tf_op jit(solution)/shard_map/logits/pallas_call | solution.py:443
  59.5 1.1 copy-done.11
  60.6 10.1 %signal.1 = (f32[1,1]{1,0:T(1,128)}, f32[4,1024]{1,0:T(4,128)S(1)}, bf16[512,1024]{1,0:T(8,128)(2,1)S(1)}, f32[2,2,4,128,256]{4,3,2,1,0:T(8,128)S(1)}, bf16[2,2,4,128,256]{4,3,2,1,0:T(8,128)(2,1)S(1)}) custom-call(s32[4]{0:T(128)S(1)} %pad_add_fusion.here_ref, s32[1,1024]{1,0:T(1,128)S(1)} %reshape.36.act_ref, ...), custom_call_target="tpu_custom_call" | custom-call | flops 4294967296 | bytes 14680064 | tf_op jit(solution)/shard_map/signal/pallas_call | solution.py:472
  71.3 3.5 %gradient.1 = (f32[2,2,4,128,256]{4,3,2,1,0:T(8,128)S(1)}, bf16[2,2,4,128,256]{4,3,2,1,0:T(8,128)(2,1)S(1)}) custom-call(s32[4]{0:T(128)S(1)} %pad_add_fusion.here_ref, bf16[512,1024]{1,0:T(8,128)(2,1)S(1)} %get-tuple-element.57.sig_ref, bf16[1024,2048]{1,0:T(8,128)(2,1)S(1)} %copy-done.9), custom_call_target="tpu_custom_call" | custom-call | flops 2147483648 | bytes 6291456 | tf_op jit(solution)/shard_map/gradient/pallas_call | solution.py:502
  75.2 1.6 %collective-permute-start.15 = (bf16[2,4,128,256]{3,2,1,0:T(8,128)(2,1)S(1)}, bf16[2,4,128,256]{3,2,1,0:T(8,128)(2,1)S(1)}, u32[]{:S(2)}, u32[]{:S(2)}) collective-permute-start(bf16[2,4,128,256]{3,2,1,0:T(8,128)(2,1)S(1)} %fusion.2), channel_id=1, source_target_pairs={{0,16},{1,17},{2,18},{3,19},{4,20},{5,21},{6,22},{7,23},{8,9},{9,8... | collective-permute-start | bytes 1572872 | tf_op jit(solution)/shard_map/ppermute | solution.py:50
  77.9 1.6 %collective-permute-start.29 = (bf16[2,4,128,256]{3,2,1,0:T(8,128)(2,1)S(1)}, bf16[2,4,128,256]{3,2,1,0:T(8,128)(2,1)S(1)}, u32[]{:S(2)}, u32[]{:S(2)}) collective-permute-start(bf16[2,4,128,256]{3,2,1,0:T(8,128)(2,1)S(1)} %fusion.3), channel_id=1, source_target_pairs={{0,16},{1,17},{2,18},{3,19},{4,20},{5,21},{6,22},{7,23},{8,9},{9,8... | collective-permute-start | bytes 1572872 | tf_op jit(solution)/shard_map/ppermute | solution.py:50
  79.4 5.0 %collective-permute-done.15 = bf16[2,4,128,256]{3,2,1,0:T(8,128)(2,1)S(1)} collective-permute-done((bf16[2,4,128,256]{3,2,1,0:T(8,128)(2,1)S(1)}, bf16[2,4,128,256]{3,2,1,0:T(8,128)(2,1)S(1)}, u32[]{:S(2)}, u32[]{:S(2)}) %collective-permute-start.15) | collective-permute-done | bytes 524320 | tf_op jit(solution)/shard_map/ppermute | solution.py:50
  84.6 1.6 %collective-permute-start.16 = (bf16[4,128,256]{2,1,0:T(8,128)(2,1)S(1)}, bf16[4,128,256]{2,1,0:T(8,128)(2,1)S(1)}, u32[]{:S(2)}, u32[]{:S(2)}) collective-permute-start(bf16[4,128,256]{2,1,0:T(8,128)(2,1)S(1)} %fusion.6), channel_id=1, source_target_pairs={{0,1},{1,0},{2,3},{3,2},{4,5},{5,4},{6,7},{7,6},{8,24},{9,25},{10,... | collective-permute-start | bytes 786440 | tf_op jit(solution)/shard_map/ppermute | solution.py:50
  86.1 6.7 %collective-permute-done.29 = bf16[2,4,128,256]{3,2,1,0:T(8,128)(2,1)S(1)} collective-permute-done((bf16[2,4,128,256]{3,2,1,0:T(8,128)(2,1)S(1)}, bf16[2,4,128,256]{3,2,1,0:T(8,128)(2,1)S(1)}, u32[]{:S(2)}, u32[]{:S(2)}) %collective-permute-start.29) | collective-permute-done | bytes 524320 | tf_op jit(solution)/shard_map/ppermute | solution.py:50
  93.1 1.6 %collective-permute-start.30 = (bf16[4,128,256]{2,1,0:T(8,128)(2,1)S(1)}, bf16[4,128,256]{2,1,0:T(8,128)(2,1)S(1)}, u32[]{:S(2)}, u32[]{:S(2)}) collective-permute-start(bf16[4,128,256]{2,1,0:T(8,128)(2,1)S(1)} %fusion.7), channel_id=1, source_target_pairs={{0,1},{1,0},{2,3},{3,2},{4,5},{5,4},{6,7},{7,6},{8,24},{9,25},{10,... | collective-permute-start | bytes 786440 | tf_op jit(solution)/shard_map/ppermute | solution.py:50
  94.8 1.8 %collective-permute-start.18 = (bf16[128,256]{1,0:T(8,128)(2,1)S(1)}, bf16[128,256]{1,0:T(8,128)(2,1)S(1)}, u32[]{:S(2)}, u32[]{:S(2)}) collective-permute-start(bf16[128,256]{1,0:T(8,128)(2,1)S(1)} %get-tuple-element.87), channel_id=1, source_target_pairs={{0,4},{1,5},{2,6},{3,7},{4,0},{5,1},{6,2},{7,3},{8,12},{9,13},{10,... | collective-permute-start | bytes 196616 | tf_op jit(solution)/shard_map/ppermute | solution.py:50
  96.6 2.6 %collective-permute-start.19 = (bf16[128,256]{1,0:T(8,128)(2,1)S(1)}, bf16[128,256]{1,0:T(8,128)(2,1)S(1)}, u32[]{:S(2)}, u32[]{:S(2)}) collective-permute-start(bf16[128,256]{1,0:T(8,128)(2,1)S(1)} %get-tuple-element.86), channel_id=1, source_target_pairs={{0,6},{1,7},{2,4},{3,5},{4,2},{5,3},{6,0},{7,1},{8,14},{9,15},{10,... | collective-permute-start | bytes 196616 | tf_op jit(solution)/shard_map/ppermute | solution.py:50
  100.5 2.3 %collective-permute-done.19.refs_2_ = bf16[128,256]{1,0:T(8,128)(2,1)S(1)} collective-permute-done((bf16[128,256]{1,0:T(8,128)(2,1)S(1)}, bf16[128,256]{1,0:T(8,128)(2,1)S(1)}, u32[]{:S(2)}, u32[]{:S(2)}) %collective-permute-start.19) | collective-permute-done | bytes 65568 | tf_op jit(solution)/shard_map/ppermute | solution.py:50
  103.6 1.6 %collective-permute-start.23 = (f32[256,128]{1,0:T(8,128)S(1)}, f32[256,128]{1,0:T(8,128)S(1)}, u32[]{:S(2)}, u32[]{:S(2)}) collective-permute-start(f32[256,128]{1,0:T(8,128)S(1)} %get-tuple-element.52), channel_id=1, source_target_pairs={{0,16},{1,17},{2,18},{3,19},{4,20},{5,21},{6,22},{7,23},{8,24},{9,... | collective-permute-start | bytes 393224 | tf_op jit(solution)/shard_map/ppermute | solution.py:50
  105.9 2.4 %collective-permute-start.32 = (bf16[128,256]{1,0:T(8,128)(2,1)S(1)}, bf16[128,256]{1,0:T(8,128)(2,1)S(1)}, u32[]{:S(2)}, u32[]{:S(2)}) collective-permute-start(bf16[128,256]{1,0:T(8,128)(2,1)S(1)} %get-tuple-element.61), channel_id=1, source_target_pairs={{0,4},{1,5},{2,6},{3,7},{4,0},{5,1},{6,2},{7,3},{8,12},{9,13},{10,... | collective-permute-start | bytes 196616 | tf_op jit(solution)/shard_map/ppermute | solution.py:50
  108.3 1.3 collective-permute-start.33
  110.4 2.3 %collective-permute-start.21 = (bf16[256,128]{1,0:T(8,128)(2,1)S(1)}, bf16[256,128]{1,0:T(8,128)(2,1)S(1)}, u32[]{:S(2)}, u32[]{:S(2)}) collective-permute-start(bf16[256,128]{1,0:T(8,128)(2,1)S(1)} %get-tuple-element.53), channel_id=1, source_target_pairs={{0,4},{1,5},{2,6},{3,7},{4,0},{5,1},{6,2},{7,3},{8,12},{9,13},{10,... | collective-permute-start | bytes 196616 | tf_op jit(solution)/shard_map/ppermute | solution.py:50
  113.2 2.4 %collective-permute-start.22 = (bf16[256,128]{1,0:T(8,128)(2,1)S(1)}, bf16[256,128]{1,0:T(8,128)(2,1)S(1)}, u32[]{:S(2)}, u32[]{:S(2)}) collective-permute-start(bf16[256,128]{1,0:T(8,128)(2,1)S(1)} %get-tuple-element.53), channel_id=1, source_target_pairs={{0,6},{1,7},{2,4},{3,5},{4,2},{5,3},{6,0},{7,1},{8,14},{9,15},{10,... | collective-permute-start | bytes 196616 | tf_op jit(solution)/shard_map/ppermute | solution.py:50
  116.4 0.9 collective-permute-start.37
  117.4 1.7 %collective-permute-start.35 = (bf16[256,128]{1,0:T(8,128)(2,1)S(1)}, bf16[256,128]{1,0:T(8,128)(2,1)S(1)}, u32[]{:S(2)}, u32[]{:S(2)}) collective-permute-start(bf16[256,128]{1,0:T(8,128)(2,1)S(1)} %get-tuple-element.65), channel_id=1, source_target_pairs={{0,4},{1,5},{2,6},{3,7},{4,0},{5,1},{6,2},{7,3},{8,12},{9,13},{10,... | collective-permute-start | bytes 196616 | tf_op jit(solution)/shard_map/ppermute | solution.py:50
  119.1 2.8 %collective-permute-start.36 = (bf16[256,128]{1,0:T(8,128)(2,1)S(1)}, bf16[256,128]{1,0:T(8,128)(2,1)S(1)}, u32[]{:S(2)}, u32[]{:S(2)}) collective-permute-start(bf16[256,128]{1,0:T(8,128)(2,1)S(1)} %get-tuple-element.65), channel_id=1, source_target_pairs={{0,6},{1,7},{2,4},{3,5},{4,2},{5,3},{6,0},{7,1},{8,14},{9,15},{10,... | collective-permute-start | bytes 196616 | tf_op jit(solution)/shard_map/ppermute | solution.py:50
  121.9 1.8 %collective-permute-start.24 = (bf16[4,256,128]{2,1,0:T(8,128)(2,1)S(1)}, bf16[4,256,128]{2,1,0:T(8,128)(2,1)S(1)}, u32[]{:S(2)}, u32[]{:S(2)}) collective-permute-start(bf16[4,256,128]{2,1,0:T(8,128)(2,1)S(1)} %get-tuple-element.85), channel_id=1, source_target_pairs={{0,1},{1,0},{2,3},{3,2},{4,5},{5,4},{6,7},{7,6},{8,24},{9,25},{10,... | collective-permute-start | bytes 786440 | tf_op jit(solution)/shard_map/ppermute | solution.py:50
  123.7 1.5 collective-permute-done.36
  125.2 2.6 %collective-permute-start.38 = (bf16[4,256,128]{2,1,0:T(8,128)(2,1)S(1)}, bf16[4,256,128]{2,1,0:T(8,128)(2,1)S(1)}, u32[]{:S(2)}, u32[]{:S(2)}) collective-permute-start(bf16[4,256,128]{2,1,0:T(8,128)(2,1)S(1)} %get-tuple-element.80), channel_id=1, source_target_pairs={{0,1},{1,0},{2,3},{3,2},{4,5},{5,4},{6,7},{7,6},{8,24},{9,25},{10,... | collective-permute-start | bytes 786440 | tf_op jit(solution)/shard_map/ppermute | solution.py:50
  127.9 3.3 %collective-permute-done.24 = bf16[4,256,128]{2,1,0:T(8,128)(2,1)S(1)} collective-permute-done((bf16[4,256,128]{2,1,0:T(8,128)(2,1)S(1)}, bf16[4,256,128]{2,1,0:T(8,128)(2,1)S(1)}, u32[]{:S(2)}, u32[]{:S(2)}) %collective-permute-start.24) | collective-permute-done | bytes 262176 | tf_op jit(solution)/shard_map/ppermute | solution.py:50
  131.2 1.3 collective-permute-start.25
  132.5 4.3 %collective-permute-done.38 = bf16[4,256,128]{2,1,0:T(8,128)(2,1)S(1)} collective-permute-done((bf16[4,256,128]{2,1,0:T(8,128)(2,1)S(1)}, bf16[4,256,128]{2,1,0:T(8,128)(2,1)S(1)}, u32[]{:S(2)}, u32[]{:S(2)}) %collective-permute-start.38) | collective-permute-done | bytes 262176 | tf_op jit(solution)/shard_map/ppermute | solution.py:50
  136.9 1.3 collective-permute-start.39
  138.7 1.8 %collective-permute-done.25.refs_1_ = bf16[2,4,256,128]{3,2,1,0:T(8,128)(2,1)S(1)} collective-permute-done((bf16[2,4,256,128]{3,2,1,0:T(8,128)(2,1)S(1)}, bf16[2,4,256,128]{3,2,1,0:T(8,128)(2,1)S(1)}, u32[]{:S(2)}, u32[]{:S(2)}) %collective-permute-start.25) | collective-permute-done | bytes 524320 | tf_op jit(solution)/shard_map/ppermute | solution.py:50
  140.5 5.6 %collective-permute-done.39.refs_5_ = bf16[2,4,256,128]{3,2,1,0:T(8,128)(2,1)S(1)} collective-permute-done((bf16[2,4,256,128]{3,2,1,0:T(8,128)(2,1)S(1)}, bf16[2,4,256,128]{3,2,1,0:T(8,128)(2,1)S(1)}, u32[]{:S(2)}, u32[]{:S(2)}) %collective-permute-start.39) | collective-permute-done | bytes 524320 | tf_op jit(solution)/shard_map/ppermute | solution.py:50
  148.5 4.4 %assemble.1 = (bf16[2048,1024]{1,0:T(8,128)(2,1)}, f32[256,1024]{1,0:T(8,128)}) custom-call(s32[4]{0:T(128)S(1)} %pad_add_fusion.here_ref, bf16[2,4,256,128]{3,2,1,0:T(8,128)(2,1)S(1)} %pad_maximum_fusion.2.refs_0_, bf16[2,4,256,128]{3,2,1,0:T(8,128)(2,1)S(1)} %collective-permute-done.25.refs_1_, ...), custom_call_target="tpu_custom_call" | custom-call | tf_op jit(solution)/shard_map/assemble/pallas_call | solution.py:562
  (108 shorter events, 17.4 us)
Async XLA Ops:
  2.4 7.1 %collective-permute-start = (bf16[128,256]{1,0:T(8,128)(2,1)}, bf16[128,256]{1,0:T(8,128)(2,1)S(1)}, u32[]{:S(2)}, u32[]{:S(2)}) collective-permute-start(bf16[128,256]{1,0:T(8,128)(2,1)} %get-tuple-element.43), channel_id=1, source_target_pairs={{0,2},{1,3},{2,0},{3,1},{4,6},{5,7},{6,4},{7,5},{8,10},{9,11},{10,... | collective-permute-start | bytes 196616 | tf_op jit(solution)/shard_map/ppermute | solution.py:50
  5.5 19.6 %collective-permute-start.8 = (bf16[128,256]{1,0:T(8,128)(2,1)}, bf16[128,256]{1,0:T(8,128)(2,1)S(1)}, u32[]{:S(2)}, u32[]{:S(2)}) collective-permute-start(bf16[128,256]{1,0:T(8,128)(2,1)} %get-tuple-element.43), channel_id=1, source_target_pairs={{0,4},{1,5},{2,6},{3,7},{4,0},{5,1},{6,2},{7,3},{8,12},{9,13},{10,... | collective-permute-start | bytes 196616 | tf_op jit(solution)/shard_map/ppermute | solution.py:50
  8.1 17.0 %collective-permute-start.9 = (bf16[128,256]{1,0:T(8,128)(2,1)}, bf16[128,256]{1,0:T(8,128)(2,1)S(1)}, u32[]{:S(2)}, u32[]{:S(2)}) collective-permute-start(bf16[128,256]{1,0:T(8,128)(2,1)} %get-tuple-element.43), channel_id=1, source_target_pairs={{0,6},{1,7},{2,4},{3,5},{4,2},{5,3},{6,0},{7,1},{8,14},{9,15},{10,... | collective-permute-start | bytes 196616 | tf_op jit(solution)/shard_map/ppermute | solution.py:50
  20.7 30.6 %copy-start.13 = (s32[32,32]{1,0:T(8,128)S(1)}, s32[32,32]{1,0:T(8,128)}, u32[]{:S(2)}) copy-start(s32[32,32]{1,0:T(8,128)} %param.15) | copy-start | bytes 12292
  20.7 6.2 %collective-permute-start.1 = (bf16[144,256]{1,0:T(8,128)(2,1)S(1)}, bf16[144,256]{1,0:T(8,128)(2,1)S(1)}, u32[]{:S(2)}, u32[]{:S(2)}) collective-permute-start(bf16[144,256]{1,0:T(8,128)(2,1)S(1)} %get-tuple-element.41), channel_id=1, source_target_pairs={{0,2},{1,3},{2,0},{3,1},{4,6},{5,7},{6,4},{7,5},{8,10},{9,11},{10,... | collective-permute-start | bytes 221192 | tf_op jit(solution)/shard_map/ppermute | solution.py:50
  21.6 7.8 %collective-permute-start.2 = (bf16[144,256]{1,0:T(8,128)(2,1)S(1)}, bf16[144,256]{1,0:T(8,128)(2,1)S(1)}, u32[]{:S(2)}, u32[]{:S(2)}) collective-permute-start(bf16[144,256]{1,0:T(8,128)(2,1)S(1)} %get-tuple-element.41), channel_id=1, source_target_pairs={{0,4},{1,5},{2,6},{3,7},{4,0},{5,1},{6,2},{7,3},{8,12},{9,13},{10,... | collective-permute-start | bytes 221192 | tf_op jit(solution)/shard_map/ppermute | solution.py:50
  25.1 6.2 %collective-permute-start.3 = (bf16[144,256]{1,0:T(8,128)(2,1)S(1)}, bf16[144,256]{1,0:T(8,128)(2,1)S(1)}, u32[]{:S(2)}, u32[]{:S(2)}) collective-permute-start(bf16[144,256]{1,0:T(8,128)(2,1)S(1)} %get-tuple-element.41), channel_id=1, source_target_pairs={{0,6},{1,7},{2,4},{3,5},{4,2},{5,3},{6,0},{7,1},{8,14},{9,15},{10,... | collective-permute-start | bytes 221192 | tf_op jit(solution)/shard_map/ppermute | solution.py:50
  25.2 7.7 %collective-permute-start.10 = (bf16[4,128,256]{2,1,0:T(8,128)(2,1)S(1)}, bf16[4,128,256]{2,1,0:T(8,128)(2,1)S(1)}, u32[]{:S(2)}, u32[]{:S(2)}) collective-permute-start(bf16[4,128,256]{2,1,0:T(8,128)(2,1)S(1)} %get-tuple-element.90), channel_id=1, source_target_pairs={{0,1},{1,0},{2,3},{3,2},{4,5},{5,4},{6,7},{7,6},{8,24},{9,25},{10,... | collective-permute-start | bytes 786440 | tf_op jit(solution)/shard_map/ppermute | solution.py:50
  31.3 10.0 %collective-permute-start.4 = (bf16[4,144,256]{2,1,0:T(8,128)(2,1)S(1)}, bf16[4,144,256]{2,1,0:T(8,128)(2,1)S(1)}, u32[]{:S(2)}, u32[]{:S(2)}) collective-permute-start(bf16[4,144,256]{2,1,0:T(8,128)(2,1)S(1)} %get-tuple-element.78), channel_id=1, source_target_pairs={{0,1},{1,0},{2,3},{3,2},{4,5},{5,4},{6,7},{7,6},{8,24},{9,25},{10,... | collective-permute-start | bytes 884744 | tf_op jit(solution)/shard_map/ppermute | solution.py:50
  32.9 10.1 %collective-permute-start.11 = (bf16[2,4,128,256]{3,2,1,0:T(8,128)(2,1)S(1)}, bf16[2,4,128,256]{3,2,1,0:T(8,128)(2,1)}, u32[]{:S(2)}, u32[]{:S(2)}) collective-permute-start(bf16[2,4,128,256]{3,2,1,0:T(8,128)(2,1)S(1)} %pad_maximum_fusion.1.refs_0_), channel_id=1, source_target_pairs={{0,16},{1,17},{2,18},{3,19},{4,20},{5,21},{6,22},{7,23},{8,9},{9,8... | collective-permute-start | bytes 1572872 | tf_op jit(solution)/shard_map/ppermute | solution.py:50
  41.4 9.9 %collective-permute-start.5 = (bf16[2,4,144,256]{3,2,1,0:T(8,128)(2,1)S(1)}, bf16[2,4,144,256]{3,2,1,0:T(8,128)(2,1)S(1)}, u32[]{:S(2)}, u32[]{:S(2)}) collective-permute-start(bf16[2,4,144,256]{3,2,1,0:T(8,128)(2,1)S(1)} %pad_maximum_fusion.refs_0_), channel_id=1, source_target_pairs={{0,16},{1,17},{2,18},{3,19},{4,20},{5,21},{6,22},{7,23},{8,9},{9,8... | collective-permute-start | bytes 1769480 | tf_op jit(solution)/shard_map/ppermute | solution.py:50
  42.9 8.5 %collective-permute-start.12 = (bf16[2,4,128,256]{3,2,1,0:T(8,128)(2,1)S(1)}, bf16[2,4,128,256]{3,2,1,0:T(8,128)(2,1)}, u32[]{:S(2)}, u32[]{:S(2)}) collective-permute-start(bf16[2,4,128,256]{3,2,1,0:T(8,128)(2,1)S(1)} %pad_maximum_fusion.1.refs_0_), channel_id=1, source_target_pairs={{0,8},{1,9},{2,10},{3,11},{4,12},{5,13},{6,14},{7,15},{8,0},{9,1},... | collective-permute-start | bytes 1572872 | tf_op jit(solution)/shard_map/ppermute | solution.py:50
  43.0 8.5 %collective-permute-start.13 = (bf16[2,4,128,256]{3,2,1,0:T(8,128)(2,1)}, bf16[2,4,128,256]{3,2,1,0:T(8,128)(2,1)}, u32[]{:S(2)}, u32[]{:S(2)}) collective-permute-start(bf16[2,4,128,256]{3,2,1,0:T(8,128)(2,1)} %collective-permute-done.11.refs_1_), channel_id=1, source_target_pairs={{0,8},{1,9},{2,10},{3,11},{4,12},{5,13},{6,14},{7,15},{8,0},{9,1},... | collective-permute-start | bytes 1572872 | tf_op jit(solution)/shard_map/ppermute | solution.py:50
  43.5 15.3 %collective-permute-start.6 = (bf16[2,4,144,256]{3,2,1,0:T(8,128)(2,1)S(1)}, bf16[2,4,144,256]{3,2,1,0:T(8,128)(2,1)S(1)}, u32[]{:S(2)}, u32[]{:S(2)}) collective-permute-start(bf16[2,4,144,256]{3,2,1,0:T(8,128)(2,1)S(1)} %pad_maximum_fusion.refs_0_), channel_id=1, source_target_pairs={{0,8},{1,9},{2,10},{3,11},{4,12},{5,13},{6,14},{7,15},{8,0},{9,1},... | collective-permute-start | bytes 1769480 | tf_op jit(solution)/shard_map/ppermute | solution.py:50
  51.3 7.4 %collective-permute-start.7 = (bf16[2,4,144,256]{3,2,1,0:T(8,128)(2,1)S(1)}, bf16[2,4,144,256]{3,2,1,0:T(8,128)(2,1)S(1)}, u32[]{:S(2)}, u32[]{:S(2)}) collective-permute-start(bf16[2,4,144,256]{3,2,1,0:T(8,128)(2,1)S(1)} %collective-permute-done.5.refs_1_), channel_id=1, source_target_pairs={{0,8},{1,9},{2,10},{3,11},{4,12},{5,13},{6,14},{7,15},{8,0},{9,1},... | collective-permute-start | bytes 1769480 | tf_op jit(solution)/shard_map/ppermute | solution.py:50
  70.7 4.2 %collective-permute-start.14 = (bf16[2,2,4,128,256]{4,3,2,1,0:T(8,128)(2,1)S(1)}, bf16[2,2,4,128,256]{4,3,2,1,0:T(8,128)(2,1)S(1)}, u32[]{:S(2)}, u32[]{:S(2)}) collective-permute-start(bf16[2,2,4,128,256]{4,3,2,1,0:T(8,128)(2,1)S(1)} %get-tuple-element.50), channel_id=1, source_target_pairs={{0,8},{1,9},{2,10},{3,11},{4,12},{5,13},{6,14},{7,15},{8,0},{9,1},... | collective-permute-start | bytes 3145736 | tf_op jit(solution)/shard_map/ppermute | solution.py:50
  74.8 2.7 %collective-permute-start.28 = (bf16[2,2,4,128,256]{4,3,2,1,0:T(8,128)(2,1)S(1)}, bf16[2,2,4,128,256]{4,3,2,1,0:T(8,128)(2,1)S(1)}, u32[]{:S(2)}, u32[]{:S(2)}) collective-permute-start(bf16[2,2,4,128,256]{4,3,2,1,0:T(8,128)(2,1)S(1)} %get-tuple-element.59), channel_id=1, source_target_pairs={{0,8},{1,9},{2,10},{3,11},{4,12},{5,13},{6,14},{7,15},{8,0},{9,1},... | collective-permute-start | bytes 3145736 | tf_op jit(solution)/shard_map/ppermute | solution.py:50
  75.2 9.2 %collective-permute-start.15 = (bf16[2,4,128,256]{3,2,1,0:T(8,128)(2,1)S(1)}, bf16[2,4,128,256]{3,2,1,0:T(8,128)(2,1)S(1)}, u32[]{:S(2)}, u32[]{:S(2)}) collective-permute-start(bf16[2,4,128,256]{3,2,1,0:T(8,128)(2,1)S(1)} %fusion.2), channel_id=1, source_target_pairs={{0,16},{1,17},{2,18},{3,19},{4,20},{5,21},{6,22},{7,23},{8,9},{9,8... | collective-permute-start | bytes 1572872 | tf_op jit(solution)/shard_map/ppermute | solution.py:50
  77.9 15.0 %collective-permute-start.29 = (bf16[2,4,128,256]{3,2,1,0:T(8,128)(2,1)S(1)}, bf16[2,4,128,256]{3,2,1,0:T(8,128)(2,1)S(1)}, u32[]{:S(2)}, u32[]{:S(2)}) collective-permute-start(bf16[2,4,128,256]{3,2,1,0:T(8,128)(2,1)S(1)} %fusion.3), channel_id=1, source_target_pairs={{0,16},{1,17},{2,18},{3,19},{4,20},{5,21},{6,22},{7,23},{8,9},{9,8... | collective-permute-start | bytes 1572872 | tf_op jit(solution)/shard_map/ppermute | solution.py:50
  84.6 10.1 %collective-permute-start.16 = (bf16[4,128,256]{2,1,0:T(8,128)(2,1)S(1)}, bf16[4,128,256]{2,1,0:T(8,128)(2,1)S(1)}, u32[]{:S(2)}, u32[]{:S(2)}) collective-permute-start(bf16[4,128,256]{2,1,0:T(8,128)(2,1)S(1)} %fusion.6), channel_id=1, source_target_pairs={{0,1},{1,0},{2,3},{3,2},{4,5},{5,4},{6,7},{7,6},{8,24},{9,25},{10,... | collective-permute-start | bytes 786440 | tf_op jit(solution)/shard_map/ppermute | solution.py:50
  93.0 9.8 %copy-start = (f32[256,1024]{1,0:T(8,128)S(1)}, f32[256,1024]{1,0:T(8,128)}, u32[]{:S(2)}) copy-start(f32[256,1024]{1,0:T(8,128)} %refs_3_.3) | copy-start | bytes 3145732
  93.0 9.8 %copy-start.2 = (f32[256,1024]{1,0:T(8,128)S(1)}, f32[256,1024]{1,0:T(8,128)}, u32[]{:S(2)}) copy-start(f32[256,1024]{1,0:T(8,128)} %refs_4_.3) | copy-start | bytes 3145732
  93.0 9.7 %copy-start.3 = (f32[256,1024]{1,0:T(8,128)S(1)}, f32[256,1024]{1,0:T(8,128)}, u32[]{:S(2)}) copy-start(f32[256,1024]{1,0:T(8,128)} %refs_5_.3) | copy-start | bytes 3145732
  93.1 6.4 %collective-permute-start.30 = (bf16[4,128,256]{2,1,0:T(8,128)(2,1)S(1)}, bf16[4,128,256]{2,1,0:T(8,128)(2,1)S(1)}, u32[]{:S(2)}, u32[]{:S(2)}) collective-permute-start(bf16[4,128,256]{2,1,0:T(8,128)(2,1)S(1)} %fusion.7), channel_id=1, source_target_pairs={{0,1},{1,0},{2,3},{3,2},{4,5},{5,4},{6,7},{7,6},{8,24},{9,25},{10,... | collective-permute-start | bytes 786440 | tf_op jit(solution)/shard_map/ppermute | solution.py:50
  94.7 5.7 %collective-permute-start.17 = (bf16[128,256]{1,0:T(8,128)(2,1)S(1)}, bf16[128,256]{1,0:T(8,128)(2,1)S(1)}, u32[]{:S(2)}, u32[]{:S(2)}) collective-permute-start(bf16[128,256]{1,0:T(8,128)(2,1)S(1)} %get-tuple-element.88), channel_id=1, source_target_pairs={{0,2},{1,3},{2,0},{3,1},{4,6},{5,7},{6,4},{7,5},{8,10},{9,11},{10,... | collective-permute-start | bytes 196616 | tf_op jit(solution)/shard_map/ppermute | solution.py:50
  94.8 5.7 %collective-permute-start.18 = (bf16[128,256]{1,0:T(8,128)(2,1)S(1)}, bf16[128,256]{1,0:T(8,128)(2,1)S(1)}, u32[]{:S(2)}, u32[]{:S(2)}) collective-permute-start(bf16[128,256]{1,0:T(8,128)(2,1)S(1)} %get-tuple-element.87), channel_id=1, source_target_pairs={{0,4},{1,5},{2,6},{3,7},{4,0},{5,1},{6,2},{7,3},{8,12},{9,13},{10,... | collective-permute-start | bytes 196616 | tf_op jit(solution)/shard_map/ppermute | solution.py:50
  96.6 6.2 %collective-permute-start.19 = (bf16[128,256]{1,0:T(8,128)(2,1)S(1)}, bf16[128,256]{1,0:T(8,128)(2,1)S(1)}, u32[]{:S(2)}, u32[]{:S(2)}) collective-permute-start(bf16[128,256]{1,0:T(8,128)(2,1)S(1)} %get-tuple-element.86), channel_id=1, source_target_pairs={{0,6},{1,7},{2,4},{3,5},{4,2},{5,3},{6,0},{7,1},{8,14},{9,15},{10,... | collective-permute-start | bytes 196616 | tf_op jit(solution)/shard_map/ppermute | solution.py:50
  103.6 13.7 %collective-permute-start.23 = (f32[256,128]{1,0:T(8,128)S(1)}, f32[256,128]{1,0:T(8,128)S(1)}, u32[]{:S(2)}, u32[]{:S(2)}) collective-permute-start(f32[256,128]{1,0:T(8,128)S(1)} %get-tuple-element.52), channel_id=1, source_target_pairs={{0,16},{1,17},{2,18},{3,19},{4,20},{5,21},{6,22},{7,23},{8,24},{9,... | collective-permute-start | bytes 393224 | tf_op jit(solution)/shard_map/ppermute | solution.py:50
  105.2 5.2 %collective-permute-start.31 = (bf16[128,256]{1,0:T(8,128)(2,1)S(1)}, bf16[128,256]{1,0:T(8,128)(2,1)S(1)}, u32[]{:S(2)}, u32[]{:S(2)}) collective-permute-start(bf16[128,256]{1,0:T(8,128)(2,1)S(1)} %get-tuple-element.60), channel_id=1, source_target_pairs={{0,2},{1,3},{2,0},{3,1},{4,6},{5,7},{6,4},{7,5},{8,10},{9,11},{10,... | collective-permute-start | bytes 196616 | tf_op jit(solution)/shard_map/ppermute | solution.py:50
  105.9 7.3 %collective-permute-start.32 = (bf16[128,256]{1,0:T(8,128)(2,1)S(1)}, bf16[128,256]{1,0:T(8,128)(2,1)S(1)}, u32[]{:S(2)}, u32[]{:S(2)}) collective-permute-start(bf16[128,256]{1,0:T(8,128)(2,1)S(1)} %get-tuple-element.61), channel_id=1, source_target_pairs={{0,4},{1,5},{2,6},{3,7},{4,0},{5,1},{6,2},{7,3},{8,12},{9,13},{10,... | collective-permute-start | bytes 196616 | tf_op jit(solution)/shard_map/ppermute | solution.py:50
  108.3 7.3 %collective-permute-start.33 = (bf16[128,256]{1,0:T(8,128)(2,1)S(1)}, bf16[128,256]{1,0:T(8,128)(2,1)S(1)}, u32[]{:S(2)}, u32[]{:S(2)}) collective-permute-start(bf16[128,256]{1,0:T(8,128)(2,1)S(1)} %get-tuple-element.62), channel_id=1, source_target_pairs={{0,6},{1,7},{2,4},{3,5},{4,2},{5,3},{6,0},{7,1},{8,14},{9,15},{10,... | collective-permute-start | bytes 196616 | tf_op jit(solution)/shard_map/ppermute | solution.py:50
  109.6 7.7 %collective-permute-start.20 = (bf16[256,128]{1,0:T(8,128)(2,1)S(1)}, bf16[256,128]{1,0:T(8,128)(2,1)S(1)}, u32[]{:S(2)}, u32[]{:S(2)}) collective-permute-start(bf16[256,128]{1,0:T(8,128)(2,1)S(1)} %get-tuple-element.53), channel_id=1, source_target_pairs={{0,2},{1,3},{2,0},{3,1},{4,6},{5,7},{6,4},{7,5},{8,10},{9,11},{10,... | collective-permute-start | bytes 196616 | tf_op jit(solution)/shard_map/ppermute | solution.py:50
  110.4 8.7 %collective-permute-start.21 = (bf16[256,128]{1,0:T(8,128)(2,1)S(1)}, bf16[256,128]{1,0:T(8,128)(2,1)S(1)}, u32[]{:S(2)}, u32[]{:S(2)}) collective-permute-start(bf16[256,128]{1,0:T(8,128)(2,1)S(1)} %get-tuple-element.53), channel_id=1, source_target_pairs={{0,4},{1,5},{2,6},{3,7},{4,0},{5,1},{6,2},{7,3},{8,12},{9,13},{10,... | collective-permute-start | bytes 196616 | tf_op jit(solution)/shard_map/ppermute | solution.py:50
  113.2 8.6 %collective-permute-start.22 = (bf16[256,128]{1,0:T(8,128)(2,1)S(1)}, bf16[256,128]{1,0:T(8,128)(2,1)S(1)}, u32[]{:S(2)}, u32[]{:S(2)}) collective-permute-start(bf16[256,128]{1,0:T(8,128)(2,1)S(1)} %get-tuple-element.53), channel_id=1, source_target_pairs={{0,6},{1,7},{2,4},{3,5},{4,2},{5,3},{6,0},{7,1},{8,14},{9,15},{10,... | collective-permute-start | bytes 196616 | tf_op jit(solution)/shard_map/ppermute | solution.py:50
  116.4 7.3 %collective-permute-start.37 = (f32[256,128]{1,0:T(8,128)S(1)}, f32[256,128]{1,0:T(8,128)S(1)}, u32[]{:S(2)}, u32[]{:S(2)}) collective-permute-start(f32[256,128]{1,0:T(8,128)S(1)} %get-tuple-element.64), channel_id=1, source_target_pairs={{0,16},{1,17},{2,18},{3,19},{4,20},{5,21},{6,22},{7,23},{8,24},{9,... | collective-permute-start | bytes 393224 | tf_op jit(solution)/shard_map/ppermute | solution.py:50
  117.3 6.4 %collective-permute-start.34 = (bf16[256,128]{1,0:T(8,128)(2,1)S(1)}, bf16[256,128]{1,0:T(8,128)(2,1)S(1)}, u32[]{:S(2)}, u32[]{:S(2)}) collective-permute-start(bf16[256,128]{1,0:T(8,128)(2,1)S(1)} %get-tuple-element.65), channel_id=1, source_target_pairs={{0,2},{1,3},{2,0},{3,1},{4,6},{5,7},{6,4},{7,5},{8,10},{9,11},{10,... | collective-permute-start | bytes 196616 | tf_op jit(solution)/shard_map/ppermute | solution.py:50
  117.4 6.3 %collective-permute-start.35 = (bf16[256,128]{1,0:T(8,128)(2,1)S(1)}, bf16[256,128]{1,0:T(8,128)(2,1)S(1)}, u32[]{:S(2)}, u32[]{:S(2)}) collective-permute-start(bf16[256,128]{1,0:T(8,128)(2,1)S(1)} %get-tuple-element.65), channel_id=1, source_target_pairs={{0,4},{1,5},{2,6},{3,7},{4,0},{5,1},{6,2},{7,3},{8,12},{9,13},{10,... | collective-permute-start | bytes 196616 | tf_op jit(solution)/shard_map/ppermute | solution.py:50
  119.1 6.1 %collective-permute-start.36 = (bf16[256,128]{1,0:T(8,128)(2,1)S(1)}, bf16[256,128]{1,0:T(8,128)(2,1)S(1)}, u32[]{:S(2)}, u32[]{:S(2)}) collective-permute-start(bf16[256,128]{1,0:T(8,128)(2,1)S(1)} %get-tuple-element.65), channel_id=1, source_target_pairs={{0,6},{1,7},{2,4},{3,5},{4,2},{5,3},{6,0},{7,1},{8,14},{9,15},{10,... | collective-permute-start | bytes 196616 | tf_op jit(solution)/shard_map/ppermute | solution.py:50
  121.9 9.3 %collective-permute-start.24 = (bf16[4,256,128]{2,1,0:T(8,128)(2,1)S(1)}, bf16[4,256,128]{2,1,0:T(8,128)(2,1)S(1)}, u32[]{:S(2)}, u32[]{:S(2)}) collective-permute-start(bf16[4,256,128]{2,1,0:T(8,128)(2,1)S(1)} %get-tuple-element.85), channel_id=1, source_target_pairs={{0,1},{1,0},{2,3},{3,2},{4,5},{5,4},{6,7},{7,6},{8,24},{9,25},{10,... | collective-permute-start | bytes 786440 | tf_op jit(solution)/shard_map/ppermute | solution.py:50
  125.2 11.6 %collective-permute-start.38 = (bf16[4,256,128]{2,1,0:T(8,128)(2,1)S(1)}, bf16[4,256,128]{2,1,0:T(8,128)(2,1)S(1)}, u32[]{:S(2)}, u32[]{:S(2)}) collective-permute-start(bf16[4,256,128]{2,1,0:T(8,128)(2,1)S(1)} %get-tuple-element.80), channel_id=1, source_target_pairs={{0,1},{1,0},{2,3},{3,2},{4,5},{5,4},{6,7},{7,6},{8,24},{9,25},{10,... | collective-permute-start | bytes 786440 | tf_op jit(solution)/shard_map/ppermute | solution.py:50
  131.2 9.2 %collective-permute-start.25 = (bf16[2,4,256,128]{3,2,1,0:T(8,128)(2,1)S(1)}, bf16[2,4,256,128]{3,2,1,0:T(8,128)(2,1)S(1)}, u32[]{:S(2)}, u32[]{:S(2)}) collective-permute-start(bf16[2,4,256,128]{3,2,1,0:T(8,128)(2,1)S(1)} %pad_maximum_fusion.2.refs_0_), channel_id=1, source_target_pairs={{0,16},{1,17},{2,18},{3,19},{4,20},{5,21},{6,22},{7,23},{8,9},{9,8... | collective-permute-start | bytes 1572872 | tf_op jit(solution)/shard_map/ppermute | solution.py:50
  136.9 9.2 %collective-permute-start.39 = (bf16[2,4,256,128]{3,2,1,0:T(8,128)(2,1)S(1)}, bf16[2,4,256,128]{3,2,1,0:T(8,128)(2,1)S(1)}, u32[]{:S(2)}, u32[]{:S(2)}) collective-permute-start(bf16[2,4,256,128]{3,2,1,0:T(8,128)(2,1)S(1)} %pad_maximum_fusion.3.refs_4_), channel_id=1, source_target_pairs={{0,16},{1,17},{2,18},{3,19},{4,20},{5,21},{6,22},{7,23},{8,9},{9,8... | collective-permute-start | bytes 1572872 | tf_op jit(solution)/shard_map/ppermute | solution.py:50
  138.1 8.0 %collective-permute-start.42 = (f32[2,256,128]{2,1,0:T(8,128)S(1)}, f32[2,256,128]{2,1,0:T(8,128)S(1)}, u32[]{:S(2)}, u32[]{:S(2)}) collective-permute-start(f32[2,256,128]{2,1,0:T(8,128)S(1)} %pad_maximum_fusion.6.refs_8_), channel_id=1, source_target_pairs={{0,8},{1,9},{2,10},{3,11},{4,12},{5,13},{6,14},{7,15},{8,0},{9,1},... | collective-permute-start | bytes 786440 | tf_op jit(solution)/shard_map/ppermute | solution.py:50
  138.1 10.4 %collective-permute-start.26 = (bf16[2,4,256,128]{3,2,1,0:T(8,128)(2,1)S(1)}, bf16[2,4,256,128]{3,2,1,0:T(8,128)(2,1)S(1)}, u32[]{:S(2)}, u32[]{:S(2)}) collective-permute-start(bf16[2,4,256,128]{3,2,1,0:T(8,128)(2,1)S(1)} %pad_maximum_fusion.2.refs_0_), channel_id=1, source_target_pairs={{0,8},{1,9},{2,10},{3,11},{4,12},{5,13},{6,14},{7,15},{8,0},{9,1},... | collective-permute-start | bytes 1572872 | tf_op jit(solution)/shard_map/ppermute | solution.py:50
  138.7 9.9 %collective-permute-start.40 = (bf16[2,4,256,128]{3,2,1,0:T(8,128)(2,1)S(1)}, bf16[2,4,256,128]{3,2,1,0:T(8,128)(2,1)}, u32[]{:S(2)}, u32[]{:S(2)}) collective-permute-start(bf16[2,4,256,128]{3,2,1,0:T(8,128)(2,1)S(1)} %pad_maximum_fusion.3.refs_4_), channel_id=1, source_target_pairs={{0,8},{1,9},{2,10},{3,11},{4,12},{5,13},{6,14},{7,15},{8,0},{9,1},... | collective-permute-start | bytes 1572872 | tf_op jit(solution)/shard_map/ppermute | solution.py:50
  140.5 8.0 %collective-permute-start.27 = (bf16[2,4,256,128]{3,2,1,0:T(8,128)(2,1)S(1)}, bf16[2,4,256,128]{3,2,1,0:T(8,128)(2,1)}, u32[]{:S(2)}, u32[]{:S(2)}) collective-permute-start(bf16[2,4,256,128]{3,2,1,0:T(8,128)(2,1)S(1)} %collective-permute-done.25.refs_1_), channel_id=1, source_target_pairs={{0,8},{1,9},{2,10},{3,11},{4,12},{5,13},{6,14},{7,15},{8,0},{9,1},... | collective-permute-start | bytes 1572872 | tf_op jit(solution)/shard_map/ppermute | solution.py:50
  146.1 2.4 %collective-permute-start.41 = (bf16[2,4,256,128]{3,2,1,0:T(8,128)(2,1)S(1)}, bf16[2,4,256,128]{3,2,1,0:T(8,128)(2,1)}, u32[]{:S(2)}, u32[]{:S(2)}) collective-permute-start(bf16[2,4,256,128]{3,2,1,0:T(8,128)(2,1)S(1)} %collective-permute-done.39.refs_5_), channel_id=1, source_target_pairs={{0,8},{1,9},{2,10},{3,11},{4,12},{5,13},{6,14},{7,15},{8,0},{9,1},... | collective-permute-start | bytes 1572872 | tf_op jit(solution)/shard_map/ppermute | solution.py:50
  146.1 2.4 %collective-permute-start.43 = (f32[2,256,128]{2,1,0:T(8,128)S(1)}, f32[2,256,128]{2,1,0:T(8,128)}, u32[]{:S(2)}, u32[]{:S(2)}) collective-permute-start(f32[2,256,128]{2,1,0:T(8,128)S(1)} %pad_maximum_fusion.8.refs_10_), channel_id=1, source_target_pairs={{0,8},{1,9},{2,10},{3,11},{4,12},{5,13},{6,14},{7,15},{8,0},{9,1},... | collective-permute-start | bytes 786440 | tf_op jit(solution)/shard_map/ppermute | solution.py:50
  (10 other events, 20.9 us)

commit v4 on v3

--- a/solution.py
+++ b/solution.py
@@ -454,8 +454,8 @@
         ],
         compiler_params=ROOM,
         cost_estimate=pl.CostEstimate(
-            flops=2 * tokens * width * rows,
-            bytes_accessed=2 * tokens * width + 2 * width * rows + 4 * tokens * rows,
+            flops=8 * 2 * tokens * width * rows,
+            bytes_accessed=1 * 2 * tokens * width + 2 * width * rows + 4 * tokens * rows,
             transcendentals=0,
         ),
         name="logits",

time: 153 us -> 150 us (0.980)
  starting transfers between devices: 52.6 us -> 47 us
  waiting for transfers between devices: 53.2 us -> 57.1 us
  local copies, waits for them, and re-layouts: 14.3 us -> 12.4 us
    ppermute x44, starting transfers between devices: 52.6 us -> 47 us  [permute(): return lax.ppermute(value, ALL, pairs)]
    ppermute x44, waiting for transfers between devices: 53.2 us -> 57.1 us  [permute(): return lax.ppermute(value, ALL, pairs)]
    unnamed x28 -> x24, local copies, waits for them, and re-layouts: 11.2 us -> 9.35 us
  transfers between devices with their start and end apart: 44 -> 44, of which waited for: 18 -> 21; matrix products, arithmetic and copies ran while one was open for 3% -> 3% of each run, Pallas kernels for 8% -> 8%
where the time goes in v4:
time: 150 us; the launch traced here: 149 us
  waiting for transfers between devices  57.1 us (38%)
  starting transfers between devices  47 us (31%)
  Pallas kernels  29.3 us (20%)
  local copies, waits for them, and re-layouts  12.4 us (8%)
  other arithmetic  2.1 us (1%)
    ppermute x44, waiting for transfers between devices, permute(): return lax.ppermute(value, ALL, pairs)  57.1 us
    ppermute x44, starting transfers between devices, permute(): return lax.ppermute(value, ALL, pairs)  47 us
    pallas_call x1, Pallas kernels, signal_and_gradient(): pl.pallas_call(functools.partial(signal_kernel, plan, segs, samples, tota...  10.1 us
    unnamed x24, local copies, waits for them, and re-layouts  9.35 us
    pallas_call x1, Pallas kernels, early_logits(): pl.pallas_call(functools.partial(logits_kernel, plan), in_specs=[SMEM] +...  4.73 us
    pallas_call x1, Pallas kernels, assemble(): pl.pallas_call(functools.partial(assemble_kernel, plan), in_specs=[SMEM]...  4.36 us
    pallas_call x1, Pallas kernels, signal_and_gradient(): pl.pallas_call(functools.partial(gradient_kernel, plan), in_specs=[SMEM,...  3.5 us
    pallas_call x1, Pallas kernels, normalize(): pl.pallas_call(norm_kernel, grid=(tokens // tile,), in_specs=[pl.BlockSpe...  3.26 us
  transfers between devices with their start and end apart: 44, of which 21 were waited for; matrix products, arithmetic and copies ran while one was open for 3% of the time, Pallas kernels for 8%

profile of v4, /device:TPU:0, one launch (start us, length us, event | category | flops | bytes accessed | tf_op | source)
XLA Modules:
  0.0 149.0 jit_solution(18339694842196777156)
XLA Ops:
  0.7 1.8 %shard.1 = (bf16[128,256]{1,0:T(8,128)(2,1)}, bf16[128,256]{1,0:T(8,128)(2,1)}) custom-call(s32[1]{0:T(128)} %bitcast.5.place_ref, f32[256,1024]{1,0:T(8,128)} %refs_3_.3), custom_call_target="tpu_custom_call" | custom-call | tf_op jit(solution)/shard_map/shard/pallas_call | solution.py:107
  2.4 3.1 %collective-permute-start = (bf16[128,256]{1,0:T(8,128)(2,1)}, bf16[128,256]{1,0:T(8,128)(2,1)S(1)}, u32[]{:S(2)}, u32[]{:S(2)}) collective-permute-start(bf16[128,256]{1,0:T(8,128)(2,1)} %get-tuple-element.43), channel_id=1, source_target_pairs={{0,2},{1,3},{2,0},{3,1},{4,6},{5,7},{6,4},{7,5},{8,10},{9,11},{10,... | collective-permute-start | bytes 196616 | tf_op jit(solution)/shard_map/ppermute | solution.py:50
  5.5 2.6 %collective-permute-start.8 = (bf16[128,256]{1,0:T(8,128)(2,1)}, bf16[128,256]{1,0:T(8,128)(2,1)S(1)}, u32[]{:S(2)}, u32[]{:S(2)}) collective-permute-start(bf16[128,256]{1,0:T(8,128)(2,1)} %get-tuple-element.43), channel_id=1, source_target_pairs={{0,4},{1,5},{2,6},{3,7},{4,0},{5,1},{6,2},{7,3},{8,12},{9,13},{10,... | collective-permute-start | bytes 196616 | tf_op jit(solution)/shard_map/ppermute | solution.py:50
  10.3 2.2 %copy-done.1 = bf16[32,32,2048]{2,1,0:T(8,128)(2,1)S(1)} copy-done((bf16[32,32,2048]{2,1,0:T(8,128)(2,1)S(1)}, bf16[32,32,2048]{2,1,0:T(8,128)(2,1)}, u32[]{:S(2)}) %copy-start.1) | copy-done | bytes 4194328
  15.4 3.3 %normalize.1 = (bf16[1024,2048]{1,0:T(8,128)(2,1)S(1)}, bf16[144,256]{1,0:T(8,128)(2,1)S(1)}) custom-call(bf16[1024,2048]{1,0:T(8,128)(2,1)S(1)} %bitcast.86, f32[1,2048]{1,0:T(1,128)S(1)} %bitcast.92, bf16[16,2048]{1,0:T(8,128)(2,1)S(1)} %broadcast_in_dim.12.value_ref, bf16[32,32]{1,0:T(8,128)(2,1)S(1)} %copy-done.7, s32[32,32]{1,0:T(8,128)S(1)} %copy-done.5, ...), custom_call_target="tpu_custom_call" | custom-call | flops 20971520 | bytes 8388608 | tf_op jit(solution)/shard_map/normalize/pallas_call | solution.py:212
  18.7 2.0 %copy-done.8 = bf16[1024,2048]{1,0:T(8,128)(2,1)} copy-done((bf16[1024,2048]{1,0:T(8,128)(2,1)}, bf16[1024,2048]{1,0:T(8,128)(2,1)S(1)}, u32[]{:S(2)}) %copy-start.8) | copy-done | bytes 4194328
  20.8 1.8 %collective-permute-start.10 = (bf16[4,128,256]{2,1,0:T(8,128)(2,1)S(1)}, bf16[4,128,256]{2,1,0:T(8,128)(2,1)S(1)}, u32[]{:S(2)}, u32[]{:S(2)}) collective-permute-start(bf16[4,128,256]{2,1,0:T(8,128)(2,1)S(1)} %get-tuple-element.90), channel_id=1, source_target_pairs={{0,1},{1,0},{2,3},{3,2},{4,5},{5,4},{6,7},{7,6},{8,24},{9,25},{10,... | collective-permute-start | bytes 786440 | tf_op jit(solution)/shard_map/ppermute | solution.py:50
  23.2 3.5 %collective-permute-start.2 = (bf16[144,256]{1,0:T(8,128)(2,1)S(1)}, bf16[144,256]{1,0:T(8,128)(2,1)S(1)}, u32[]{:S(2)}, u32[]{:S(2)}) collective-permute-start(bf16[144,256]{1,0:T(8,128)(2,1)S(1)} %get-tuple-element.41), channel_id=1, source_target_pairs={{0,4},{1,5},{2,6},{3,7},{4,0},{5,1},{6,2},{7,3},{8,12},{9,13},{10,... | collective-permute-start | bytes 221192 | tf_op jit(solution)/shard_map/ppermute | solution.py:50
  27.4 1.7 %collective-permute-start.11 = (bf16[2,4,128,256]{3,2,1,0:T(8,128)(2,1)S(1)}, bf16[2,4,128,256]{3,2,1,0:T(8,128)(2,1)S(1)}, u32[]{:S(2)}, u32[]{:S(2)}) collective-permute-start(bf16[2,4,128,256]{3,2,1,0:T(8,128)(2,1)S(1)} %pad_maximum_fusion.1.refs_0_), channel_id=1, source_target_pairs={{0,16},{1,17},{2,18},{3,19},{4,20},{5,21},{6,22},{7,23},{8,9},{9,8... | collective-permute-start | bytes 1572872 | tf_op jit(solution)/shard_map/ppermute | solution.py:50
  29.1 1.7 %collective-permute-done.2 = bf16[144,256]{1,0:T(8,128)(2,1)S(1)} collective-permute-done((bf16[144,256]{1,0:T(8,128)(2,1)S(1)}, bf16[144,256]{1,0:T(8,128)(2,1)S(1)}, u32[]{:S(2)}, u32[]{:S(2)}) %collective-permute-start.2) | collective-permute-done | bytes 73760 | tf_op jit(solution)/shard_map/ppermute | solution.py:50
  30.8 2.1 %collective-permute-done.3 = bf16[144,256]{1,0:T(8,128)(2,1)S(1)} collective-permute-done((bf16[144,256]{1,0:T(8,128)(2,1)S(1)}, bf16[144,256]{1,0:T(8,128)(2,1)S(1)}, u32[]{:S(2)}, u32[]{:S(2)}) %collective-permute-start.3) | collective-permute-done | bytes 73760 | tf_op jit(solution)/shard_map/ppermute | solution.py:50
  33.6 6.1 %collective-permute-done.4 = bf16[4,144,256]{2,1,0:T(8,128)(2,1)S(1)} collective-permute-done((bf16[4,144,256]{2,1,0:T(8,128)(2,1)S(1)}, bf16[4,144,256]{2,1,0:T(8,128)(2,1)S(1)}, u32[]{:S(2)}, u32[]{:S(2)}) %collective-permute-start.4) | collective-permute-done | bytes 294944 | tf_op jit(solution)/shard_map/ppermute | solution.py:50
  39.8 1.6 %collective-permute-start.5 = (bf16[2,4,144,256]{3,2,1,0:T(8,128)(2,1)S(1)}, bf16[2,4,144,256]{3,2,1,0:T(8,128)(2,1)S(1)}, u32[]{:S(2)}, u32[]{:S(2)}) collective-permute-start(bf16[2,4,144,256]{3,2,1,0:T(8,128)(2,1)S(1)} %pad_maximum_fusion.refs_0_), channel_id=1, source_target_pairs={{0,16},{1,17},{2,18},{3,19},{4,20},{5,21},{6,22},{7,23},{8,9},{9,8... | collective-permute-start | bytes 1769480 | tf_op jit(solution)/shard_map/ppermute | solution.py:50
  42.0 7.7 %collective-permute-done.5.refs_1_ = bf16[2,4,144,256]{3,2,1,0:T(8,128)(2,1)S(1)} collective-permute-done((bf16[2,4,144,256]{3,2,1,0:T(8,128)(2,1)S(1)}, bf16[2,4,144,256]{3,2,1,0:T(8,128)(2,1)S(1)}, u32[]{:S(2)}, u32[]{:S(2)}) %collective-permute-start.5) | collective-permute-done | bytes 589856 | tf_op jit(solution)/shard_map/ppermute | solution.py:50
  49.7 2.2 %copy-done.9 = bf16[1024,2048]{1,0:T(8,128)(2,1)S(1)} copy-done((bf16[1024,2048]{1,0:T(8,128)(2,1)S(1)}, bf16[1024,2048]{1,0:T(8,128)(2,1)}, u32[]{:S(2)}) %copy-start.9) | copy-done | bytes 4194328
  51.9 4.7 %logits.1 = (f32[4,512,256]{2,1,0:T(8,128)S(1)}, f32[4,1,256]{2,1,0:T(1,128)S(1)}) custom-call(s32[4]{0:T(128)S(1)} %pad_add_fusion.here_ref, bf16[2,4,128,256]{3,2,1,0:T(8,128)(2,1)S(1)} %pad_maximum_fusion.1.refs_0_, bf16[2,4,128,256]{3,2,1,0:T(8,128)(2,1)S(1)} %collective-permute-done.11.refs_1_, ...), custom_call_target="tpu_custom_call" | custom-call | flops 17179869184 | bytes 8388608 | tf_op jit(solution)/shard_map/logits/pallas_call | solution.py:443
  56.7 10.1 %signal.1 = (f32[1,1]{1,0:T(1,128)}, f32[4,1024]{1,0:T(4,128)S(1)}, bf16[512,1024]{1,0:T(8,128)(2,1)S(1)}, f32[2,2,4,128,256]{4,3,2,1,0:T(8,128)S(1)}, bf16[2,2,4,128,256]{4,3,2,1,0:T(8,128)(2,1)S(1)}) custom-call(s32[4]{0:T(128)S(1)} %pad_add_fusion.here_ref, s32[1,1024]{1,0:T(1,128)S(1)} %reshape.36.act_ref, ...), custom_call_target="tpu_custom_call" | custom-call | flops 4294967296 | bytes 14680064 | tf_op jit(solution)/shard_map/signal/pallas_call | solution.py:472
  67.4 3.5 %gradient.1 = (f32[2,2,4,128,256]{4,3,2,1,0:T(8,128)S(1)}, bf16[2,2,4,128,256]{4,3,2,1,0:T(8,128)(2,1)S(1)}) custom-call(s32[4]{0:T(128)S(1)} %pad_add_fusion.here_ref, bf16[512,1024]{1,0:T(8,128)(2,1)S(1)} %get-tuple-element.57.sig_ref, bf16[1024,2048]{1,0:T(8,128)(2,1)S(1)} %copy-done.9), custom_call_target="tpu_custom_call" | custom-call | flops 2147483648 | bytes 6291456 | tf_op jit(solution)/shard_map/gradient/pallas_call | solution.py:502
  71.2 1.6 %collective-permute-start.15 = (bf16[2,4,128,256]{3,2,1,0:T(8,128)(2,1)S(1)}, bf16[2,4,128,256]{3,2,1,0:T(8,128)(2,1)S(1)}, u32[]{:S(2)}, u32[]{:S(2)}) collective-permute-start(bf16[2,4,128,256]{3,2,1,0:T(8,128)(2,1)S(1)} %fusion.2), channel_id=1, source_target_pairs={{0,16},{1,17},{2,18},{3,19},{4,20},{5,21},{6,22},{7,23},{8,9},{9,8... | collective-permute-start | bytes 1572872 | tf_op jit(solution)/shard_map/ppermute | solution.py:50
  73.9 1.6 %collective-permute-start.29 = (bf16[2,4,128,256]{3,2,1,0:T(8,128)(2,1)S(1)}, bf16[2,4,128,256]{3,2,1,0:T(8,128)(2,1)S(1)}, u32[]{:S(2)}, u32[]{:S(2)}) collective-permute-start(bf16[2,4,128,256]{3,2,1,0:T(8,128)(2,1)S(1)} %fusion.3), channel_id=1, source_target_pairs={{0,16},{1,17},{2,18},{3,19},{4,20},{5,21},{6,22},{7,23},{8,9},{9,8... | collective-permute-start | bytes 1572872 | tf_op jit(solution)/shard_map/ppermute | solution.py:50
  75.5 5.0 %collective-permute-done.15 = bf16[2,4,128,256]{3,2,1,0:T(8,128)(2,1)S(1)} collective-permute-done((bf16[2,4,128,256]{3,2,1,0:T(8,128)(2,1)S(1)}, bf16[2,4,128,256]{3,2,1,0:T(8,128)(2,1)S(1)}, u32[]{:S(2)}, u32[]{:S(2)}) %collective-permute-start.15) | collective-permute-done | bytes 524320 | tf_op jit(solution)/shard_map/ppermute | solution.py:50
  81.4 7.6 %collective-permute-done.29 = bf16[2,4,128,256]{3,2,1,0:T(8,128)(2,1)S(1)} collective-permute-done((bf16[2,4,128,256]{3,2,1,0:T(8,128)(2,1)S(1)}, bf16[2,4,128,256]{3,2,1,0:T(8,128)(2,1)S(1)}, u32[]{:S(2)}, u32[]{:S(2)}) %collective-permute-start.29) | collective-permute-done | bytes 524320 | tf_op jit(solution)/shard_map/ppermute | solution.py:50
  90.0 1.0 collective-permute-start.17
  90.9 1.6 %collective-permute-start.18 = (bf16[128,256]{1,0:T(8,128)(2,1)S(1)}, bf16[128,256]{1,0:T(8,128)(2,1)S(1)}, u32[]{:S(2)}, u32[]{:S(2)}) collective-permute-start(bf16[128,256]{1,0:T(8,128)(2,1)S(1)} %get-tuple-element.87), channel_id=1, source_target_pairs={{0,4},{1,5},{2,6},{3,7},{4,0},{5,1},{6,2},{7,3},{8,12},{9,13},{10,... | collective-permute-start | bytes 196616 | tf_op jit(solution)/shard_map/ppermute | solution.py:50
  92.5 1.9 %collective-permute-start.19 = (bf16[128,256]{1,0:T(8,128)(2,1)S(1)}, bf16[128,256]{1,0:T(8,128)(2,1)S(1)}, u32[]{:S(2)}, u32[]{:S(2)}) collective-permute-start(bf16[128,256]{1,0:T(8,128)(2,1)S(1)} %get-tuple-element.86), channel_id=1, source_target_pairs={{0,6},{1,7},{2,4},{3,5},{4,2},{5,3},{6,0},{7,1},{8,14},{9,15},{10,... | collective-permute-start | bytes 196616 | tf_op jit(solution)/shard_map/ppermute | solution.py:50
  94.4 1.2 collective-permute-done.30
  95.7 1.3 collective-permute-done.18.refs_1_
  96.9 1.6 %collective-permute-done.19.refs_2_ = bf16[128,256]{1,0:T(8,128)(2,1)S(1)} collective-permute-done((bf16[128,256]{1,0:T(8,128)(2,1)S(1)}, bf16[128,256]{1,0:T(8,128)(2,1)S(1)}, u32[]{:S(2)}, u32[]{:S(2)}) %collective-permute-start.19) | collective-permute-done | bytes 65568 | tf_op jit(solution)/shard_map/ppermute | solution.py:50
  99.4 2.0 %collective-permute-start.23 = (f32[256,128]{1,0:T(8,128)S(1)}, f32[256,128]{1,0:T(8,128)S(1)}, u32[]{:S(2)}, u32[]{:S(2)}) collective-permute-start(f32[256,128]{1,0:T(8,128)S(1)} %get-tuple-element.52), channel_id=1, source_target_pairs={{0,16},{1,17},{2,18},{3,19},{4,20},{5,21},{6,22},{7,23},{8,24},{9,... | collective-permute-start | bytes 393224 | tf_op jit(solution)/shard_map/ppermute | solution.py:50
  101.5 2.0 %collective-permute-start.32 = (bf16[128,256]{1,0:T(8,128)(2,1)S(1)}, bf16[128,256]{1,0:T(8,128)(2,1)S(1)}, u32[]{:S(2)}, u32[]{:S(2)}) collective-permute-start(bf16[128,256]{1,0:T(8,128)(2,1)S(1)} %get-tuple-element.61), channel_id=1, source_target_pairs={{0,4},{1,5},{2,6},{3,7},{4,0},{5,1},{6,2},{7,3},{8,12},{9,13},{10,... | collective-permute-start | bytes 196616 | tf_op jit(solution)/shard_map/ppermute | solution.py:50
  103.5 2.4 %collective-permute-start.33 = (bf16[128,256]{1,0:T(8,128)(2,1)S(1)}, bf16[128,256]{1,0:T(8,128)(2,1)S(1)}, u32[]{:S(2)}, u32[]{:S(2)}) collective-permute-start(bf16[128,256]{1,0:T(8,128)(2,1)S(1)} %get-tuple-element.62), channel_id=1, source_target_pairs={{0,6},{1,7},{2,4},{3,5},{4,2},{5,3},{6,0},{7,1},{8,14},{9,15},{10,... | collective-permute-start | bytes 196616 | tf_op jit(solution)/shard_map/ppermute | solution.py:50
  105.8 1.1 collective-permute-done.31.refs_0_
  107.0 0.9 collective-permute-start.21
  107.8 2.3 %collective-permute-done.32.refs_1_ = bf16[128,256]{1,0:T(8,128)(2,1)S(1)} collective-permute-done((bf16[128,256]{1,0:T(8,128)(2,1)S(1)}, bf16[128,256]{1,0:T(8,128)(2,1)S(1)}, u32[]{:S(2)}, u32[]{:S(2)}) %collective-permute-start.32) | collective-permute-done | bytes 65568 | tf_op jit(solution)/shard_map/ppermute | solution.py:50
  111.7 1.7 %collective-permute-start.37 = (f32[256,128]{1,0:T(8,128)S(1)}, f32[256,128]{1,0:T(8,128)S(1)}, u32[]{:S(2)}, u32[]{:S(2)}) collective-permute-start(f32[256,128]{1,0:T(8,128)S(1)} %get-tuple-element.64), channel_id=1, source_target_pairs={{0,16},{1,17},{2,18},{3,19},{4,20},{5,21},{6,22},{7,23},{8,24},{9,... | collective-permute-start | bytes 393224 | tf_op jit(solution)/shard_map/ppermute | solution.py:50
  113.4 1.7 %collective-permute-start.34 = (bf16[256,128]{1,0:T(8,128)(2,1)S(1)}, bf16[256,128]{1,0:T(8,128)(2,1)S(1)}, u32[]{:S(2)}, u32[]{:S(2)}) collective-permute-start(bf16[256,128]{1,0:T(8,128)(2,1)S(1)} %get-tuple-element.65), channel_id=1, source_target_pairs={{0,2},{1,3},{2,0},{3,1},{4,6},{5,7},{6,4},{7,5},{8,10},{9,11},{10,... | collective-permute-start | bytes 196616 | tf_op jit(solution)/shard_map/ppermute | solution.py:50
  115.7 2.2 %collective-permute-start.36 = (bf16[256,128]{1,0:T(8,128)(2,1)S(1)}, bf16[256,128]{1,0:T(8,128)(2,1)S(1)}, u32[]{:S(2)}, u32[]{:S(2)}) collective-permute-start(bf16[256,128]{1,0:T(8,128)(2,1)S(1)} %get-tuple-element.65), channel_id=1, source_target_pairs={{0,6},{1,7},{2,4},{3,5},{4,2},{5,3},{6,0},{7,1},{8,14},{9,15},{10,... | collective-permute-start | bytes 196616 | tf_op jit(solution)/shard_map/ppermute | solution.py:50
  117.9 1.1 collective-permute-start.24
  119.1 1.7 %collective-permute-done.35 = bf16[256,128]{1,0:T(8,128)(2,1)S(1)} collective-permute-done((bf16[256,128]{1,0:T(8,128)(2,1)S(1)}, bf16[256,128]{1,0:T(8,128)(2,1)S(1)}, u32[]{:S(2)}, u32[]{:S(2)}) %collective-permute-start.35) | collective-permute-done | bytes 65568 | tf_op jit(solution)/shard_map/ppermute | solution.py:50
  120.8 1.1 collective-permute-done.36
  122.0 1.3 collective-permute-start.38
  123.2 4.0 %collective-permute-done.24 = bf16[4,256,128]{2,1,0:T(8,128)(2,1)S(1)} collective-permute-done((bf16[4,256,128]{2,1,0:T(8,128)(2,1)S(1)}, bf16[4,256,128]{2,1,0:T(8,128)(2,1)S(1)}, u32[]{:S(2)}, u32[]{:S(2)}) %collective-permute-start.24) | collective-permute-done | bytes 262176 | tf_op jit(solution)/shard_map/ppermute | solution.py:50
  127.3 1.7 %collective-permute-start.25 = (bf16[2,4,256,128]{3,2,1,0:T(8,128)(2,1)S(1)}, bf16[2,4,256,128]{3,2,1,0:T(8,128)(2,1)S(1)}, u32[]{:S(2)}, u32[]{:S(2)}) collective-permute-start(bf16[2,4,256,128]{3,2,1,0:T(8,128)(2,1)S(1)} %pad_maximum_fusion.2.refs_0_), channel_id=1, source_target_pairs={{0,16},{1,17},{2,18},{3,19},{4,20},{5,21},{6,22},{7,23},{8,9},{9,8... | collective-permute-start | bytes 1572872 | tf_op jit(solution)/shard_map/ppermute | solution.py:50
  129.0 3.9 %collective-permute-done.38 = bf16[4,256,128]{2,1,0:T(8,128)(2,1)S(1)} collective-permute-done((bf16[4,256,128]{2,1,0:T(8,128)(2,1)S(1)}, bf16[4,256,128]{2,1,0:T(8,128)(2,1)S(1)}, u32[]{:S(2)}, u32[]{:S(2)}) %collective-permute-start.38) | collective-permute-done | bytes 262176 | tf_op jit(solution)/shard_map/ppermute | solution.py:50
  132.9 1.7 %collective-permute-start.39 = (bf16[2,4,256,128]{3,2,1,0:T(8,128)(2,1)S(1)}, bf16[2,4,256,128]{3,2,1,0:T(8,128)(2,1)S(1)}, u32[]{:S(2)}, u32[]{:S(2)}) collective-permute-start(bf16[2,4,256,128]{3,2,1,0:T(8,128)(2,1)S(1)} %pad_maximum_fusion.3.refs_4_), channel_id=1, source_target_pairs={{0,16},{1,17},{2,18},{3,19},{4,20},{5,21},{6,22},{7,23},{8,9},{9,8... | collective-permute-start | bytes 1572872 | tf_op jit(solution)/shard_map/ppermute | solution.py:50
  135.1 1.4 collective-permute-done.25.refs_1_
  136.6 5.6 %collective-permute-done.39.refs_5_ = bf16[2,4,256,128]{3,2,1,0:T(8,128)(2,1)S(1)} collective-permute-done((bf16[2,4,256,128]{3,2,1,0:T(8,128)(2,1)S(1)}, bf16[2,4,256,128]{3,2,1,0:T(8,128)(2,1)S(1)}, u32[]{:S(2)}, u32[]{:S(2)}) %collective-permute-start.39) | collective-permute-done | bytes 524320 | tf_op jit(solution)/shard_map/ppermute | solution.py:50
  144.6 4.4 %assemble.1 = (bf16[2048,1024]{1,0:T(8,128)(2,1)}, f32[256,1024]{1,0:T(8,128)}) custom-call(s32[4]{0:T(128)S(1)} %pad_add_fusion.here_ref, bf16[2,4,256,128]{3,2,1,0:T(8,128)(2,1)S(1)} %pad_maximum_fusion.2.refs_0_, bf16[2,4,256,128]{3,2,1,0:T(8,128)(2,1)S(1)} %collective-permute-done.25.refs_1_, ...), custom_call_target="tpu_custom_call" | custom-call | tf_op jit(solution)/shard_map/assemble/pallas_call | solution.py:562
  (104 shorter events, 18.2 us)
Async XLA Ops:
  2.4 7.1 %collective-permute-start = (bf16[128,256]{1,0:T(8,128)(2,1)}, bf16[128,256]{1,0:T(8,128)(2,1)S(1)}, u32[]{:S(2)}, u32[]{:S(2)}) collective-permute-start(bf16[128,256]{1,0:T(8,128)(2,1)} %get-tuple-element.43), channel_id=1, source_target_pairs={{0,2},{1,3},{2,0},{3,1},{4,6},{5,7},{6,4},{7,5},{8,10},{9,11},{10,... | collective-permute-start | bytes 196616 | tf_op jit(solution)/shard_map/ppermute | solution.py:50
  5.5 15.2 %collective-permute-start.8 = (bf16[128,256]{1,0:T(8,128)(2,1)}, bf16[128,256]{1,0:T(8,128)(2,1)S(1)}, u32[]{:S(2)}, u32[]{:S(2)}) collective-permute-start(bf16[128,256]{1,0:T(8,128)(2,1)} %get-tuple-element.43), channel_id=1, source_target_pairs={{0,4},{1,5},{2,6},{3,7},{4,0},{5,1},{6,2},{7,3},{8,12},{9,13},{10,... | collective-permute-start | bytes 196616 | tf_op jit(solution)/shard_map/ppermute | solution.py:50
  8.1 12.6 %collective-permute-start.9 = (bf16[128,256]{1,0:T(8,128)(2,1)}, bf16[128,256]{1,0:T(8,128)(2,1)S(1)}, u32[]{:S(2)}, u32[]{:S(2)}) collective-permute-start(bf16[128,256]{1,0:T(8,128)(2,1)} %get-tuple-element.43), channel_id=1, source_target_pairs={{0,6},{1,7},{2,4},{3,5},{4,2},{5,3},{6,0},{7,1},{8,14},{9,15},{10,... | collective-permute-start | bytes 196616 | tf_op jit(solution)/shard_map/ppermute | solution.py:50
  20.7 21.2 %copy-start.11 = (s32[32,32]{1,0:T(8,128)S(1)}, s32[32,32]{1,0:T(8,128)}, u32[]{:S(2)}) copy-start(s32[32,32]{1,0:T(8,128)} %param.15) | copy-start | bytes 12292
  20.8 6.4 %collective-permute-start.10 = (bf16[4,128,256]{2,1,0:T(8,128)(2,1)S(1)}, bf16[4,128,256]{2,1,0:T(8,128)(2,1)S(1)}, u32[]{:S(2)}, u32[]{:S(2)}) collective-permute-start(bf16[4,128,256]{2,1,0:T(8,128)(2,1)S(1)} %get-tuple-element.90), channel_id=1, source_target_pairs={{0,1},{1,0},{2,3},{3,2},{4,5},{5,4},{6,7},{7,6},{8,24},{9,25},{10,... | collective-permute-start | bytes 786440 | tf_op jit(solution)/shard_map/ppermute | solution.py:50
  22.5 4.9 %collective-permute-start.1 = (bf16[144,256]{1,0:T(8,128)(2,1)S(1)}, bf16[144,256]{1,0:T(8,128)(2,1)S(1)}, u32[]{:S(2)}, u32[]{:S(2)}) collective-permute-start(bf16[144,256]{1,0:T(8,128)(2,1)S(1)} %get-tuple-element.41), channel_id=1, source_target_pairs={{0,2},{1,3},{2,0},{3,1},{4,6},{5,7},{6,4},{7,5},{8,10},{9,11},{10,... | collective-permute-start | bytes 221192 | tf_op jit(solution)/shard_map/ppermute | solution.py:50
  23.2 7.5 %collective-permute-start.2 = (bf16[144,256]{1,0:T(8,128)(2,1)S(1)}, bf16[144,256]{1,0:T(8,128)(2,1)S(1)}, u32[]{:S(2)}, u32[]{:S(2)}) collective-permute-start(bf16[144,256]{1,0:T(8,128)(2,1)S(1)} %get-tuple-element.41), channel_id=1, source_target_pairs={{0,4},{1,5},{2,6},{3,7},{4,0},{5,1},{6,2},{7,3},{8,12},{9,13},{10,... | collective-permute-start | bytes 221192 | tf_op jit(solution)/shard_map/ppermute | solution.py:50
  26.7 6.2 %collective-permute-start.3 = (bf16[144,256]{1,0:T(8,128)(2,1)S(1)}, bf16[144,256]{1,0:T(8,128)(2,1)S(1)}, u32[]{:S(2)}, u32[]{:S(2)}) collective-permute-start(bf16[144,256]{1,0:T(8,128)(2,1)S(1)} %get-tuple-element.41), channel_id=1, source_target_pairs={{0,6},{1,7},{2,4},{3,5},{4,2},{5,3},{6,0},{7,1},{8,14},{9,15},{10,... | collective-permute-start | bytes 221192 | tf_op jit(solution)/shard_map/ppermute | solution.py:50
  27.4 13.9 %collective-permute-start.11 = (bf16[2,4,128,256]{3,2,1,0:T(8,128)(2,1)S(1)}, bf16[2,4,128,256]{3,2,1,0:T(8,128)(2,1)S(1)}, u32[]{:S(2)}, u32[]{:S(2)}) collective-permute-start(bf16[2,4,128,256]{3,2,1,0:T(8,128)(2,1)S(1)} %pad_maximum_fusion.1.refs_0_), channel_id=1, source_target_pairs={{0,16},{1,17},{2,18},{3,19},{4,20},{5,21},{6,22},{7,23},{8,9},{9,8... | collective-permute-start | bytes 1572872 | tf_op jit(solution)/shard_map/ppermute | solution.py:50
  32.9 6.8 %collective-permute-start.4 = (bf16[4,144,256]{2,1,0:T(8,128)(2,1)S(1)}, bf16[4,144,256]{2,1,0:T(8,128)(2,1)S(1)}, u32[]{:S(2)}, u32[]{:S(2)}) collective-permute-start(bf16[4,144,256]{2,1,0:T(8,128)(2,1)S(1)} %get-tuple-element.78), channel_id=1, source_target_pairs={{0,1},{1,0},{2,3},{3,2},{4,5},{5,4},{6,7},{7,6},{8,24},{9,25},{10,... | collective-permute-start | bytes 884744 | tf_op jit(solution)/shard_map/ppermute | solution.py:50
  39.8 9.9 %collective-permute-start.5 = (bf16[2,4,144,256]{3,2,1,0:T(8,128)(2,1)S(1)}, bf16[2,4,144,256]{3,2,1,0:T(8,128)(2,1)S(1)}, u32[]{:S(2)}, u32[]{:S(2)}) collective-permute-start(bf16[2,4,144,256]{3,2,1,0:T(8,128)(2,1)S(1)} %pad_maximum_fusion.refs_0_), channel_id=1, source_target_pairs={{0,16},{1,17},{2,18},{3,19},{4,20},{5,21},{6,22},{7,23},{8,9},{9,8... | collective-permute-start | bytes 1769480 | tf_op jit(solution)/shard_map/ppermute | solution.py:50
  41.3 8.4 %collective-permute-start.12 = (bf16[2,4,128,256]{3,2,1,0:T(8,128)(2,1)S(1)}, bf16[2,4,128,256]{3,2,1,0:T(8,128)(2,1)S(1)}, u32[]{:S(2)}, u32[]{:S(2)}) collective-permute-start(bf16[2,4,128,256]{3,2,1,0:T(8,128)(2,1)S(1)} %pad_maximum_fusion.1.refs_0_), channel_id=1, source_target_pairs={{0,8},{1,9},{2,10},{3,11},{4,12},{5,13},{6,14},{7,15},{8,0},{9,1},... | collective-permute-start | bytes 1572872 | tf_op jit(solution)/shard_map/ppermute | solution.py:50
  41.4 8.4 %collective-permute-start.13 = (bf16[2,4,128,256]{3,2,1,0:T(8,128)(2,1)S(1)}, bf16[2,4,128,256]{3,2,1,0:T(8,128)(2,1)}, u32[]{:S(2)}, u32[]{:S(2)}) collective-permute-start(bf16[2,4,128,256]{3,2,1,0:T(8,128)(2,1)S(1)} %collective-permute-done.11.refs_1_), channel_id=1, source_target_pairs={{0,8},{1,9},{2,10},{3,11},{4,12},{5,13},{6,14},{7,15},{8,0},{9,1},... | collective-permute-start | bytes 1572872 | tf_op jit(solution)/shard_map/ppermute | solution.py:50
  42.0 14.6 %collective-permute-start.6 = (bf16[2,4,144,256]{3,2,1,0:T(8,128)(2,1)S(1)}, bf16[2,4,144,256]{3,2,1,0:T(8,128)(2,1)S(1)}, u32[]{:S(2)}, u32[]{:S(2)}) collective-permute-start(bf16[2,4,144,256]{3,2,1,0:T(8,128)(2,1)S(1)} %pad_maximum_fusion.refs_0_), channel_id=1, source_target_pairs={{0,8},{1,9},{2,10},{3,11},{4,12},{5,13},{6,14},{7,15},{8,0},{9,1},... | collective-permute-start | bytes 1769480 | tf_op jit(solution)/shard_map/ppermute | solution.py:50
  49.7 7.0 %collective-permute-start.7 = (bf16[2,4,144,256]{3,2,1,0:T(8,128)(2,1)S(1)}, bf16[2,4,144,256]{3,2,1,0:T(8,128)(2,1)S(1)}, u32[]{:S(2)}, u32[]{:S(2)}) collective-permute-start(bf16[2,4,144,256]{3,2,1,0:T(8,128)(2,1)S(1)} %collective-permute-done.5.refs_1_), channel_id=1, source_target_pairs={{0,8},{1,9},{2,10},{3,11},{4,12},{5,13},{6,14},{7,15},{8,0},{9,1},... | collective-permute-start | bytes 1769480 | tf_op jit(solution)/shard_map/ppermute | solution.py:50
  66.8 4.2 %collective-permute-start.14 = (bf16[2,2,4,128,256]{4,3,2,1,0:T(8,128)(2,1)S(1)}, bf16[2,2,4,128,256]{4,3,2,1,0:T(8,128)(2,1)S(1)}, u32[]{:S(2)}, u32[]{:S(2)}) collective-permute-start(bf16[2,2,4,128,256]{4,3,2,1,0:T(8,128)(2,1)S(1)} %get-tuple-element.50), channel_id=1, source_target_pairs={{0,8},{1,9},{2,10},{3,11},{4,12},{5,13},{6,14},{7,15},{8,0},{9,1},... | collective-permute-start | bytes 3145736 | tf_op jit(solution)/shard_map/ppermute | solution.py:50
  70.9 2.7 %collective-permute-start.28 = (bf16[2,2,4,128,256]{4,3,2,1,0:T(8,128)(2,1)S(1)}, bf16[2,2,4,128,256]{4,3,2,1,0:T(8,128)(2,1)S(1)}, u32[]{:S(2)}, u32[]{:S(2)}) collective-permute-start(bf16[2,2,4,128,256]{4,3,2,1,0:T(8,128)(2,1)S(1)} %get-tuple-element.59), channel_id=1, source_target_pairs={{0,8},{1,9},{2,10},{3,11},{4,12},{5,13},{6,14},{7,15},{8,0},{9,1},... | collective-permute-start | bytes 3145736 | tf_op jit(solution)/shard_map/ppermute | solution.py:50
  71.2 9.2 %collective-permute-start.15 = (bf16[2,4,128,256]{3,2,1,0:T(8,128)(2,1)S(1)}, bf16[2,4,128,256]{3,2,1,0:T(8,128)(2,1)S(1)}, u32[]{:S(2)}, u32[]{:S(2)}) collective-permute-start(bf16[2,4,128,256]{3,2,1,0:T(8,128)(2,1)S(1)} %fusion.2), channel_id=1, source_target_pairs={{0,16},{1,17},{2,18},{3,19},{4,20},{5,21},{6,22},{7,23},{8,9},{9,8... | collective-permute-start | bytes 1572872 | tf_op jit(solution)/shard_map/ppermute | solution.py:50
  73.9 15.0 %collective-permute-start.29 = (bf16[2,4,128,256]{3,2,1,0:T(8,128)(2,1)S(1)}, bf16[2,4,128,256]{3,2,1,0:T(8,128)(2,1)S(1)}, u32[]{:S(2)}, u32[]{:S(2)}) collective-permute-start(bf16[2,4,128,256]{3,2,1,0:T(8,128)(2,1)S(1)} %fusion.3), channel_id=1, source_target_pairs={{0,16},{1,17},{2,18},{3,19},{4,20},{5,21},{6,22},{7,23},{8,9},{9,8... | collective-permute-start | bytes 1572872 | tf_op jit(solution)/shard_map/ppermute | solution.py:50
  80.6 9.2 %collective-permute-start.16 = (bf16[4,128,256]{2,1,0:T(8,128)(2,1)S(1)}, bf16[4,128,256]{2,1,0:T(8,128)(2,1)S(1)}, u32[]{:S(2)}, u32[]{:S(2)}) collective-permute-start(bf16[4,128,256]{2,1,0:T(8,128)(2,1)S(1)} %fusion.6), channel_id=1, source_target_pairs={{0,1},{1,0},{2,3},{3,2},{4,5},{5,4},{6,7},{7,6},{8,24},{9,25},{10,... | collective-permute-start | bytes 786440 | tf_op jit(solution)/shard_map/ppermute | solution.py:50
  89.1 9.5 %copy-start = (f32[256,1024]{1,0:T(8,128)S(1)}, f32[256,1024]{1,0:T(8,128)}, u32[]{:S(2)}) copy-start(f32[256,1024]{1,0:T(8,128)} %refs_3_.3) | copy-start | bytes 3145732
  89.1 9.5 %copy-start.2 = (f32[256,1024]{1,0:T(8,128)S(1)}, f32[256,1024]{1,0:T(8,128)}, u32[]{:S(2)}) copy-start(f32[256,1024]{1,0:T(8,128)} %refs_4_.3) | copy-start | bytes 3145732
  89.1 9.5 %copy-start.3 = (f32[256,1024]{1,0:T(8,128)S(1)}, f32[256,1024]{1,0:T(8,128)}, u32[]{:S(2)}) copy-start(f32[256,1024]{1,0:T(8,128)} %refs_5_.3) | copy-start | bytes 3145732
  89.1 6.4 %collective-permute-start.30 = (bf16[4,128,256]{2,1,0:T(8,128)(2,1)S(1)}, bf16[4,128,256]{2,1,0:T(8,128)(2,1)S(1)}, u32[]{:S(2)}, u32[]{:S(2)}) collective-permute-start(bf16[4,128,256]{2,1,0:T(8,128)(2,1)S(1)} %fusion.7), channel_id=1, source_target_pairs={{0,1},{1,0},{2,3},{3,2},{4,5},{5,4},{6,7},{7,6},{8,24},{9,25},{10,... | collective-permute-start | bytes 786440 | tf_op jit(solution)/shard_map/ppermute | solution.py:50
  90.0 5.7 %collective-permute-start.17 = (bf16[128,256]{1,0:T(8,128)(2,1)S(1)}, bf16[128,256]{1,0:T(8,128)(2,1)S(1)}, u32[]{:S(2)}, u32[]{:S(2)}) collective-permute-start(bf16[128,256]{1,0:T(8,128)(2,1)S(1)} %get-tuple-element.88), channel_id=1, source_target_pairs={{0,2},{1,3},{2,0},{3,1},{4,6},{5,7},{6,4},{7,5},{8,10},{9,11},{10,... | collective-permute-start | bytes 196616 | tf_op jit(solution)/shard_map/ppermute | solution.py:50
  90.9 6.0 %collective-permute-start.18 = (bf16[128,256]{1,0:T(8,128)(2,1)S(1)}, bf16[128,256]{1,0:T(8,128)(2,1)S(1)}, u32[]{:S(2)}, u32[]{:S(2)}) collective-permute-start(bf16[128,256]{1,0:T(8,128)(2,1)S(1)} %get-tuple-element.87), channel_id=1, source_target_pairs={{0,4},{1,5},{2,6},{3,7},{4,0},{5,1},{6,2},{7,3},{8,12},{9,13},{10,... | collective-permute-start | bytes 196616 | tf_op jit(solution)/shard_map/ppermute | solution.py:50
  92.5 6.1 %collective-permute-start.19 = (bf16[128,256]{1,0:T(8,128)(2,1)S(1)}, bf16[128,256]{1,0:T(8,128)(2,1)S(1)}, u32[]{:S(2)}, u32[]{:S(2)}) collective-permute-start(bf16[128,256]{1,0:T(8,128)(2,1)S(1)} %get-tuple-element.86), channel_id=1, source_target_pairs={{0,6},{1,7},{2,4},{3,5},{4,2},{5,3},{6,0},{7,1},{8,14},{9,15},{10,... | collective-permute-start | bytes 196616 | tf_op jit(solution)/shard_map/ppermute | solution.py:50
  99.4 14.0 %collective-permute-start.23 = (f32[256,128]{1,0:T(8,128)S(1)}, f32[256,128]{1,0:T(8,128)S(1)}, u32[]{:S(2)}, u32[]{:S(2)}) collective-permute-start(f32[256,128]{1,0:T(8,128)S(1)} %get-tuple-element.52), channel_id=1, source_target_pairs={{0,16},{1,17},{2,18},{3,19},{4,20},{5,21},{6,22},{7,23},{8,24},{9,... | collective-permute-start | bytes 393224 | tf_op jit(solution)/shard_map/ppermute | solution.py:50
  101.4 5.6 %collective-permute-start.31 = (bf16[128,256]{1,0:T(8,128)(2,1)S(1)}, bf16[128,256]{1,0:T(8,128)(2,1)S(1)}, u32[]{:S(2)}, u32[]{:S(2)}) collective-permute-start(bf16[128,256]{1,0:T(8,128)(2,1)S(1)} %get-tuple-element.60), channel_id=1, source_target_pairs={{0,2},{1,3},{2,0},{3,1},{4,6},{5,7},{6,4},{7,5},{8,10},{9,11},{10,... | collective-permute-start | bytes 196616 | tf_op jit(solution)/shard_map/ppermute | solution.py:50
  101.5 8.7 %collective-permute-start.32 = (bf16[128,256]{1,0:T(8,128)(2,1)S(1)}, bf16[128,256]{1,0:T(8,128)(2,1)S(1)}, u32[]{:S(2)}, u32[]{:S(2)}) collective-permute-start(bf16[128,256]{1,0:T(8,128)(2,1)S(1)} %get-tuple-element.61), channel_id=1, source_target_pairs={{0,4},{1,5},{2,6},{3,7},{4,0},{5,1},{6,2},{7,3},{8,12},{9,13},{10,... | collective-permute-start | bytes 196616 | tf_op jit(solution)/shard_map/ppermute | solution.py:50
  103.5 7.4 %collective-permute-start.33 = (bf16[128,256]{1,0:T(8,128)(2,1)S(1)}, bf16[128,256]{1,0:T(8,128)(2,1)S(1)}, u32[]{:S(2)}, u32[]{:S(2)}) collective-permute-start(bf16[128,256]{1,0:T(8,128)(2,1)S(1)} %get-tuple-element.62), channel_id=1, source_target_pairs={{0,6},{1,7},{2,4},{3,5},{4,2},{5,3},{6,0},{7,1},{8,14},{9,15},{10,... | collective-permute-start | bytes 196616 | tf_op jit(solution)/shard_map/ppermute | solution.py:50
  105.8 9.3 %collective-permute-start.20 = (bf16[256,128]{1,0:T(8,128)(2,1)S(1)}, bf16[256,128]{1,0:T(8,128)(2,1)S(1)}, u32[]{:S(2)}, u32[]{:S(2)}) collective-permute-start(bf16[256,128]{1,0:T(8,128)(2,1)S(1)} %get-tuple-element.53), channel_id=1, source_target_pairs={{0,2},{1,3},{2,0},{3,1},{4,6},{5,7},{6,4},{7,5},{8,10},{9,11},{10,... | collective-permute-start | bytes 196616 | tf_op jit(solution)/shard_map/ppermute | solution.py:50
  107.0 8.8 %collective-permute-start.21 = (bf16[256,128]{1,0:T(8,128)(2,1)S(1)}, bf16[256,128]{1,0:T(8,128)(2,1)S(1)}, u32[]{:S(2)}, u32[]{:S(2)}) collective-permute-start(bf16[256,128]{1,0:T(8,128)(2,1)S(1)} %get-tuple-element.53), channel_id=1, source_target_pairs={{0,4},{1,5},{2,6},{3,7},{4,0},{5,1},{6,2},{7,3},{8,12},{9,13},{10,... | collective-permute-start | bytes 196616 | tf_op jit(solution)/shard_map/ppermute | solution.py:50
  110.2 7.7 %collective-permute-start.22 = (bf16[256,128]{1,0:T(8,128)(2,1)S(1)}, bf16[256,128]{1,0:T(8,128)(2,1)S(1)}, u32[]{:S(2)}, u32[]{:S(2)}) collective-permute-start(bf16[256,128]{1,0:T(8,128)(2,1)S(1)} %get-tuple-element.53), channel_id=1, source_target_pairs={{0,6},{1,7},{2,4},{3,5},{4,2},{5,3},{6,0},{7,1},{8,14},{9,15},{10,... | collective-permute-start | bytes 196616 | tf_op jit(solution)/shard_map/ppermute | solution.py:50
  111.7 7.4 %collective-permute-start.37 = (f32[256,128]{1,0:T(8,128)S(1)}, f32[256,128]{1,0:T(8,128)S(1)}, u32[]{:S(2)}, u32[]{:S(2)}) collective-permute-start(f32[256,128]{1,0:T(8,128)S(1)} %get-tuple-element.64), channel_id=1, source_target_pairs={{0,16},{1,17},{2,18},{3,19},{4,20},{5,21},{6,22},{7,23},{8,24},{9,... | collective-permute-start | bytes 393224 | tf_op jit(solution)/shard_map/ppermute | solution.py:50
  113.4 5.7 %collective-permute-start.34 = (bf16[256,128]{1,0:T(8,128)(2,1)S(1)}, bf16[256,128]{1,0:T(8,128)(2,1)S(1)}, u32[]{:S(2)}, u32[]{:S(2)}) collective-permute-start(bf16[256,128]{1,0:T(8,128)(2,1)S(1)} %get-tuple-element.65), channel_id=1, source_target_pairs={{0,2},{1,3},{2,0},{3,1},{4,6},{5,7},{6,4},{7,5},{8,10},{9,11},{10,... | collective-permute-start | bytes 196616 | tf_op jit(solution)/shard_map/ppermute | solution.py:50
  115.2 5.7 %collective-permute-start.35 = (bf16[256,128]{1,0:T(8,128)(2,1)S(1)}, bf16[256,128]{1,0:T(8,128)(2,1)S(1)}, u32[]{:S(2)}, u32[]{:S(2)}) collective-permute-start(bf16[256,128]{1,0:T(8,128)(2,1)S(1)} %get-tuple-element.65), channel_id=1, source_target_pairs={{0,4},{1,5},{2,6},{3,7},{4,0},{5,1},{6,2},{7,3},{8,12},{9,13},{10,... | collective-permute-start | bytes 196616 | tf_op jit(solution)/shard_map/ppermute | solution.py:50
  115.7 6.2 %collective-permute-start.36 = (bf16[256,128]{1,0:T(8,128)(2,1)S(1)}, bf16[256,128]{1,0:T(8,128)(2,1)S(1)}, u32[]{:S(2)}, u32[]{:S(2)}) collective-permute-start(bf16[256,128]{1,0:T(8,128)(2,1)S(1)} %get-tuple-element.65), channel_id=1, source_target_pairs={{0,6},{1,7},{2,4},{3,5},{4,2},{5,3},{6,0},{7,1},{8,14},{9,15},{10,... | collective-permute-start | bytes 196616 | tf_op jit(solution)/shard_map/ppermute | solution.py:50
  117.9 9.3 %collective-permute-start.24 = (bf16[4,256,128]{2,1,0:T(8,128)(2,1)S(1)}, bf16[4,256,128]{2,1,0:T(8,128)(2,1)S(1)}, u32[]{:S(2)}, u32[]{:S(2)}) collective-permute-start(bf16[4,256,128]{2,1,0:T(8,128)(2,1)S(1)} %get-tuple-element.85), channel_id=1, source_target_pairs={{0,1},{1,0},{2,3},{3,2},{4,5},{5,4},{6,7},{7,6},{8,24},{9,25},{10,... | collective-permute-start | bytes 786440 | tf_op jit(solution)/shard_map/ppermute | solution.py:50
  122.0 10.9 %collective-permute-start.38 = (bf16[4,256,128]{2,1,0:T(8,128)(2,1)S(1)}, bf16[4,256,128]{2,1,0:T(8,128)(2,1)S(1)}, u32[]{:S(2)}, u32[]{:S(2)}) collective-permute-start(bf16[4,256,128]{2,1,0:T(8,128)(2,1)S(1)} %get-tuple-element.80), channel_id=1, source_target_pairs={{0,1},{1,0},{2,3},{3,2},{4,5},{5,4},{6,7},{7,6},{8,24},{9,25},{10,... | collective-permute-start | bytes 786440 | tf_op jit(solution)/shard_map/ppermute | solution.py:50
  127.3 9.2 %collective-permute-start.25 = (bf16[2,4,256,128]{3,2,1,0:T(8,128)(2,1)S(1)}, bf16[2,4,256,128]{3,2,1,0:T(8,128)(2,1)S(1)}, u32[]{:S(2)}, u32[]{:S(2)}) collective-permute-start(bf16[2,4,256,128]{3,2,1,0:T(8,128)(2,1)S(1)} %pad_maximum_fusion.2.refs_0_), channel_id=1, source_target_pairs={{0,16},{1,17},{2,18},{3,19},{4,20},{5,21},{6,22},{7,23},{8,9},{9,8... | collective-permute-start | bytes 1572872 | tf_op jit(solution)/shard_map/ppermute | solution.py:50
  132.9 9.2 %collective-permute-start.39 = (bf16[2,4,256,128]{3,2,1,0:T(8,128)(2,1)S(1)}, bf16[2,4,256,128]{3,2,1,0:T(8,128)(2,1)S(1)}, u32[]{:S(2)}, u32[]{:S(2)}) collective-permute-start(bf16[2,4,256,128]{3,2,1,0:T(8,128)(2,1)S(1)} %pad_maximum_fusion.3.refs_4_), channel_id=1, source_target_pairs={{0,16},{1,17},{2,18},{3,19},{4,20},{5,21},{6,22},{7,23},{8,9},{9,8... | collective-permute-start | bytes 1572872 | tf_op jit(solution)/shard_map/ppermute | solution.py:50
  134.6 7.5 %collective-permute-start.42 = (f32[2,256,128]{2,1,0:T(8,128)S(1)}, f32[2,256,128]{2,1,0:T(8,128)S(1)}, u32[]{:S(2)}, u32[]{:S(2)}) collective-permute-start(f32[2,256,128]{2,1,0:T(8,128)S(1)} %pad_maximum_fusion.6.refs_8_), channel_id=1, source_target_pairs={{0,8},{1,9},{2,10},{3,11},{4,12},{5,13},{6,14},{7,15},{8,0},{9,1},... | collective-permute-start | bytes 786440 | tf_op jit(solution)/shard_map/ppermute | solution.py:50
  134.6 10.0 %collective-permute-start.26 = (bf16[2,4,256,128]{3,2,1,0:T(8,128)(2,1)S(1)}, bf16[2,4,256,128]{3,2,1,0:T(8,128)(2,1)S(1)}, u32[]{:S(2)}, u32[]{:S(2)}) collective-permute-start(bf16[2,4,256,128]{3,2,1,0:T(8,128)(2,1)S(1)} %pad_maximum_fusion.2.refs_0_), channel_id=1, source_target_pairs={{0,8},{1,9},{2,10},{3,11},{4,12},{5,13},{6,14},{7,15},{8,0},{9,1},... | collective-permute-start | bytes 1572872 | tf_op jit(solution)/shard_map/ppermute | solution.py:50
  135.1 9.4 %collective-permute-start.40 = (bf16[2,4,256,128]{3,2,1,0:T(8,128)(2,1)S(1)}, bf16[2,4,256,128]{3,2,1,0:T(8,128)(2,1)}, u32[]{:S(2)}, u32[]{:S(2)}) collective-permute-start(bf16[2,4,256,128]{3,2,1,0:T(8,128)(2,1)S(1)} %pad_maximum_fusion.3.refs_4_), channel_id=1, source_target_pairs={{0,8},{1,9},{2,10},{3,11},{4,12},{5,13},{6,14},{7,15},{8,0},{9,1},... | collective-permute-start | bytes 1572872 | tf_op jit(solution)/shard_map/ppermute | solution.py:50
  136.6 8.0 %collective-permute-start.27 = (bf16[2,4,256,128]{3,2,1,0:T(8,128)(2,1)S(1)}, bf16[2,4,256,128]{3,2,1,0:T(8,128)(2,1)}, u32[]{:S(2)}, u32[]{:S(2)}) collective-permute-start(bf16[2,4,256,128]{3,2,1,0:T(8,128)(2,1)S(1)} %collective-permute-done.25.refs_1_), channel_id=1, source_target_pairs={{0,8},{1,9},{2,10},{3,11},{4,12},{5,13},{6,14},{7,15},{8,0},{9,1},... | collective-permute-start | bytes 1572872 | tf_op jit(solution)/shard_map/ppermute | solution.py:50
  142.2 2.4 %collective-permute-start.41 = (bf16[2,4,256,128]{3,2,1,0:T(8,128)(2,1)S(1)}, bf16[2,4,256,128]{3,2,1,0:T(8,128)(2,1)}, u32[]{:S(2)}, u32[]{:S(2)}) collective-permute-start(bf16[2,4,256,128]{3,2,1,0:T(8,128)(2,1)S(1)} %collective-permute-done.39.refs_5_), channel_id=1, source_target_pairs={{0,8},{1,9},{2,10},{3,11},{4,12},{5,13},{6,14},{7,15},{8,0},{9,1},... | collective-permute-start | bytes 1572872 | tf_op jit(solution)/shard_map/ppermute | solution.py:50
  142.2 2.4 %collective-permute-start.43 = (f32[2,256,128]{2,1,0:T(8,128)S(1)}, f32[2,256,128]{2,1,0:T(8,128)}, u32[]{:S(2)}, u32[]{:S(2)}) collective-permute-start(f32[2,256,128]{2,1,0:T(8,128)S(1)} %pad_maximum_fusion.8.refs_10_), channel_id=1, source_target_pairs={{0,8},{1,9},{2,10},{3,11},{4,12},{5,13},{6,14},{7,15},{8,0},{9,1},... | collective-permute-start | bytes 786440 | tf_op jit(solution)/shard_map/ppermute | solution.py:50
  (8 other events, 14.6 us)

commit v5 on v4

--- a/solution.py
+++ b/solution.py
@@ -228,7 +228,7 @@
             jax.ShapeDtypeStruct((high, depth), BF16),
         ],
         scratch_shapes=[pltpu.VMEM((16, tokens), F32)],
-        compiler_params=ROOM,
+        compiler_params=pltpu.CompilerParams(vmem_limit_bytes=56 * 2**20),
         cost_estimate=pl.CostEstimate(
             flops=10 * tokens * width, bytes_accessed=4 * tokens * width, transcendentals=0
         ),

time: 150 us -> 149 us (level)
  local copies, waits for them, and re-layouts: 12.4 us -> 7.04 us
  Pallas kernels: 29.3 us -> 32.6 us
    unnamed x24 -> x12, local copies, waits for them, and re-layouts: 9.35 us -> 2.21 us
    pallas_call x1, Pallas kernels: 3.26 us -> 6.5 us  [normalize(): pl.pallas_call(norm_kernel, grid=(tokens // tile,), in_specs=[pl.BlockSpe...]
  transfers between devices with their start and end apart: 44 -> 44, of which waited for: 21 -> 21; matrix products, arithmetic and copies ran while one was open for 3% -> 5% of each run, Pallas kernels for 8% -> 10%
where the time goes in v5:
time: 149 us; the launch traced here: 148 us
  waiting for transfers between devices  58.2 us (39%)
  starting transfers between devices  46.4 us (31%)
  Pallas kernels  32.6 us (22%)
  local copies, waits for them, and re-layouts  7.04 us (5%)
  other arithmetic  2.99 us (2%)
    ppermute x44, waiting for transfers between devices, permute(): return lax.ppermute(value, ALL, pairs)  58.2 us
    ppermute x44, starting transfers between devices, permute(): return lax.ppermute(value, ALL, pairs)  46.4 us
    pallas_call x1, Pallas kernels, signal_and_gradient(): pl.pallas_call(functools.partial(signal_kernel, plan, segs, samples, tota...  10.1 us
    pallas_call x1, Pallas kernels, normalize(): pl.pallas_call(norm_kernel, grid=(tokens // tile,), in_specs=[pl.BlockSpe...  6.5 us
    pallas_call x1, Pallas kernels, early_logits(): pl.pallas_call(functools.partial(logits_kernel, plan), in_specs=[SMEM] +...  4.73 us
    pallas_call x1, Pallas kernels, assemble(): pl.pallas_call(functools.partial(assemble_kernel, plan), in_specs=[SMEM]...  4.36 us
    pallas_call x1, Pallas kernels, signal_and_gradient(): pl.pallas_call(functools.partial(gradient_kernel, plan), in_specs=[SMEM,...  3.5 us
  transfers between devices with their start and end apart: 44, of which 21 were waited for; matrix products, arithmetic and copies ran while one was open for 5% of the time, Pallas kernels for 10%

profile of v5, /device:TPU:0, one launch (start us, length us, event | category | flops | bytes accessed | tf_op | source)
XLA Modules:
  0.0 148.2 jit_solution(14736099752269613204)
XLA Ops:
  0.7 1.8 %shard.1 = (bf16[128,256]{1,0:T(8,128)(2,1)}, bf16[128,256]{1,0:T(8,128)(2,1)}) custom-call(s32[1]{0:T(128)} %bitcast.5.place_ref, f32[256,1024]{1,0:T(8,128)} %refs_3_.3), custom_call_target="tpu_custom_call" | custom-call | tf_op jit(solution)/shard_map/shard/pallas_call | solution.py:107
  2.4 3.1 %collective-permute-start = (bf16[128,256]{1,0:T(8,128)(2,1)}, bf16[128,256]{1,0:T(8,128)(2,1)S(1)}, u32[]{:S(2)}, u32[]{:S(2)}) collective-permute-start(bf16[128,256]{1,0:T(8,128)(2,1)} %get-tuple-element.43), channel_id=1, source_target_pairs={{0,2},{1,3},{2,0},{3,1},{4,6},{5,7},{6,4},{7,5},{8,10},{9,11},{10,... | collective-permute-start | bytes 196616 | tf_op jit(solution)/shard_map/ppermute | solution.py:50
  5.5 2.6 %collective-permute-start.8 = (bf16[128,256]{1,0:T(8,128)(2,1)}, bf16[128,256]{1,0:T(8,128)(2,1)S(1)}, u32[]{:S(2)}, u32[]{:S(2)}) collective-permute-start(bf16[128,256]{1,0:T(8,128)(2,1)} %get-tuple-element.43), channel_id=1, source_target_pairs={{0,4},{1,5},{2,6},{3,7},{4,0},{5,1},{6,2},{7,3},{8,12},{9,13},{10,... | collective-permute-start | bytes 196616 | tf_op jit(solution)/shard_map/ppermute | solution.py:50
  8.8 1.3 copy.16.tail_ref
  10.7 1.3 broadcast_in_dim.12.value_ref
  12.0 6.5 %normalize.1 = (bf16[1024,2048]{1,0:T(8,128)(2,1)}, bf16[144,256]{1,0:T(8,128)(2,1)}) custom-call(bf16[1024,2048]{1,0:T(8,128)(2,1)} %bitcast.90, f32[1,2048]{1,0:T(1,128)} %bitcast.111, bf16[16,2048]{1,0:T(8,128)(2,1)} %broadcast_in_dim.12.value_ref, bf16[32,32]{1,0:T(8,128)(2,1)} %r_ref.1, s32[32,32]{1,0:T(8,128)} %e_ref.1, bf16[32,1]{1,0:T(8,128)(2,1)} %copy.16.tail_ref, ...), custom_call_target="tpu_custom_call" | custom-call | flops 20971520 | bytes 8388608 | tf_op jit(solution)/shard_map/normalize/pallas_call | solution.py:212
  18.6 1.8 %collective-permute-start.10 = (bf16[4,128,256]{2,1,0:T(8,128)(2,1)S(1)}, bf16[4,128,256]{2,1,0:T(8,128)(2,1)S(1)}, u32[]{:S(2)}, u32[]{:S(2)}) collective-permute-start(bf16[4,128,256]{2,1,0:T(8,128)(2,1)S(1)} %get-tuple-element.90), channel_id=1, source_target_pairs={{0,1},{1,0},{2,3},{3,2},{4,5},{5,4},{6,7},{7,6},{8,24},{9,25},{10,... | collective-permute-start | bytes 786440 | tf_op jit(solution)/shard_map/ppermute | solution.py:50
  21.1 3.5 %collective-permute-start.2 = (bf16[144,256]{1,0:T(8,128)(2,1)}, bf16[144,256]{1,0:T(8,128)(2,1)S(1)}, u32[]{:S(2)}, u32[]{:S(2)}) collective-permute-start(bf16[144,256]{1,0:T(8,128)(2,1)} %get-tuple-element.41), channel_id=1, source_target_pairs={{0,4},{1,5},{2,6},{3,7},{4,0},{5,1},{6,2},{7,3},{8,12},{9,13},{10,... | collective-permute-start | bytes 221192 | tf_op jit(solution)/shard_map/ppermute | solution.py:50
  25.5 1.4 collective-permute-start.11
  26.9 1.9 %collective-permute-done.2 = bf16[144,256]{1,0:T(8,128)(2,1)S(1)} collective-permute-done((bf16[144,256]{1,0:T(8,128)(2,1)}, bf16[144,256]{1,0:T(8,128)(2,1)S(1)}, u32[]{:S(2)}, u32[]{:S(2)}) %collective-permute-start.2) | collective-permute-done | bytes 73760 | tf_op jit(solution)/shard_map/ppermute | solution.py:50
  28.9 2.1 %collective-permute-done.3 = bf16[144,256]{1,0:T(8,128)(2,1)S(1)} collective-permute-done((bf16[144,256]{1,0:T(8,128)(2,1)}, bf16[144,256]{1,0:T(8,128)(2,1)S(1)}, u32[]{:S(2)}, u32[]{:S(2)}) %collective-permute-start.3) | collective-permute-done | bytes 73760 | tf_op jit(solution)/shard_map/ppermute | solution.py:50
  30.9 0.9 fusion.14
  32.6 6.1 %collective-permute-done.4 = bf16[4,144,256]{2,1,0:T(8,128)(2,1)S(1)} collective-permute-done((bf16[4,144,256]{2,1,0:T(8,128)(2,1)S(1)}, bf16[4,144,256]{2,1,0:T(8,128)(2,1)S(1)}, u32[]{:S(2)}, u32[]{:S(2)}) %collective-permute-start.4) | collective-permute-done | bytes 294944 | tf_op jit(solution)/shard_map/ppermute | solution.py:50
  38.7 1.6 %collective-permute-start.5 = (bf16[2,4,144,256]{3,2,1,0:T(8,128)(2,1)S(1)}, bf16[2,4,144,256]{3,2,1,0:T(8,128)(2,1)S(1)}, u32[]{:S(2)}, u32[]{:S(2)}) collective-permute-start(bf16[2,4,144,256]{3,2,1,0:T(8,128)(2,1)S(1)} %pad_maximum_fusion.refs_0_), channel_id=1, source_target_pairs={{0,16},{1,17},{2,18},{3,19},{4,20},{5,21},{6,22},{7,23},{8,9},{9,8... | collective-permute-start | bytes 1769480 | tf_op jit(solution)/shard_map/ppermute | solution.py:50
  41.0 7.7 %collective-permute-done.5.refs_1_ = bf16[2,4,144,256]{3,2,1,0:T(8,128)(2,1)S(1)} collective-permute-done((bf16[2,4,144,256]{3,2,1,0:T(8,128)(2,1)S(1)}, bf16[2,4,144,256]{3,2,1,0:T(8,128)(2,1)S(1)}, u32[]{:S(2)}, u32[]{:S(2)}) %collective-permute-start.5) | collective-permute-done | bytes 589856 | tf_op jit(solution)/shard_map/ppermute | solution.py:50
  48.7 2.2 %copy-done.3 = bf16[1024,2048]{1,0:T(8,128)(2,1)S(1)} copy-done((bf16[1024,2048]{1,0:T(8,128)(2,1)S(1)}, bf16[1024,2048]{1,0:T(8,128)(2,1)}, u32[]{:S(2)}) %copy-start.3) | copy-done | bytes 4194328
  50.9 4.7 %logits.1 = (f32[4,512,256]{2,1,0:T(8,128)S(1)}, f32[4,1,256]{2,1,0:T(1,128)S(1)}) custom-call(s32[4]{0:T(128)S(1)} %pad_add_fusion.here_ref, bf16[2,4,128,256]{3,2,1,0:T(8,128)(2,1)S(1)} %pad_maximum_fusion.1.refs_0_, bf16[2,4,128,256]{3,2,1,0:T(8,128)(2,1)S(1)} %collective-permute-done.11.refs_1_, ...), custom_call_target="tpu_custom_call" | custom-call | flops 17179869184 | bytes 8388608 | tf_op jit(solution)/shard_map/logits/pallas_call | solution.py:443
  55.6 10.1 %signal.1 = (f32[1,1]{1,0:T(1,128)}, f32[4,1024]{1,0:T(4,128)S(1)}, bf16[512,1024]{1,0:T(8,128)(2,1)S(1)}, f32[2,2,4,128,256]{4,3,2,1,0:T(8,128)S(1)}, bf16[2,2,4,128,256]{4,3,2,1,0:T(8,128)(2,1)S(1)}) custom-call(s32[4]{0:T(128)S(1)} %pad_add_fusion.here_ref, s32[1,1024]{1,0:T(1,128)S(1)} %reshape.36.act_ref, ...), custom_call_target="tpu_custom_call" | custom-call | flops 4294967296 | bytes 14680064 | tf_op jit(solution)/shard_map/signal/pallas_call | solution.py:472
  66.3 3.5 %gradient.1 = (f32[2,2,4,128,256]{4,3,2,1,0:T(8,128)S(1)}, bf16[2,2,4,128,256]{4,3,2,1,0:T(8,128)(2,1)S(1)}) custom-call(s32[4]{0:T(128)S(1)} %pad_add_fusion.here_ref, bf16[512,1024]{1,0:T(8,128)(2,1)S(1)} %get-tuple-element.57.sig_ref, bf16[1024,2048]{1,0:T(8,128)(2,1)S(1)} %copy-done.3), custom_call_target="tpu_custom_call" | custom-call | flops 2147483648 | bytes 6291456 | tf_op jit(solution)/shard_map/gradient/pallas_call | solution.py:502
  70.2 1.6 %collective-permute-start.15 = (bf16[2,4,128,256]{3,2,1,0:T(8,128)(2,1)S(1)}, bf16[2,4,128,256]{3,2,1,0:T(8,128)(2,1)S(1)}, u32[]{:S(2)}, u32[]{:S(2)}) collective-permute-start(bf16[2,4,128,256]{3,2,1,0:T(8,128)(2,1)S(1)} %fusion.2), channel_id=1, source_target_pairs={{0,16},{1,17},{2,18},{3,19},{4,20},{5,21},{6,22},{7,23},{8,9},{9,8... | collective-permute-start | bytes 1572872 | tf_op jit(solution)/shard_map/ppermute | solution.py:50
  72.9 1.6 %collective-permute-start.29 = (bf16[2,4,128,256]{3,2,1,0:T(8,128)(2,1)S(1)}, bf16[2,4,128,256]{3,2,1,0:T(8,128)(2,1)S(1)}, u32[]{:S(2)}, u32[]{:S(2)}) collective-permute-start(bf16[2,4,128,256]{3,2,1,0:T(8,128)(2,1)S(1)} %fusion.3), channel_id=1, source_target_pairs={{0,16},{1,17},{2,18},{3,19},{4,20},{5,21},{6,22},{7,23},{8,9},{9,8... | collective-permute-start | bytes 1572872 | tf_op jit(solution)/shard_map/ppermute | solution.py:50
  74.5 5.0 %collective-permute-done.15 = bf16[2,4,128,256]{3,2,1,0:T(8,128)(2,1)S(1)} collective-permute-done((bf16[2,4,128,256]{3,2,1,0:T(8,128)(2,1)S(1)}, bf16[2,4,128,256]{3,2,1,0:T(8,128)(2,1)S(1)}, u32[]{:S(2)}, u32[]{:S(2)}) %collective-permute-start.15) | collective-permute-done | bytes 524320 | tf_op jit(solution)/shard_map/ppermute | solution.py:50
  80.3 7.6 %collective-permute-done.29 = bf16[2,4,128,256]{3,2,1,0:T(8,128)(2,1)S(1)} collective-permute-done((bf16[2,4,128,256]{3,2,1,0:T(8,128)(2,1)S(1)}, bf16[2,4,128,256]{3,2,1,0:T(8,128)(2,1)S(1)}, u32[]{:S(2)}, u32[]{:S(2)}) %collective-permute-start.29) | collective-permute-done | bytes 524320 | tf_op jit(solution)/shard_map/ppermute | solution.py:50
  88.9 1.0 collective-permute-start.17
  89.9 1.5 %collective-permute-start.18 = (bf16[128,256]{1,0:T(8,128)(2,1)S(1)}, bf16[128,256]{1,0:T(8,128)(2,1)S(1)}, u32[]{:S(2)}, u32[]{:S(2)}) collective-permute-start(bf16[128,256]{1,0:T(8,128)(2,1)S(1)} %get-tuple-element.87), channel_id=1, source_target_pairs={{0,4},{1,5},{2,6},{3,7},{4,0},{5,1},{6,2},{7,3},{8,12},{9,13},{10,... | collective-permute-start | bytes 196616 | tf_op jit(solution)/shard_map/ppermute | solution.py:50
  91.4 1.9 %collective-permute-start.19 = (bf16[128,256]{1,0:T(8,128)(2,1)S(1)}, bf16[128,256]{1,0:T(8,128)(2,1)S(1)}, u32[]{:S(2)}, u32[]{:S(2)}) collective-permute-start(bf16[128,256]{1,0:T(8,128)(2,1)S(1)} %get-tuple-element.86), channel_id=1, source_target_pairs={{0,6},{1,7},{2,4},{3,5},{4,2},{5,3},{6,0},{7,1},{8,14},{9,15},{10,... | collective-permute-start | bytes 196616 | tf_op jit(solution)/shard_map/ppermute | solution.py:50
  93.4 1.2 collective-permute-done.30
  94.6 1.2 collective-permute-done.18.refs_1_
  95.8 1.7 %collective-permute-done.19.refs_2_ = bf16[128,256]{1,0:T(8,128)(2,1)S(1)} collective-permute-done((bf16[128,256]{1,0:T(8,128)(2,1)S(1)}, bf16[128,256]{1,0:T(8,128)(2,1)S(1)}, u32[]{:S(2)}, u32[]{:S(2)}) %collective-permute-start.19) | collective-permute-done | bytes 65568 | tf_op jit(solution)/shard_map/ppermute | solution.py:50
  99.0 1.2 collective-permute-start.31
  100.1 2.2 %collective-permute-start.32 = (bf16[128,256]{1,0:T(8,128)(2,1)S(1)}, bf16[128,256]{1,0:T(8,128)(2,1)S(1)}, u32[]{:S(2)}, u32[]{:S(2)}) collective-permute-start(bf16[128,256]{1,0:T(8,128)(2,1)S(1)} %get-tuple-element.61), channel_id=1, source_target_pairs={{0,4},{1,5},{2,6},{3,7},{4,0},{5,1},{6,2},{7,3},{8,12},{9,13},{10,... | collective-permute-start | bytes 196616 | tf_op jit(solution)/shard_map/ppermute | solution.py:50
  102.4 1.1 collective-permute-start.33
  103.8 3.0 %collective-permute-start.21 = (bf16[256,128]{1,0:T(8,128)(2,1)S(1)}, bf16[256,128]{1,0:T(8,128)(2,1)S(1)}, u32[]{:S(2)}, u32[]{:S(2)}) collective-permute-start(bf16[256,128]{1,0:T(8,128)(2,1)S(1)} %get-tuple-element.53), channel_id=1, source_target_pairs={{0,4},{1,5},{2,6},{3,7},{4,0},{5,1},{6,2},{7,3},{8,12},{9,13},{10,... | collective-permute-start | bytes 196616 | tf_op jit(solution)/shard_map/ppermute | solution.py:50
  106.8 2.3 %collective-permute-done.32.refs_1_ = bf16[128,256]{1,0:T(8,128)(2,1)S(1)} collective-permute-done((bf16[128,256]{1,0:T(8,128)(2,1)S(1)}, bf16[128,256]{1,0:T(8,128)(2,1)S(1)}, u32[]{:S(2)}, u32[]{:S(2)}) %collective-permute-start.32) | collective-permute-done | bytes 65568 | tf_op jit(solution)/shard_map/ppermute | solution.py:50
  109.0 1.6 %collective-permute-start.22 = (bf16[256,128]{1,0:T(8,128)(2,1)S(1)}, bf16[256,128]{1,0:T(8,128)(2,1)S(1)}, u32[]{:S(2)}, u32[]{:S(2)}) collective-permute-start(bf16[256,128]{1,0:T(8,128)(2,1)S(1)} %get-tuple-element.53), channel_id=1, source_target_pairs={{0,6},{1,7},{2,4},{3,5},{4,2},{5,3},{6,0},{7,1},{8,14},{9,15},{10,... | collective-permute-start | bytes 196616 | tf_op jit(solution)/shard_map/ppermute | solution.py:50
  111.5 1.2 collective-permute-start.37
  113.4 1.3 collective-permute-start.35
  114.7 2.4 %collective-permute-start.36 = (bf16[256,128]{1,0:T(8,128)(2,1)S(1)}, bf16[256,128]{1,0:T(8,128)(2,1)S(1)}, u32[]{:S(2)}, u32[]{:S(2)}) collective-permute-start(bf16[256,128]{1,0:T(8,128)(2,1)S(1)} %get-tuple-element.65), channel_id=1, source_target_pairs={{0,6},{1,7},{2,4},{3,5},{4,2},{5,3},{6,0},{7,1},{8,14},{9,15},{10,... | collective-permute-start | bytes 196616 | tf_op jit(solution)/shard_map/ppermute | solution.py:50
  117.2 0.9 collective-permute-start.24
  118.7 2.1 %collective-permute-done.36 = bf16[256,128]{1,0:T(8,128)(2,1)S(1)} collective-permute-done((bf16[256,128]{1,0:T(8,128)(2,1)S(1)}, bf16[256,128]{1,0:T(8,128)(2,1)S(1)}, u32[]{:S(2)}, u32[]{:S(2)}) %collective-permute-start.36) | collective-permute-done | bytes 65568 | tf_op jit(solution)/shard_map/ppermute | solution.py:50
  120.8 1.2 collective-permute-start.38
  122.0 4.5 %collective-permute-done.24 = bf16[4,256,128]{2,1,0:T(8,128)(2,1)S(1)} collective-permute-done((bf16[4,256,128]{2,1,0:T(8,128)(2,1)S(1)}, bf16[4,256,128]{2,1,0:T(8,128)(2,1)S(1)}, u32[]{:S(2)}, u32[]{:S(2)}) %collective-permute-start.24) | collective-permute-done | bytes 262176 | tf_op jit(solution)/shard_map/ppermute | solution.py:50
  126.5 1.0 collective-permute-start.25
  127.5 4.5 %collective-permute-done.38 = bf16[4,256,128]{2,1,0:T(8,128)(2,1)S(1)} collective-permute-done((bf16[4,256,128]{2,1,0:T(8,128)(2,1)S(1)}, bf16[4,256,128]{2,1,0:T(8,128)(2,1)S(1)}, u32[]{:S(2)}, u32[]{:S(2)}) %collective-permute-start.38) | collective-permute-done | bytes 262176 | tf_op jit(solution)/shard_map/ppermute | solution.py:50
  132.1 1.0 collective-permute-start.39
  133.7 2.1 %collective-permute-done.25.refs_1_ = bf16[2,4,256,128]{3,2,1,0:T(8,128)(2,1)S(1)} collective-permute-done((bf16[2,4,256,128]{3,2,1,0:T(8,128)(2,1)S(1)}, bf16[2,4,256,128]{3,2,1,0:T(8,128)(2,1)S(1)}, u32[]{:S(2)}, u32[]{:S(2)}) %collective-permute-start.25) | collective-permute-done | bytes 524320 | tf_op jit(solution)/shard_map/ppermute | solution.py:50
  135.8 5.6 %collective-permute-done.39.refs_5_ = bf16[2,4,256,128]{3,2,1,0:T(8,128)(2,1)S(1)} collective-permute-done((bf16[2,4,256,128]{3,2,1,0:T(8,128)(2,1)S(1)}, bf16[2,4,256,128]{3,2,1,0:T(8,128)(2,1)S(1)}, u32[]{:S(2)}, u32[]{:S(2)}) %collective-permute-start.39) | collective-permute-done | bytes 524320 | tf_op jit(solution)/shard_map/ppermute | solution.py:50
  143.8 4.4 %assemble.1 = (bf16[2048,1024]{1,0:T(8,128)(2,1)}, f32[256,1024]{1,0:T(8,128)}) custom-call(s32[4]{0:T(128)S(1)} %pad_add_fusion.here_ref, bf16[2,4,256,128]{3,2,1,0:T(8,128)(2,1)S(1)} %pad_maximum_fusion.2.refs_0_, bf16[2,4,256,128]{3,2,1,0:T(8,128)(2,1)S(1)} %collective-permute-done.25.refs_1_, ...), custom_call_target="tpu_custom_call" | custom-call | tf_op jit(solution)/shard_map/assemble/pallas_call | solution.py:562
  (92 shorter events, 15.4 us)
Async XLA Ops:
  2.4 8.3 %collective-permute-start = (bf16[128,256]{1,0:T(8,128)(2,1)}, bf16[128,256]{1,0:T(8,128)(2,1)S(1)}, u32[]{:S(2)}, u32[]{:S(2)}) collective-permute-start(bf16[128,256]{1,0:T(8,128)(2,1)} %get-tuple-element.43), channel_id=1, source_target_pairs={{0,2},{1,3},{2,0},{3,1},{4,6},{5,7},{6,4},{7,5},{8,10},{9,11},{10,... | collective-permute-start | bytes 196616 | tf_op jit(solution)/shard_map/ppermute | solution.py:50
  5.5 13.0 %collective-permute-start.8 = (bf16[128,256]{1,0:T(8,128)(2,1)}, bf16[128,256]{1,0:T(8,128)(2,1)S(1)}, u32[]{:S(2)}, u32[]{:S(2)}) collective-permute-start(bf16[128,256]{1,0:T(8,128)(2,1)} %get-tuple-element.43), channel_id=1, source_target_pairs={{0,4},{1,5},{2,6},{3,7},{4,0},{5,1},{6,2},{7,3},{8,12},{9,13},{10,... | collective-permute-start | bytes 196616 | tf_op jit(solution)/shard_map/ppermute | solution.py:50
  8.1 10.5 %collective-permute-start.9 = (bf16[128,256]{1,0:T(8,128)(2,1)}, bf16[128,256]{1,0:T(8,128)(2,1)S(1)}, u32[]{:S(2)}, u32[]{:S(2)}) collective-permute-start(bf16[128,256]{1,0:T(8,128)(2,1)} %get-tuple-element.43), channel_id=1, source_target_pairs={{0,6},{1,7},{2,4},{3,5},{4,2},{5,3},{6,0},{7,1},{8,14},{9,15},{10,... | collective-permute-start | bytes 196616 | tf_op jit(solution)/shard_map/ppermute | solution.py:50
  18.5 22.3 %copy-start.5 = (s32[32,32]{1,0:T(8,128)S(1)}, s32[32,32]{1,0:T(8,128)}, u32[]{:S(2)}) copy-start(s32[32,32]{1,0:T(8,128)} %param.15) | copy-start | bytes 12292
  18.6 6.4 %collective-permute-start.10 = (bf16[4,128,256]{2,1,0:T(8,128)(2,1)S(1)}, bf16[4,128,256]{2,1,0:T(8,128)(2,1)S(1)}, u32[]{:S(2)}, u32[]{:S(2)}) collective-permute-start(bf16[4,128,256]{2,1,0:T(8,128)(2,1)S(1)} %get-tuple-element.90), channel_id=1, source_target_pairs={{0,1},{1,0},{2,3},{3,2},{4,5},{5,4},{6,7},{7,6},{8,24},{9,25},{10,... | collective-permute-start | bytes 786440 | tf_op jit(solution)/shard_map/ppermute | solution.py:50
  20.4 5.1 %collective-permute-start.1 = (bf16[144,256]{1,0:T(8,128)(2,1)}, bf16[144,256]{1,0:T(8,128)(2,1)S(1)}, u32[]{:S(2)}, u32[]{:S(2)}) collective-permute-start(bf16[144,256]{1,0:T(8,128)(2,1)} %get-tuple-element.41), channel_id=1, source_target_pairs={{0,2},{1,3},{2,0},{3,1},{4,6},{5,7},{6,4},{7,5},{8,10},{9,11},{10,... | collective-permute-start | bytes 221192 | tf_op jit(solution)/shard_map/ppermute | solution.py:50
  21.1 7.8 %collective-permute-start.2 = (bf16[144,256]{1,0:T(8,128)(2,1)}, bf16[144,256]{1,0:T(8,128)(2,1)S(1)}, u32[]{:S(2)}, u32[]{:S(2)}) collective-permute-start(bf16[144,256]{1,0:T(8,128)(2,1)} %get-tuple-element.41), channel_id=1, source_target_pairs={{0,4},{1,5},{2,6},{3,7},{4,0},{5,1},{6,2},{7,3},{8,12},{9,13},{10,... | collective-permute-start | bytes 221192 | tf_op jit(solution)/shard_map/ppermute | solution.py:50
  24.6 6.4 %collective-permute-start.3 = (bf16[144,256]{1,0:T(8,128)(2,1)}, bf16[144,256]{1,0:T(8,128)(2,1)S(1)}, u32[]{:S(2)}, u32[]{:S(2)}) collective-permute-start(bf16[144,256]{1,0:T(8,128)(2,1)} %get-tuple-element.41), channel_id=1, source_target_pairs={{0,6},{1,7},{2,4},{3,5},{4,2},{5,3},{6,0},{7,1},{8,14},{9,15},{10,... | collective-permute-start | bytes 221192 | tf_op jit(solution)/shard_map/ppermute | solution.py:50
  25.5 14.8 %collective-permute-start.11 = (bf16[2,4,128,256]{3,2,1,0:T(8,128)(2,1)S(1)}, bf16[2,4,128,256]{3,2,1,0:T(8,128)(2,1)S(1)}, u32[]{:S(2)}, u32[]{:S(2)}) collective-permute-start(bf16[2,4,128,256]{3,2,1,0:T(8,128)(2,1)S(1)} %pad_maximum_fusion.1.refs_0_), channel_id=1, source_target_pairs={{0,16},{1,17},{2,18},{3,19},{4,20},{5,21},{6,22},{7,23},{8,9},{9,8... | collective-permute-start | bytes 1572872 | tf_op jit(solution)/shard_map/ppermute | solution.py:50
  31.9 6.8 %collective-permute-start.4 = (bf16[4,144,256]{2,1,0:T(8,128)(2,1)S(1)}, bf16[4,144,256]{2,1,0:T(8,128)(2,1)S(1)}, u32[]{:S(2)}, u32[]{:S(2)}) collective-permute-start(bf16[4,144,256]{2,1,0:T(8,128)(2,1)S(1)} %get-tuple-element.78), channel_id=1, source_target_pairs={{0,1},{1,0},{2,3},{3,2},{4,5},{5,4},{6,7},{7,6},{8,24},{9,25},{10,... | collective-permute-start | bytes 884744 | tf_op jit(solution)/shard_map/ppermute | solution.py:50
  38.7 9.9 %collective-permute-start.5 = (bf16[2,4,144,256]{3,2,1,0:T(8,128)(2,1)S(1)}, bf16[2,4,144,256]{3,2,1,0:T(8,128)(2,1)S(1)}, u32[]{:S(2)}, u32[]{:S(2)}) collective-permute-start(bf16[2,4,144,256]{3,2,1,0:T(8,128)(2,1)S(1)} %pad_maximum_fusion.refs_0_), channel_id=1, source_target_pairs={{0,16},{1,17},{2,18},{3,19},{4,20},{5,21},{6,22},{7,23},{8,9},{9,8... | collective-permute-start | bytes 1769480 | tf_op jit(solution)/shard_map/ppermute | solution.py:50
  40.3 8.4 %collective-permute-start.12 = (bf16[2,4,128,256]{3,2,1,0:T(8,128)(2,1)S(1)}, bf16[2,4,128,256]{3,2,1,0:T(8,128)(2,1)S(1)}, u32[]{:S(2)}, u32[]{:S(2)}) collective-permute-start(bf16[2,4,128,256]{3,2,1,0:T(8,128)(2,1)S(1)} %pad_maximum_fusion.1.refs_0_), channel_id=1, source_target_pairs={{0,8},{1,9},{2,10},{3,11},{4,12},{5,13},{6,14},{7,15},{8,0},{9,1},... | collective-permute-start | bytes 1572872 | tf_op jit(solution)/shard_map/ppermute | solution.py:50
  40.3 8.4 %collective-permute-start.13 = (bf16[2,4,128,256]{3,2,1,0:T(8,128)(2,1)S(1)}, bf16[2,4,128,256]{3,2,1,0:T(8,128)(2,1)}, u32[]{:S(2)}, u32[]{:S(2)}) collective-permute-start(bf16[2,4,128,256]{3,2,1,0:T(8,128)(2,1)S(1)} %collective-permute-done.11.refs_1_), channel_id=1, source_target_pairs={{0,8},{1,9},{2,10},{3,11},{4,12},{5,13},{6,14},{7,15},{8,0},{9,1},... | collective-permute-start | bytes 1572872 | tf_op jit(solution)/shard_map/ppermute | solution.py:50
  41.0 14.6 %collective-permute-start.6 = (bf16[2,4,144,256]{3,2,1,0:T(8,128)(2,1)S(1)}, bf16[2,4,144,256]{3,2,1,0:T(8,128)(2,1)S(1)}, u32[]{:S(2)}, u32[]{:S(2)}) collective-permute-start(bf16[2,4,144,256]{3,2,1,0:T(8,128)(2,1)S(1)} %pad_maximum_fusion.refs_0_), channel_id=1, source_target_pairs={{0,8},{1,9},{2,10},{3,11},{4,12},{5,13},{6,14},{7,15},{8,0},{9,1},... | collective-permute-start | bytes 1769480 | tf_op jit(solution)/shard_map/ppermute | solution.py:50
  48.7 7.0 %collective-permute-start.7 = (bf16[2,4,144,256]{3,2,1,0:T(8,128)(2,1)S(1)}, bf16[2,4,144,256]{3,2,1,0:T(8,128)(2,1)S(1)}, u32[]{:S(2)}, u32[]{:S(2)}) collective-permute-start(bf16[2,4,144,256]{3,2,1,0:T(8,128)(2,1)S(1)} %collective-permute-done.5.refs_1_), channel_id=1, source_target_pairs={{0,8},{1,9},{2,10},{3,11},{4,12},{5,13},{6,14},{7,15},{8,0},{9,1},... | collective-permute-start | bytes 1769480 | tf_op jit(solution)/shard_map/ppermute | solution.py:50
  65.7 4.2 %collective-permute-start.14 = (bf16[2,2,4,128,256]{4,3,2,1,0:T(8,128)(2,1)S(1)}, bf16[2,2,4,128,256]{4,3,2,1,0:T(8,128)(2,1)S(1)}, u32[]{:S(2)}, u32[]{:S(2)}) collective-permute-start(bf16[2,2,4,128,256]{4,3,2,1,0:T(8,128)(2,1)S(1)} %get-tuple-element.50), channel_id=1, source_target_pairs={{0,8},{1,9},{2,10},{3,11},{4,12},{5,13},{6,14},{7,15},{8,0},{9,1},... | collective-permute-start | bytes 3145736 | tf_op jit(solution)/shard_map/ppermute | solution.py:50
  69.8 2.7 %collective-permute-start.28 = (bf16[2,2,4,128,256]{4,3,2,1,0:T(8,128)(2,1)S(1)}, bf16[2,2,4,128,256]{4,3,2,1,0:T(8,128)(2,1)S(1)}, u32[]{:S(2)}, u32[]{:S(2)}) collective-permute-start(bf16[2,2,4,128,256]{4,3,2,1,0:T(8,128)(2,1)S(1)} %get-tuple-element.59), channel_id=1, source_target_pairs={{0,8},{1,9},{2,10},{3,11},{4,12},{5,13},{6,14},{7,15},{8,0},{9,1},... | collective-permute-start | bytes 3145736 | tf_op jit(solution)/shard_map/ppermute | solution.py:50
  70.2 9.2 %collective-permute-start.15 = (bf16[2,4,128,256]{3,2,1,0:T(8,128)(2,1)S(1)}, bf16[2,4,128,256]{3,2,1,0:T(8,128)(2,1)S(1)}, u32[]{:S(2)}, u32[]{:S(2)}) collective-permute-start(bf16[2,4,128,256]{3,2,1,0:T(8,128)(2,1)S(1)} %fusion.2), channel_id=1, source_target_pairs={{0,16},{1,17},{2,18},{3,19},{4,20},{5,21},{6,22},{7,23},{8,9},{9,8... | collective-permute-start | bytes 1572872 | tf_op jit(solution)/shard_map/ppermute | solution.py:50
  72.9 15.0 %collective-permute-start.29 = (bf16[2,4,128,256]{3,2,1,0:T(8,128)(2,1)S(1)}, bf16[2,4,128,256]{3,2,1,0:T(8,128)(2,1)S(1)}, u32[]{:S(2)}, u32[]{:S(2)}) collective-permute-start(bf16[2,4,128,256]{3,2,1,0:T(8,128)(2,1)S(1)} %fusion.3), channel_id=1, source_target_pairs={{0,16},{1,17},{2,18},{3,19},{4,20},{5,21},{6,22},{7,23},{8,9},{9,8... | collective-permute-start | bytes 1572872 | tf_op jit(solution)/shard_map/ppermute | solution.py:50
  79.6 9.2 %collective-permute-start.16 = (bf16[4,128,256]{2,1,0:T(8,128)(2,1)S(1)}, bf16[4,128,256]{2,1,0:T(8,128)(2,1)S(1)}, u32[]{:S(2)}, u32[]{:S(2)}) collective-permute-start(bf16[4,128,256]{2,1,0:T(8,128)(2,1)S(1)} %fusion.6), channel_id=1, source_target_pairs={{0,1},{1,0},{2,3},{3,2},{4,5},{5,4},{6,7},{7,6},{8,24},{9,25},{10,... | collective-permute-start | bytes 786440 | tf_op jit(solution)/shard_map/ppermute | solution.py:50
  88.0 9.5 %copy-start = (f32[256,1024]{1,0:T(8,128)S(1)}, f32[256,1024]{1,0:T(8,128)}, u32[]{:S(2)}) copy-start(f32[256,1024]{1,0:T(8,128)} %refs_3_.3) | copy-start | bytes 3145732
  88.0 9.5 %copy-start.1 = (f32[256,1024]{1,0:T(8,128)S(1)}, f32[256,1024]{1,0:T(8,128)}, u32[]{:S(2)}) copy-start(f32[256,1024]{1,0:T(8,128)} %refs_4_.3) | copy-start | bytes 3145732
  88.0 9.5 %copy-start.2 = (f32[256,1024]{1,0:T(8,128)S(1)}, f32[256,1024]{1,0:T(8,128)}, u32[]{:S(2)}) copy-start(f32[256,1024]{1,0:T(8,128)} %refs_5_.3) | copy-start | bytes 3145732
  88.1 6.4 %collective-permute-start.30 = (bf16[4,128,256]{2,1,0:T(8,128)(2,1)S(1)}, bf16[4,128,256]{2,1,0:T(8,128)(2,1)S(1)}, u32[]{:S(2)}, u32[]{:S(2)}) collective-permute-start(bf16[4,128,256]{2,1,0:T(8,128)(2,1)S(1)} %fusion.7), channel_id=1, source_target_pairs={{0,1},{1,0},{2,3},{3,2},{4,5},{5,4},{6,7},{7,6},{8,24},{9,25},{10,... | collective-permute-start | bytes 786440 | tf_op jit(solution)/shard_map/ppermute | solution.py:50
  88.9 5.7 %collective-permute-start.17 = (bf16[128,256]{1,0:T(8,128)(2,1)S(1)}, bf16[128,256]{1,0:T(8,128)(2,1)S(1)}, u32[]{:S(2)}, u32[]{:S(2)}) collective-permute-start(bf16[128,256]{1,0:T(8,128)(2,1)S(1)} %get-tuple-element.88), channel_id=1, source_target_pairs={{0,2},{1,3},{2,0},{3,1},{4,6},{5,7},{6,4},{7,5},{8,10},{9,11},{10,... | collective-permute-start | bytes 196616 | tf_op jit(solution)/shard_map/ppermute | solution.py:50
  89.9 5.9 %collective-permute-start.18 = (bf16[128,256]{1,0:T(8,128)(2,1)S(1)}, bf16[128,256]{1,0:T(8,128)(2,1)S(1)}, u32[]{:S(2)}, u32[]{:S(2)}) collective-permute-start(bf16[128,256]{1,0:T(8,128)(2,1)S(1)} %get-tuple-element.87), channel_id=1, source_target_pairs={{0,4},{1,5},{2,6},{3,7},{4,0},{5,1},{6,2},{7,3},{8,12},{9,13},{10,... | collective-permute-start | bytes 196616 | tf_op jit(solution)/shard_map/ppermute | solution.py:50
  91.4 6.1 %collective-permute-start.19 = (bf16[128,256]{1,0:T(8,128)(2,1)S(1)}, bf16[128,256]{1,0:T(8,128)(2,1)S(1)}, u32[]{:S(2)}, u32[]{:S(2)}) collective-permute-start(bf16[128,256]{1,0:T(8,128)(2,1)S(1)} %get-tuple-element.86), channel_id=1, source_target_pairs={{0,6},{1,7},{2,4},{3,5},{4,2},{5,3},{6,0},{7,1},{8,14},{9,15},{10,... | collective-permute-start | bytes 196616 | tf_op jit(solution)/shard_map/ppermute | solution.py:50
  98.3 14.3 %collective-permute-start.23 = (f32[256,128]{1,0:T(8,128)S(1)}, f32[256,128]{1,0:T(8,128)S(1)}, u32[]{:S(2)}, u32[]{:S(2)}) collective-permute-start(f32[256,128]{1,0:T(8,128)S(1)} %get-tuple-element.52), channel_id=1, source_target_pairs={{0,16},{1,17},{2,18},{3,19},{4,20},{5,21},{6,22},{7,23},{8,24},{9,... | collective-permute-start | bytes 393224 | tf_op jit(solution)/shard_map/ppermute | solution.py:50
  99.0 4.8 %collective-permute-start.31 = (bf16[128,256]{1,0:T(8,128)(2,1)S(1)}, bf16[128,256]{1,0:T(8,128)(2,1)S(1)}, u32[]{:S(2)}, u32[]{:S(2)}) collective-permute-start(bf16[128,256]{1,0:T(8,128)(2,1)S(1)} %get-tuple-element.60), channel_id=1, source_target_pairs={{0,2},{1,3},{2,0},{3,1},{4,6},{5,7},{6,4},{7,5},{8,10},{9,11},{10,... | collective-permute-start | bytes 196616 | tf_op jit(solution)/shard_map/ppermute | solution.py:50
  100.1 8.9 %collective-permute-start.32 = (bf16[128,256]{1,0:T(8,128)(2,1)S(1)}, bf16[128,256]{1,0:T(8,128)(2,1)S(1)}, u32[]{:S(2)}, u32[]{:S(2)}) collective-permute-start(bf16[128,256]{1,0:T(8,128)(2,1)S(1)} %get-tuple-element.61), channel_id=1, source_target_pairs={{0,4},{1,5},{2,6},{3,7},{4,0},{5,1},{6,2},{7,3},{8,12},{9,13},{10,... | collective-permute-start | bytes 196616 | tf_op jit(solution)/shard_map/ppermute | solution.py:50
  102.4 8.3 %collective-permute-start.33 = (bf16[128,256]{1,0:T(8,128)(2,1)S(1)}, bf16[128,256]{1,0:T(8,128)(2,1)S(1)}, u32[]{:S(2)}, u32[]{:S(2)}) collective-permute-start(bf16[128,256]{1,0:T(8,128)(2,1)S(1)} %get-tuple-element.62), channel_id=1, source_target_pairs={{0,6},{1,7},{2,4},{3,5},{4,2},{5,3},{6,0},{7,1},{8,14},{9,15},{10,... | collective-permute-start | bytes 196616 | tf_op jit(solution)/shard_map/ppermute | solution.py:50
  103.4 10.0 %collective-permute-start.20 = (bf16[256,128]{1,0:T(8,128)(2,1)S(1)}, bf16[256,128]{1,0:T(8,128)(2,1)S(1)}, u32[]{:S(2)}, u32[]{:S(2)}) collective-permute-start(bf16[256,128]{1,0:T(8,128)(2,1)S(1)} %get-tuple-element.53), channel_id=1, source_target_pairs={{0,2},{1,3},{2,0},{3,1},{4,6},{5,7},{6,4},{7,5},{8,10},{9,11},{10,... | collective-permute-start | bytes 196616 | tf_op jit(solution)/shard_map/ppermute | solution.py:50
  103.8 10.9 %collective-permute-start.21 = (bf16[256,128]{1,0:T(8,128)(2,1)S(1)}, bf16[256,128]{1,0:T(8,128)(2,1)S(1)}, u32[]{:S(2)}, u32[]{:S(2)}) collective-permute-start(bf16[256,128]{1,0:T(8,128)(2,1)S(1)} %get-tuple-element.53), channel_id=1, source_target_pairs={{0,4},{1,5},{2,6},{3,7},{4,0},{5,1},{6,2},{7,3},{8,12},{9,13},{10,... | collective-permute-start | bytes 196616 | tf_op jit(solution)/shard_map/ppermute | solution.py:50
  109.0 8.1 %collective-permute-start.22 = (bf16[256,128]{1,0:T(8,128)(2,1)S(1)}, bf16[256,128]{1,0:T(8,128)(2,1)S(1)}, u32[]{:S(2)}, u32[]{:S(2)}) collective-permute-start(bf16[256,128]{1,0:T(8,128)(2,1)S(1)} %get-tuple-element.53), channel_id=1, source_target_pairs={{0,6},{1,7},{2,4},{3,5},{4,2},{5,3},{6,0},{7,1},{8,14},{9,15},{10,... | collective-permute-start | bytes 196616 | tf_op jit(solution)/shard_map/ppermute | solution.py:50
  111.5 6.6 %collective-permute-start.37 = (f32[256,128]{1,0:T(8,128)S(1)}, f32[256,128]{1,0:T(8,128)S(1)}, u32[]{:S(2)}, u32[]{:S(2)}) collective-permute-start(f32[256,128]{1,0:T(8,128)S(1)} %get-tuple-element.64), channel_id=1, source_target_pairs={{0,16},{1,17},{2,18},{3,19},{4,20},{5,21},{6,22},{7,23},{8,24},{9,... | collective-permute-start | bytes 393224 | tf_op jit(solution)/shard_map/ppermute | solution.py:50
  112.6 5.5 %collective-permute-start.34 = (bf16[256,128]{1,0:T(8,128)(2,1)S(1)}, bf16[256,128]{1,0:T(8,128)(2,1)S(1)}, u32[]{:S(2)}, u32[]{:S(2)}) collective-permute-start(bf16[256,128]{1,0:T(8,128)(2,1)S(1)} %get-tuple-element.65), channel_id=1, source_target_pairs={{0,2},{1,3},{2,0},{3,1},{4,6},{5,7},{6,4},{7,5},{8,10},{9,11},{10,... | collective-permute-start | bytes 196616 | tf_op jit(solution)/shard_map/ppermute | solution.py:50
  113.4 5.2 %collective-permute-start.35 = (bf16[256,128]{1,0:T(8,128)(2,1)S(1)}, bf16[256,128]{1,0:T(8,128)(2,1)S(1)}, u32[]{:S(2)}, u32[]{:S(2)}) collective-permute-start(bf16[256,128]{1,0:T(8,128)(2,1)S(1)} %get-tuple-element.65), channel_id=1, source_target_pairs={{0,4},{1,5},{2,6},{3,7},{4,0},{5,1},{6,2},{7,3},{8,12},{9,13},{10,... | collective-permute-start | bytes 196616 | tf_op jit(solution)/shard_map/ppermute | solution.py:50
  114.7 6.1 %collective-permute-start.36 = (bf16[256,128]{1,0:T(8,128)(2,1)S(1)}, bf16[256,128]{1,0:T(8,128)(2,1)S(1)}, u32[]{:S(2)}, u32[]{:S(2)}) collective-permute-start(bf16[256,128]{1,0:T(8,128)(2,1)S(1)} %get-tuple-element.65), channel_id=1, source_target_pairs={{0,6},{1,7},{2,4},{3,5},{4,2},{5,3},{6,0},{7,1},{8,14},{9,15},{10,... | collective-permute-start | bytes 196616 | tf_op jit(solution)/shard_map/ppermute | solution.py:50
  117.2 9.3 %collective-permute-start.24 = (bf16[4,256,128]{2,1,0:T(8,128)(2,1)S(1)}, bf16[4,256,128]{2,1,0:T(8,128)(2,1)S(1)}, u32[]{:S(2)}, u32[]{:S(2)}) collective-permute-start(bf16[4,256,128]{2,1,0:T(8,128)(2,1)S(1)} %get-tuple-element.85), channel_id=1, source_target_pairs={{0,1},{1,0},{2,3},{3,2},{4,5},{5,4},{6,7},{7,6},{8,24},{9,25},{10,... | collective-permute-start | bytes 786440 | tf_op jit(solution)/shard_map/ppermute | solution.py:50
  120.8 11.2 %collective-permute-start.38 = (bf16[4,256,128]{2,1,0:T(8,128)(2,1)S(1)}, bf16[4,256,128]{2,1,0:T(8,128)(2,1)S(1)}, u32[]{:S(2)}, u32[]{:S(2)}) collective-permute-start(bf16[4,256,128]{2,1,0:T(8,128)(2,1)S(1)} %get-tuple-element.80), channel_id=1, source_target_pairs={{0,1},{1,0},{2,3},{3,2},{4,5},{5,4},{6,7},{7,6},{8,24},{9,25},{10,... | collective-permute-start | bytes 786440 | tf_op jit(solution)/shard_map/ppermute | solution.py:50
  126.5 9.2 %collective-permute-start.25 = (bf16[2,4,256,128]{3,2,1,0:T(8,128)(2,1)S(1)}, bf16[2,4,256,128]{3,2,1,0:T(8,128)(2,1)S(1)}, u32[]{:S(2)}, u32[]{:S(2)}) collective-permute-start(bf16[2,4,256,128]{3,2,1,0:T(8,128)(2,1)S(1)} %pad_maximum_fusion.2.refs_0_), channel_id=1, source_target_pairs={{0,16},{1,17},{2,18},{3,19},{4,20},{5,21},{6,22},{7,23},{8,9},{9,8... | collective-permute-start | bytes 1572872 | tf_op jit(solution)/shard_map/ppermute | solution.py:50
  132.1 9.2 %collective-permute-start.39 = (bf16[2,4,256,128]{3,2,1,0:T(8,128)(2,1)S(1)}, bf16[2,4,256,128]{3,2,1,0:T(8,128)(2,1)S(1)}, u32[]{:S(2)}, u32[]{:S(2)}) collective-permute-start(bf16[2,4,256,128]{3,2,1,0:T(8,128)(2,1)S(1)} %pad_maximum_fusion.3.refs_4_), channel_id=1, source_target_pairs={{0,16},{1,17},{2,18},{3,19},{4,20},{5,21},{6,22},{7,23},{8,9},{9,8... | collective-permute-start | bytes 1572872 | tf_op jit(solution)/shard_map/ppermute | solution.py:50
  133.2 8.2 %collective-permute-start.42 = (f32[2,256,128]{2,1,0:T(8,128)S(1)}, f32[2,256,128]{2,1,0:T(8,128)S(1)}, u32[]{:S(2)}, u32[]{:S(2)}) collective-permute-start(f32[2,256,128]{2,1,0:T(8,128)S(1)} %pad_maximum_fusion.6.refs_8_), channel_id=1, source_target_pairs={{0,8},{1,9},{2,10},{3,11},{4,12},{5,13},{6,14},{7,15},{8,0},{9,1},... | collective-permute-start | bytes 786440 | tf_op jit(solution)/shard_map/ppermute | solution.py:50
  133.2 10.6 %collective-permute-start.26 = (bf16[2,4,256,128]{3,2,1,0:T(8,128)(2,1)S(1)}, bf16[2,4,256,128]{3,2,1,0:T(8,128)(2,1)S(1)}, u32[]{:S(2)}, u32[]{:S(2)}) collective-permute-start(bf16[2,4,256,128]{3,2,1,0:T(8,128)(2,1)S(1)} %pad_maximum_fusion.2.refs_0_), channel_id=1, source_target_pairs={{0,8},{1,9},{2,10},{3,11},{4,12},{5,13},{6,14},{7,15},{8,0},{9,1},... | collective-permute-start | bytes 1572872 | tf_op jit(solution)/shard_map/ppermute | solution.py:50
  133.7 10.1 %collective-permute-start.40 = (bf16[2,4,256,128]{3,2,1,0:T(8,128)(2,1)S(1)}, bf16[2,4,256,128]{3,2,1,0:T(8,128)(2,1)}, u32[]{:S(2)}, u32[]{:S(2)}) collective-permute-start(bf16[2,4,256,128]{3,2,1,0:T(8,128)(2,1)S(1)} %pad_maximum_fusion.3.refs_4_), channel_id=1, source_target_pairs={{0,8},{1,9},{2,10},{3,11},{4,12},{5,13},{6,14},{7,15},{8,0},{9,1},... | collective-permute-start | bytes 1572872 | tf_op jit(solution)/shard_map/ppermute | solution.py:50
  135.8 8.0 %collective-permute-start.27 = (bf16[2,4,256,128]{3,2,1,0:T(8,128)(2,1)S(1)}, bf16[2,4,256,128]{3,2,1,0:T(8,128)(2,1)}, u32[]{:S(2)}, u32[]{:S(2)}) collective-permute-start(bf16[2,4,256,128]{3,2,1,0:T(8,128)(2,1)S(1)} %collective-permute-done.25.refs_1_), channel_id=1, source_target_pairs={{0,8},{1,9},{2,10},{3,11},{4,12},{5,13},{6,14},{7,15},{8,0},{9,1},... | collective-permute-start | bytes 1572872 | tf_op jit(solution)/shard_map/ppermute | solution.py:50
  141.4 2.4 %collective-permute-start.41 = (bf16[2,4,256,128]{3,2,1,0:T(8,128)(2,1)S(1)}, bf16[2,4,256,128]{3,2,1,0:T(8,128)(2,1)}, u32[]{:S(2)}, u32[]{:S(2)}) collective-permute-start(bf16[2,4,256,128]{3,2,1,0:T(8,128)(2,1)S(1)} %collective-permute-done.39.refs_5_), channel_id=1, source_target_pairs={{0,8},{1,9},{2,10},{3,11},{4,12},{5,13},{6,14},{7,15},{8,0},{9,1},... | collective-permute-start | bytes 1572872 | tf_op jit(solution)/shard_map/ppermute | solution.py:50
  141.4 2.4 %collective-permute-start.43 = (f32[2,256,128]{2,1,0:T(8,128)S(1)}, f32[2,256,128]{2,1,0:T(8,128)}, u32[]{:S(2)}, u32[]{:S(2)}) collective-permute-start(f32[2,256,128]{2,1,0:T(8,128)S(1)} %pad_maximum_fusion.8.refs_10_), channel_id=1, source_target_pairs={{0,8},{1,9},{2,10},{3,11},{4,12},{5,13},{6,14},{7,15},{8,0},{9,1},... | collective-permute-start | bytes 786440 | tf_op jit(solution)/shard_map/ppermute | solution.py:50
  (2 other events, 8.7 us)
